TPU v7x, 512 devices: a whole 4x8x8 slice. The times are simulated.
512 devices in a mesh: slab: 64 (over x, z, y_lo), cross: 8 (over y_hi, core).
Axes of the slice: x: 4, y: 8 (y_hi: 4, y_lo: 2; y = y_hi * 2 + y_lo), z: 8, core: 2. Of those that a mesh axis runs over, the one named last changes fastest.
Arguments:
- adjoint_source: float32 [384, 48, 384], P('slab', 'cross'), may hold values from -24 to 24
- potential: float32 [384, 48, 384], P('slab', 'cross'), may hold values from -6 to 6
- element_matrix: float32 [64, 64], replicated
- region_labels: int32 [128, 16, 128], P('slab', 'cross'), may hold values from 0 to 3
- conductivity: float32 [4], replicated, may hold values from 0.3 to 3
- restriction_map: int32 [384, 48, 384], P('slab', 'cross'), may hold values from 0 to 7
Outputs:
- solution: float32 [384, 48, 384], P('slab', 'cross')
- residual: float32 [384, 48, 384], P('slab', 'cross')
All inputs are finite; a program needn't handle non-finite values.
Results may differ from a plain program's by a relative error of at most 0.0025.
Values sent between devices are 32-bit elements; how exact they have to be, the bound alone decides.
No kernel may reach another device: no remote copies, remote signals or barrier semaphores. Data moves between devices by JAX's collectives and lax.ppermute only.
A program may use at most 128 MiB of HBM per device.

v0:
```python
import functools

import jax
import jax.numpy as jnp
from jax import lax
from jax.experimental import pallas as pl
from jax.experimental.pallas import tpu as pltpu
from jax.sharding import PartitionSpec as P

LABELS = 8
DAMPING = 0.8
COUPLING = 0.2
SHARE = 0.1
REACH = 3


F32 = jnp.float32
BF16 = jnp.bfloat16
SPAN = (-1, 0, 1)


def lanes(shape):
    return lax.broadcasted_iota(jnp.int32, shape, len(shape) - 1)


def call(kernel, out_shapes, scratch, *operands, smem=(), away=()):
    specs = [
        pl.BlockSpec(memory_space=pltpu.SMEM if index in smem else pl.ANY if index in away else pltpu.VMEM)
        for index in range(len(operands))
    ]
    return pl.pallas_call(
        kernel,
        out_shape=[jax.ShapeDtypeStruct(shape, F32) for shape in out_shapes],
        in_specs=specs,
        out_specs=[pl.BlockSpec(memory_space=pltpu.VMEM)] * len(out_shapes),
        scratch_shapes=[pltpu.VMEM(shape, F32) if isinstance(shape, tuple) else shape for shape in scratch],
        compiler_params=pltpu.CompilerParams(vmem_limit_bytes=24 << 20),
    )(*operands)


def restrict(field, labels):
    rows = []
    for label in range(LABELS):
        kept = jnp.sum(jnp.where(labels == float(label), field, 0.0), axis=0)
        rows.append(jnp.sum(kept, axis=0, keepdims=True))
    sums = jnp.concatenate(rows, 0)
    even = lanes((8, 128)) % 2 == 0
    return sums + jnp.where(even, pltpu.roll(sums, 127, 1), pltpu.roll(sums, 1, 1))


def prolong(coarse, labels):
    field = jnp.zeros_like(labels)
    for label in range(LABELS):
        field = jnp.where(labels == float(label), coarse[label : label + 1, :][None], field)
    return field


def assemble(product_of, total_ref):
    total_ref[...] = jnp.zeros_like(total_ref)
    start = lanes((16, 128)) == 0
    for i in SPAN:
        low_a, high_a = {-1: (3, 4), 0: (0, 4), 1: (0, 3)}[i]
        for j in SPAN:
            product = product_of((i + 1) * 3 + j + 1)
            last = pltpu.roll(product[48:64], 1, 1)
            pieces = [
                product[0:16] + jnp.where(start, 0.0, last),
                product[16:32],
                product[32:48],
            ]
            for c in range(3):
                for b in range(4):
                    y = 3 * j + b
                    if 0 <= y < 6:
                        x = 3 * i + low_a
                        rows = pieces[c][4 * b + low_a : 4 * b + high_a]
                        total_ref[c * 6 + y, x : x + high_a - low_a, :] += rows


def unpack_kernel(source_hbm, potential_hbm, map_hbm, r_ref, ionic_ref, label_ref, coarse_ref,
                  rows_ref, turned_ref, source_ref, potential_ref, map_ref, sems):
    copies = [
        pltpu.make_async_copy(away, here, sems.at[index])
        for index, (away, here) in enumerate(
            ((source_hbm, source_ref), (potential_hbm, potential_ref), (map_hbm, map_ref))
        )
    ]
    for copy in copies:
        copy.start()
    rows_ref[...] = jnp.zeros_like(rows_ref)
    for copy in copies:
        copy.wait()
    for y in range(6):
        for x in range(6):
            row = y * 6 + x
            rows_ref[row : row + 1, :] = source_ref[x, y : y + 1, :]
            rows_ref[36 + row : 37 + row, :] = potential_ref[x, y : y + 1, :]
            rows_ref[72 + row : 73 + row, :] = map_ref[x, y : y + 1, :].astype(F32)
    for piece in range(3):
        turned_ref[128 * piece : 128 * piece + 128, :] = rows_ref[:, 128 * piece : 128 * piece + 128].T
    r_ref[...] = jnp.zeros_like(r_ref)
    ionic_ref[...] = jnp.zeros_like(ionic_ref)
    label_ref[...] = jnp.full_like(label_ref, -1.0)
    for c in range(3):
        split = turned_ref[pl.ds(c, 128, stride=3), :].T
        for y in range(6):
            r_ref[c * 6 + y, 0:6, :] = split[6 * y : 6 * y + 6]
            tangent = jnp.tanh(split[36 + 6 * y : 42 + 6 * y])
            ionic_ref[c * 6 + y, 0:6, :] = 1.0 + 2.0 * (1.0 - tangent * tangent)
            label_ref[c * 6 + y, 0:6, :] = split[72 + 6 * y : 78 + 6 * y]
    coarse_ref[...] = restrict(r_ref[...], label_ref[...])


def diagonal_kernel(own_ref, beside_ref, below_ref, table_ref, matrix_ref, ionic_ref, label_ref, coarse_ref,
                    sigma_ref, diagonal_ref, message_ref, total_ref):
    def conductance(region):
        value = jnp.zeros(region.shape, F32)
        for index in range(4):
            value = jnp.where(region == index + 1, table_ref[index], value)
        return value

    sigma_ref[0:3, :] = conductance(below_ref[...])
    for i in range(2):
        sigma_ref[3 + 3 * i : 4 + 3 * i, :] = conductance(beside_ref[i : i + 1, :])
        sigma_ref[4 + 3 * i : 6 + 3 * i, :] = conductance(own_ref[i] + 1)
    square = (64, 64)
    eye = lax.broadcasted_iota(jnp.int32, square, 0) == lax.broadcasted_iota(jnp.int32, square, 1)
    corner = jnp.sum(jnp.where(eye, matrix_ref[...], 0.0), axis=1, keepdims=True)
    assemble(lambda e: corner * sigma_ref[e : e + 1, :], total_ref)
    labels = label_ref[...]
    diagonal = jnp.where(labels < 0.0, 1.0, total_ref[...] + ionic_ref[...])
    diagonal_ref[...] = diagonal
    coarse_diag = SHARE * restrict(diagonal, labels)
    even = lanes((8, 128)) % 2 == 0
    message = jnp.where(even, coarse_ref[...], coarse_diag)
    message_ref[...] = jnp.broadcast_to(message[None], message_ref.shape)


def along(values):
    lane = lanes(values.shape)
    row = lax.broadcasted_iota(jnp.int32, values.shape, 1)
    after = pltpu.roll(values, 7, 1)
    carried = jnp.where(lane < 126, pltpu.roll(after, 126, 2), 0.0)
    after = jnp.where(row == 7, carried, after)
    before = pltpu.roll(values, 1, 1)
    carried = jnp.where(lane >= 2, pltpu.roll(before, 2, 2), 0.0)
    return after + jnp.where(row == 0, carried, before)


def smooth(start, valid):
    level = start
    for sweep in range(REACH):
        beside = level[2:] + level[:-2] + along(level[1:-1])
        here = slice(sweep + 1, 2 * REACH - sweep)
        level = start[here] + (1.0 - DAMPING) * level[1:-1] + (DAMPING * COUPLING) * beside
        level = level * valid[here]
    return level[0]


def around(place_ref, count):
    rows, valid = [], []
    for step in range(-REACH, REACH + 1):
        row = place_ref[0] + step
        inside = jnp.logical_and(row >= 0, row < count)
        rows.append(jnp.clip(row, 0, count - 1))
        valid.append(jnp.where(inside, jnp.ones((1, 8, 128), F32), 0.0))
    return rows, jnp.concatenate(valid, 0)


def even_part(tiles):
    even = lanes(tiles.shape) % 2 == 0
    return jnp.where(even, tiles, pltpu.roll(tiles, 1, tiles.ndim - 1))


def odd_part(tiles):
    even = lanes(tiles.shape) % 2 == 0
    return jnp.where(even, pltpu.roll(tiles, 127, tiles.ndim - 1), tiles)


def send_cross(field_ref, up_ref, down_ref):
    for c in range(3):
        up_ref[3 * c : 3 * c + 3] = field_ref[6 * c + 3 : 6 * c + 6]
        down_ref[c : c + 1] = field_ref[6 * c : 6 * c + 1]


def first_solve_kernel(place_ref, gathered_ref, r_ref, diagonal_ref, label_ref, z_ref, up_ref, down_ref, scale_ref):
    count = gathered_ref.shape[0]
    rows, valid = around(place_ref, count)
    near = jnp.concatenate([gathered_ref[pl.ds(row, 1)] for row in rows], 0)
    sums = jnp.sum(gathered_ref[...], axis=0)
    inverse = valid / jnp.sqrt(odd_part(near))
    share = 1.0 / odd_part(sums)
    scale_ref[0 : 2 * REACH + 1] = inverse
    scale_ref[2 * REACH + 1] = share
    level = smooth(DAMPING * even_part(near) * inverse, valid)
    coarse = level * inverse[REACH] + even_part(sums) * share
    z_ref[...] = r_ref[...] / diagonal_ref[...] + prolong(coarse, label_ref[...])
    send_cross(z_ref, up_ref, down_ref)


def next_solve_kernel(place_ref, gathered_ref, q_ref, diagonal_ref, label_ref, scale_ref, w_ref, up_ref, down_ref):
    rows, valid = around(place_ref, gathered_ref.shape[0])
    near = jnp.concatenate([gathered_ref[pl.ds(row, 1)] for row in rows], 0)
    sums = jnp.sum(gathered_ref[...], axis=0)
    inverse = scale_ref[0 : 2 * REACH + 1]
    level = smooth(DAMPING * near * inverse, valid)
    coarse = level * inverse[REACH] + sums * scale_ref[2 * REACH + 1]
    w_ref[...] = q_ref[...] / diagonal_ref[...] + prolong(coarse, label_ref[...])
    send_cross(w_ref, up_ref, down_ref)


def send_slab_kernel(field_ref, above_ref, under_ref, up_ref, down_ref):
    up_ref[90:96, :] = jnp.zeros((6, 128), F32)
    down_ref[30:32, :] = jnp.zeros((2, 128), F32)
    for c in range(3):
        for y in range(10):
            if y < 3:
                tile = above_ref[3 * c + y]
            elif y < 9:
                tile = field_ref[6 * c + y - 3]
            else:
                tile = under_ref[c]
            n = c * 10 + y
            up_ref[3 * n : 3 * n + 3, :] = tile[3:6]
            down_ref[n : n + 1, :] = tile[0:1]


def operate(field_ref, above_ref, under_ref, low_ref, high_ref, sigma_ref, matrix_ref, ionic_ref,
            grid_ref, local_ref, product_ref, total_ref):
    for c in range(3):
        for y in range(10):
            n = c * 10 + y
            if y < 3:
                tile = above_ref[3 * c + y]
            elif y < 9:
                tile = field_ref[6 * c + y - 3]
            else:
                tile = under_ref[c]
            grid_ref[n, 3:9, :] = tile[0:6]
            grid_ref[n, 0:3, :] = low_ref[3 * n : 3 * n + 3, :]
            grid_ref[n, 9:10, :] = high_ref[n : n + 1, :]
    end = lanes((10, 128)) == 127
    for y in range(10):
        grid_ref[30 + y, 0:10, :] = jnp.where(end, 0.0, pltpu.roll(grid_ref[y, 0:10, :], 127, 1))
    for i in SPAN:
        for j in SPAN:
            left = ((i + 1) * 3 + j + 1) * 128
            for c in range(4):
                for b in range(4):
                    row = 16 * c + 4 * b
                    n = c * 10 + 3 * (j + 1) + b
                    local_ref[row : row + 4, left : left + 128] = grid_ref[n, 3 * i + 3 : 3 * i + 7, :]
    matrix = matrix_ref[...]
    matrix_high = matrix.astype(BF16)
    matrix_low = (matrix - matrix_high.astype(F32)).astype(BF16)
    local = local_ref[...]
    high = local.astype(BF16)
    low = (local - high.astype(F32)).astype(BF16)
    dot = functools.partial(jnp.dot, preferred_element_type=F32)
    product_ref[...] = dot(matrix_high, high) + (dot(matrix_high, low) + dot(matrix_low, high))
    assemble(lambda e: product_ref[:, 128 * e : 128 * e + 128] * sigma_ref[e : e + 1, :], total_ref)
    return total_ref[...] + ionic_ref[...] * field_ref[...]


def first_image_kernel(z_ref, above_ref, under_ref, low_ref, high_ref, sigma_ref, matrix_ref, ionic_ref, label_ref,
                       q_ref, message_ref, *scratch):
    image = operate(z_ref, above_ref, under_ref, low_ref, high_ref, sigma_ref, matrix_ref, ionic_ref, *scratch)
    q_ref[...] = image
    message_ref[...] = jnp.broadcast_to(restrict(image, label_ref[...])[None], message_ref.shape)


def next_image_kernel(w_ref, above_ref, under_ref, low_ref, high_ref, sigma_ref, matrix_ref, ionic_ref,
                      r_ref, z_ref, q_ref, t_ref, tile_ref, *scratch):
    image = operate(w_ref, above_ref, under_ref, low_ref, high_ref, sigma_ref, matrix_ref, ionic_ref, *scratch)
    t_ref[...] = image
    r, z, q, w = r_ref[...], z_ref[...], q_ref[...], w_ref[...]
    rows = []
    for left, right in ((r, z), (z, q), (r, w), (q, w), (z, image), (w, image)):
        rows.append(jnp.sum(jnp.sum(left * right, axis=0), axis=0, keepdims=True))
    rows.append(jnp.zeros((2, 128), F32))
    tile_ref[...] = jnp.concatenate(rows, 0)


def finish_kernel(dots_ref, r_ref, z_ref, q_ref, w_ref, t_ref, solution_ref, residual_ref, rows_ref, turned_ref):
    dots = jnp.sum(jnp.sum(dots_ref[...], axis=0), axis=1, keepdims=True)
    rz, zq, rw, qw, zt, wt = [dots[index : index + 1] for index in range(6)]
    alpha = rz / zq
    rz_next = alpha * (alpha * qw - rw)
    beta = rz_next / rz
    more = 1.0 + beta
    second = rz_next / (more * more * zq - more * alpha * (zt + qw) + alpha * alpha * wt)
    from_z = alpha + second * more
    from_w = second * alpha
    rows_ref[...] = jnp.zeros_like(rows_ref)
    for c in range(3):
        for y in range(6):
            n = 6 * c + y
            answer = from_z * z_ref[n] - from_w * w_ref[n]
            left = r_ref[n] - from_z * q_ref[n] + from_w * t_ref[n]
            rows_ref[6 * y : 6 * y + 6, :] = answer[0:6]
            rows_ref[36 + 6 * y : 42 + 6 * y, :] = left[0:6]
        turned_ref[pl.ds(c, 128, stride=3), :] = rows_ref[...].T
    for piece in range(3):
        back = turned_ref[128 * piece : 128 * piece + 128, :].T
        for y in range(6):
            for x in range(6):
                row = y * 6 + x
                solution_ref[x, y : y + 1, 128 * piece : 128 * piece + 128] = back[row : row + 1]
                residual_ref[x, y : y + 1, 128 * piece : 128 * piece + 128] = back[36 + row : 37 + row]


def body(adjoint_source, potential, element_matrix, region_labels, conductivity, restriction_map):
    n_slab = lax.axis_size("slab")
    n_cross = lax.axis_size("cross")
    place = lax.axis_index("slab").astype(jnp.int32).reshape(1)
    def shifted(value, axis, step):
        count = lax.axis_size(axis)
        pairs = [(source, source + step) for source in range(count) if 0 <= source + step < count]
        return lax.ppermute(value, axis, pairs)

    def gather(copies):
        return lax.all_to_all(copies, "slab", 0, 0, tiled=True)

    def add_up(tile):
        step = 1
        while step < n_cross:
            tile = tile + lax.ppermute(tile, "cross", [(source, source ^ step) for source in range(n_cross)])
            step *= 2
        return gather(jnp.broadcast_to(tile[None], (n_slab, 8, 128)))

    field, above, under = (18, 8, 128), (9, 8, 128), (3, 8, 128)
    space = [(40, 16, 128), (64, 1152), (64, 1152), field]
    beside = shifted(region_labels[:, 1] + 1, "cross", 1)
    below = shifted(jnp.concatenate([beside[1:2], region_labels[1] + 1], 0), "slab", 1)
    r, ionic, labels, coarse = call(
        unpack_kernel, [field] * 3 + [(8, 128)],
        [(128, 384), (384, 128), (6, 6, 384), (6, 6, 384), pltpu.VMEM((6, 6, 384), jnp.int32), pltpu.SemaphoreType.DMA((3,))],
        adjoint_source, potential, restriction_map, away=(0, 1, 2),
    )
    sigma, diagonal, message = call(
        diagonal_kernel, [(9, 128), field, (n_slab, 8, 128)], [field],
        region_labels, beside, below, conductivity, element_matrix, ionic, labels, coarse, smem=(3,),
    )

    def with_halo(value, up, down):
        over = shifted(up, "cross", 1)
        low = shifted(down, "cross", -1)
        up, down = call(send_slab_kernel, [(96, 128), (32, 128)], [], value, over, low)
        return (value, over, low, shifted(up, "slab", 1), shifted(down, "slab", -1), sigma, element_matrix, ionic)

    z, up, down, scale = call(
        first_solve_kernel, [field, above, under, (8, 8, 128)], [], place, gather(message), r, diagonal, labels, smem=(0,)
    )
    q, message = call(first_image_kernel, [field, (n_slab, 8, 128)], space, *with_halo(z, up, down), labels)
    w, up, down = call(
        next_solve_kernel, [field, above, under], [], place, gather(message), q, diagonal, labels, scale, smem=(0,)
    )
    t, tile = call(next_image_kernel, [field, (8, 128)], space, *with_halo(w, up, down), r, z, q)
    return tuple(
        call(finish_kernel, [(6, 6, 384)] * 2, [(128, 128), (384, 128)], add_up(tile), r, z, q, w, t)
    )


def solution(mesh):
    return jax.shard_map(
        body,
        mesh=mesh,
        in_specs=(
            P("slab", "cross", None),
            P("slab", "cross", None),
            P(),
            P("slab", "cross", None),
            P(),
            P("slab", "cross", None),
        ),
        out_specs=(P("slab", "cross", None), P("slab", "cross", None)),
        check_vma=False,
    )
```

profile of v0, /device:TPU:24, one launch (start us, length us, event | category | flops | bytes accessed | tf_op | source)
XLA Modules:
  0.0 144.5 jit_solution(45745651319621893)
XLA Ops:
  0.6 0.7 slice.9
  1.3 0.0 copy-start.4
  1.3 2.0 %collective-permute-start = (s32[2,128]{1,0:T(2,128)S(1)}, s32[2,128]{1,0:T(2,128)S(1)}, u32[]{:S(2)}, u32[]{:S(2)}) collective-permute-start(s32[2,128]{1,0:T(2,128)S(1)} %add_bitcast_fusion.1), channel_id=1, source_target_pairs={{0,1},{1,2},{2,3},{3,4},{4,5},{5,6},{6,7},{8,9},{9,10},{10,11},{11... | collective-permute-start | bytes 3080 | tf_op jit(solution)/shard_map/ppermute | solution.py:319
  3.4 0.0 copy-done.4
  3.4 3.8 %collective-permute-done.beside_ref = s32[2,128]{1,0:T(2,128)S(1)} collective-permute-done((s32[2,128]{1,0:T(2,128)S(1)}, s32[2,128]{1,0:T(2,128)S(1)}, u32[]{:S(2)}, u32[]{:S(2)}) %collective-permute-start) | collective-permute-done | bytes 1056 | tf_op jit(solution)/shard_map/ppermute | solution.py:319
  7.2 0.0 copy-start
  7.3 4.2 %collective-permute-start.1 = (s32[3,128]{1,0:T(4,128)S(1)}, s32[3,128]{1,0:T(4,128)S(1)}, u32[]{:S(2)}, u32[]{:S(2)}) collective-permute-start(s32[3,128]{1,0:T(4,128)S(1)} %pad_add_fusion), channel_id=1, source_target_pairs={{0,8},{8,16},{16,24},{24,32},{32,40},{40,48},{48,56},{56,64},{64,7... | collective-permute-start | bytes 4616 | tf_op jit(solution)/shard_map/ppermute | solution.py:319
  11.4 0.0 copy-start.1
  11.4 0.9 copy-done.1
  12.3 0.0 copy-start.2
  12.3 0.9 copy-done.2
  13.2 0.0 copy-start.3
  13.2 0.9 copy-done.3
  14.1 0.7 shard_map.77
  14.8 0.0 collective-permute-done.1.below_ref
  14.8 0.0 copy-start.5
  14.8 0.0 copy-done
  14.8 0.6 copy-done.5
  15.5 1.6 %shard_map.78 = (f32[9,128]{1,0:T(8,128)S(1)}, f32[18,8,128]{2,1,0:T(8,128)S(1)}, f32[64,8,128]{2,1,0:T(8,128)}) custom-call(s32[2,2,128]{2,1,0:T(2,128)S(1)} %copy-done.4, s32[2,128]{1,0:T(2,128)S(1)} %collective-permute-done.beside_ref, s32[3,128]{1,0:T(4,128)S(1)} %collective-permute-done.1.below_ref, f32[4]{0:T(128)S(1)} %copy-done.5, ...), custom_call_target="tpu_custom_call" | custom-call | tf_op jit(solution)/shard_map/pallas_call | solution.py:31
  17.1 13.9 %all-to-all-start = ((f32[64,8,128]{2,1,0:T(8,128)}), f32[64,8,128]{2,1,0:T(8,128)S(1)}, u32[]{:S(2)}, u32[]{:S(2)}) async-start(f32[64,8,128]{2,1,0:T(8,128)} %get-tuple-element.27), calls=%async_computation | async-start | bytes 524288 | tf_op jit(solution)/shard_map/all_to_all | solution.py:322
  31.0 12.4 %all-to-all-done.gathered_ref = f32[64,8,128]{2,1,0:T(8,128)S(1)} async-done(((f32[64,8,128]{2,1,0:T(8,128)}), f32[64,8,128]{2,1,0:T(8,128)S(1)}, u32[]{:S(2)}, u32[]{:S(2)}) %all-to-all-start) | async-done | bytes 262176 | tf_op jit(solution)/shard_map/all_to_all | solution.py:322
  43.4 0.4 shard_map.79
  43.7 1.9 %collective-permute-start.2 = (f32[9,8,128]{2,1,0:T(8,128)S(1)}, f32[9,8,128]{2,1,0:T(8,128)S(1)}, u32[]{:S(2)}, u32[]{:S(2)}) collective-permute-start(f32[9,8,128]{2,1,0:T(8,128)S(1)} %get-tuple-element.31), channel_id=1, source_target_pairs={{0,1},{1,2},{2,3},{3,4},{4,5},{5,6},{6,7},{8,9},{9,10},{10,11},{11... | collective-permute-start | bytes 110600 | tf_op jit(solution)/shard_map/ppermute | solution.py:319
  45.7 4.5 %collective-permute-start.3 = (f32[3,8,128]{2,1,0:T(8,128)S(1)}, f32[3,8,128]{2,1,0:T(8,128)S(1)}, u32[]{:S(2)}, u32[]{:S(2)}) collective-permute-start(f32[3,8,128]{2,1,0:T(8,128)S(1)} %get-tuple-element.32), channel_id=1, source_target_pairs={{1,0},{2,1},{3,2},{4,3},{5,4},{6,5},{7,6},{9,8},{10,9},{11,10},{12... | collective-permute-start | bytes 36872 | tf_op jit(solution)/shard_map/ppermute | solution.py:319
  50.2 1.9 %collective-permute-done.3.under_ref = f32[3,8,128]{2,1,0:T(8,128)S(1)} collective-permute-done((f32[3,8,128]{2,1,0:T(8,128)S(1)}, f32[3,8,128]{2,1,0:T(8,128)S(1)}, u32[]{:S(2)}, u32[]{:S(2)}) %collective-permute-start.3) | collective-permute-done | bytes 12320 | tf_op jit(solution)/shard_map/ppermute | solution.py:319
  52.1 0.0 collective-permute-done.2.above_ref
  52.1 3.2 %collective-permute-start.4 = (f32[96,128]{1,0:T(8,128)S(1)}, f32[96,128]{1,0:T(8,128)S(1)}, u32[]{:S(2)}, u32[]{:S(2)}) collective-permute-start(f32[96,128]{1,0:T(8,128)S(1)} %get-tuple-element.33), channel_id=1, source_target_pairs={{0,8},{8,16},{16,24},{24,32},{32,40},{40,48},{48,56},{56,64},{64,7... | collective-permute-start | bytes 147464 | tf_op jit(solution)/shard_map/ppermute | solution.py:319
  55.3 2.7 %collective-permute-start.5 = (f32[32,128]{1,0:T(8,128)S(1)}, f32[32,128]{1,0:T(8,128)S(1)}, u32[]{:S(2)}, u32[]{:S(2)}) collective-permute-start(f32[32,128]{1,0:T(8,128)S(1)} %get-tuple-element.34), channel_id=1, source_target_pairs={{8,0},{16,8},{24,16},{32,24},{40,32},{48,40},{56,48},{64,56},{72,6... | collective-permute-start | bytes 49160 | tf_op jit(solution)/shard_map/ppermute | solution.py:319
  58.0 4.0 %collective-permute-done.5.high_ref = f32[32,128]{1,0:T(8,128)S(1)} collective-permute-done((f32[32,128]{1,0:T(8,128)S(1)}, f32[32,128]{1,0:T(8,128)S(1)}, u32[]{:S(2)}, u32[]{:S(2)}) %collective-permute-start.5) | collective-permute-done | bytes 16416 | tf_op jit(solution)/shard_map/ppermute | solution.py:319
  62.0 0.0 collective-permute-done.4.low_ref
  62.0 0.6 shard_map.81
  62.6 21.5 %all_to_all.15.gathered_ref = f32[64,8,128]{2,1,0:T(8,128)S(1)} all-to-all(f32[64,8,128]{2,1,0:T(8,128)S(1)} %get-tuple-element.36), channel_id=1, replica_groups=mesh['slab'=64,'cross'=8] {'slab'}, dimensions={0} | all-to-all | bytes 524288 | tf_op jit(solution)/shard_map/all_to_all | solution.py:322
  84.1 0.3 shard_map.82
  84.4 2.3 %collective-permute-start.6 = (f32[9,8,128]{2,1,0:T(8,128)S(1)}, f32[9,8,128]{2,1,0:T(8,128)S(1)}, u32[]{:S(2)}, u32[]{:S(2)}) collective-permute-start(f32[9,8,128]{2,1,0:T(8,128)S(1)} %get-tuple-element.40), channel_id=1, source_target_pairs={{0,1},{1,2},{2,3},{3,4},{4,5},{5,6},{6,7},{8,9},{9,10},{10,11},{11... | collective-permute-start | bytes 110600 | tf_op jit(solution)/shard_map/ppermute | solution.py:319
  86.7 4.2 %collective-permute-start.7 = (f32[3,8,128]{2,1,0:T(8,128)S(1)}, f32[3,8,128]{2,1,0:T(8,128)S(1)}, u32[]{:S(2)}, u32[]{:S(2)}) collective-permute-start(f32[3,8,128]{2,1,0:T(8,128)S(1)} %get-tuple-element.41), channel_id=1, source_target_pairs={{1,0},{2,1},{3,2},{4,3},{5,4},{6,5},{7,6},{9,8},{10,9},{11,10},{12... | collective-permute-start | bytes 36872 | tf_op jit(solution)/shard_map/ppermute | solution.py:319
  90.9 1.4 collective-permute-done.7.under_ref
  92.3 0.0 collective-permute-done.6.above_ref
  92.3 1.9 %collective-permute-start.8 = (f32[96,128]{1,0:T(8,128)S(1)}, f32[96,128]{1,0:T(8,128)S(1)}, u32[]{:S(2)}, u32[]{:S(2)}) collective-permute-start(f32[96,128]{1,0:T(8,128)S(1)} %get-tuple-element.42), channel_id=1, source_target_pairs={{0,8},{8,16},{16,24},{24,32},{32,40},{40,48},{48,56},{56,64},{64,7... | collective-permute-start | bytes 147464 | tf_op jit(solution)/shard_map/ppermute | solution.py:319
  94.2 3.9 %collective-permute-start.9 = (f32[32,128]{1,0:T(8,128)S(1)}, f32[32,128]{1,0:T(8,128)S(1)}, u32[]{:S(2)}, u32[]{:S(2)}) collective-permute-start(f32[32,128]{1,0:T(8,128)S(1)} %get-tuple-element.43), channel_id=1, source_target_pairs={{8,0},{16,8},{24,16},{32,24},{40,32},{48,40},{56,48},{64,56},{72,6... | collective-permute-start | bytes 49160 | tf_op jit(solution)/shard_map/ppermute | solution.py:319
  98.2 2.6 %collective-permute-done.9.high_ref = f32[32,128]{1,0:T(8,128)S(1)} collective-permute-done((f32[32,128]{1,0:T(8,128)S(1)}, f32[32,128]{1,0:T(8,128)S(1)}, u32[]{:S(2)}, u32[]{:S(2)}) %collective-permute-start.9) | collective-permute-done | bytes 16416 | tf_op jit(solution)/shard_map/ppermute | solution.py:319
  100.8 0.0 collective-permute-done.8.low_ref
  100.8 0.5 shard_map.84
  101.3 4.8 %collective-permute-start.10 = (f32[8,128]{1,0:T(8,128)S(1)}, f32[8,128]{1,0:T(8,128)S(1)}, u32[]{:S(2)}, u32[]{:S(2)}) collective-permute-start(f32[8,128]{1,0:T(8,128)S(1)} %get-tuple-element.44), channel_id=1, source_target_pairs={{0,1},{1,0},{2,3},{3,2},{4,5},{5,4},{6,7},{7,6},{8,9},{9,8},{10,11... | collective-permute-start | bytes 12296 | tf_op jit(solution)/shard_map/ppermute | solution.py:327
  106.0 0.8 collective-permute-done.10
  106.9 1.9 %collective-permute-start.11 = (f32[8,128]{1,0:T(8,128)S(1)}, f32[8,128]{1,0:T(8,128)S(1)}, u32[]{:S(2)}, u32[]{:S(2)}) collective-permute-start(f32[8,128]{1,0:T(8,128)S(1)} %add.25), channel_id=1, source_target_pairs={{0,2},{1,3},{2,0},{3,1},{4,6},{5,7},{6,4},{7,5},{8,10},{9,11},{10,... | collective-permute-start | bytes 12296 | tf_op jit(solution)/shard_map/ppermute | solution.py:327
  108.8 4.5 %collective-permute-done.11 = f32[8,128]{1,0:T(8,128)S(1)} collective-permute-done((f32[8,128]{1,0:T(8,128)S(1)}, f32[8,128]{1,0:T(8,128)S(1)}, u32[]{:S(2)}, u32[]{:S(2)}) %collective-permute-start.11) | collective-permute-done | bytes 4128 | tf_op jit(solution)/shard_map/ppermute | solution.py:327
  113.2 2.9 %collective-permute-start.12 = (f32[8,128]{1,0:T(8,128)S(1)}, f32[8,128]{1,0:T(8,128)S(1)}, u32[]{:S(2)}, u32[]{:S(2)}) collective-permute-start(f32[8,128]{1,0:T(8,128)S(1)} %add.26), channel_id=1, source_target_pairs={{0,4},{1,5},{2,6},{3,7},{4,0},{5,1},{6,2},{7,3},{8,12},{9,13},{10,... | collective-permute-start | bytes 12296 | tf_op jit(solution)/shard_map/ppermute | solution.py:327
  116.2 6.4 %collective-permute-done.12 = f32[8,128]{1,0:T(8,128)S(1)} collective-permute-done((f32[8,128]{1,0:T(8,128)S(1)}, f32[8,128]{1,0:T(8,128)S(1)}, u32[]{:S(2)}, u32[]{:S(2)}) %collective-permute-start.12) | collective-permute-done | bytes 4128 | tf_op jit(solution)/shard_map/ppermute | solution.py:327
  122.7 20.7 %all_to_all.16.dots_ref = f32[64,8,128]{2,1,0:T(8,128)S(1)} all-to-all(f32[64,8,128]{2,1,0:T(8,128)S(1)} %broadcast_in_dim.2), channel_id=1, replica_groups=mesh['slab'=64,'cross'=8] {'slab'}, dimensions={0} | all-to-all | bytes 524288 | tf_op jit(solution)/shard_map/all_to_all | solution.py:322
  143.4 1.1 shard_map.85
  (10 shorter events, 0.1 us)
Async XLA Ops:
  1.3 2.1 %copy-start.4 = (s32[2,2,128]{2,1,0:T(2,128)S(1)}, s32[2,2,128]{2,1,0:T(2,128)}, u32[]{:S(2)}) copy-start(s32[2,2,128]{2,1,0:T(2,128)} %own_ref.1) | copy-start | bytes 6148
  1.3 5.9 %collective-permute-start = (s32[2,128]{1,0:T(2,128)S(1)}, s32[2,128]{1,0:T(2,128)S(1)}, u32[]{:S(2)}, u32[]{:S(2)}) collective-permute-start(s32[2,128]{1,0:T(2,128)S(1)} %add_bitcast_fusion.1), channel_id=1, source_target_pairs={{0,1},{1,2},{2,3},{3,4},{4,5},{5,6},{6,7},{8,9},{9,10},{10,11},{11... | collective-permute-start | bytes 3080 | tf_op jit(solution)/shard_map/ppermute | solution.py:319
  7.2 7.6 %copy-start = (f32[64,64]{1,0:T(8,128)S(1)}, f32[64,64]{1,0:T(8,128)}, u32[]{:S(2)}) copy-start(f32[64,64]{1,0:T(8,128)} %matrix_ref.5) | copy-start | bytes 49156
  7.3 7.6 %collective-permute-start.1 = (s32[3,128]{1,0:T(4,128)S(1)}, s32[3,128]{1,0:T(4,128)S(1)}, u32[]{:S(2)}, u32[]{:S(2)}) collective-permute-start(s32[3,128]{1,0:T(4,128)S(1)} %pad_add_fusion), channel_id=1, source_target_pairs={{0,8},{8,16},{16,24},{24,32},{32,40},{40,48},{48,56},{56,64},{64,7... | collective-permute-start | bytes 4616 | tf_op jit(solution)/shard_map/ppermute | solution.py:319
  11.4 0.9 copy-start.1
  12.3 0.9 copy-start.2
  13.2 0.9 copy-start.3
  14.8 0.7 copy-start.5
  17.1 26.2 %all-to-all-start = ((f32[64,8,128]{2,1,0:T(8,128)}), f32[64,8,128]{2,1,0:T(8,128)S(1)}, u32[]{:S(2)}, u32[]{:S(2)}) async-start(f32[64,8,128]{2,1,0:T(8,128)} %get-tuple-element.27), calls=%async_computation | async-start | bytes 524288 | tf_op jit(solution)/shard_map/all_to_all | solution.py:322
  43.7 8.4 %collective-permute-start.2 = (f32[9,8,128]{2,1,0:T(8,128)S(1)}, f32[9,8,128]{2,1,0:T(8,128)S(1)}, u32[]{:S(2)}, u32[]{:S(2)}) collective-permute-start(f32[9,8,128]{2,1,0:T(8,128)S(1)} %get-tuple-element.31), channel_id=1, source_target_pairs={{0,1},{1,2},{2,3},{3,4},{4,5},{5,6},{6,7},{8,9},{9,10},{10,11},{11... | collective-permute-start | bytes 110600 | tf_op jit(solution)/shard_map/ppermute | solution.py:319
  45.7 6.5 %collective-permute-start.3 = (f32[3,8,128]{2,1,0:T(8,128)S(1)}, f32[3,8,128]{2,1,0:T(8,128)S(1)}, u32[]{:S(2)}, u32[]{:S(2)}) collective-permute-start(f32[3,8,128]{2,1,0:T(8,128)S(1)} %get-tuple-element.32), channel_id=1, source_target_pairs={{1,0},{2,1},{3,2},{4,3},{5,4},{6,5},{7,6},{9,8},{10,9},{11,10},{12... | collective-permute-start | bytes 36872 | tf_op jit(solution)/shard_map/ppermute | solution.py:319
  52.1 9.9 %collective-permute-start.4 = (f32[96,128]{1,0:T(8,128)S(1)}, f32[96,128]{1,0:T(8,128)S(1)}, u32[]{:S(2)}, u32[]{:S(2)}) collective-permute-start(f32[96,128]{1,0:T(8,128)S(1)} %get-tuple-element.33), channel_id=1, source_target_pairs={{0,8},{8,16},{16,24},{24,32},{32,40},{40,48},{48,56},{56,64},{64,7... | collective-permute-start | bytes 147464 | tf_op jit(solution)/shard_map/ppermute | solution.py:319
  55.3 6.7 %collective-permute-start.5 = (f32[32,128]{1,0:T(8,128)S(1)}, f32[32,128]{1,0:T(8,128)S(1)}, u32[]{:S(2)}, u32[]{:S(2)}) collective-permute-start(f32[32,128]{1,0:T(8,128)S(1)} %get-tuple-element.34), channel_id=1, source_target_pairs={{8,0},{16,8},{24,16},{32,24},{40,32},{48,40},{56,48},{64,56},{72,6... | collective-permute-start | bytes 49160 | tf_op jit(solution)/shard_map/ppermute | solution.py:319
  84.4 7.9 %collective-permute-start.6 = (f32[9,8,128]{2,1,0:T(8,128)S(1)}, f32[9,8,128]{2,1,0:T(8,128)S(1)}, u32[]{:S(2)}, u32[]{:S(2)}) collective-permute-start(f32[9,8,128]{2,1,0:T(8,128)S(1)} %get-tuple-element.40), channel_id=1, source_target_pairs={{0,1},{1,2},{2,3},{3,4},{4,5},{5,6},{6,7},{8,9},{9,10},{10,11},{11... | collective-permute-start | bytes 110600 | tf_op jit(solution)/shard_map/ppermute | solution.py:319
  86.7 5.6 %collective-permute-start.7 = (f32[3,8,128]{2,1,0:T(8,128)S(1)}, f32[3,8,128]{2,1,0:T(8,128)S(1)}, u32[]{:S(2)}, u32[]{:S(2)}) collective-permute-start(f32[3,8,128]{2,1,0:T(8,128)S(1)} %get-tuple-element.41), channel_id=1, source_target_pairs={{1,0},{2,1},{3,2},{4,3},{5,4},{6,5},{7,6},{9,8},{10,9},{11,10},{12... | collective-permute-start | bytes 36872 | tf_op jit(solution)/shard_map/ppermute | solution.py:319
  92.3 8.5 %collective-permute-start.8 = (f32[96,128]{1,0:T(8,128)S(1)}, f32[96,128]{1,0:T(8,128)S(1)}, u32[]{:S(2)}, u32[]{:S(2)}) collective-permute-start(f32[96,128]{1,0:T(8,128)S(1)} %get-tuple-element.42), channel_id=1, source_target_pairs={{0,8},{8,16},{16,24},{24,32},{32,40},{40,48},{48,56},{56,64},{64,7... | collective-permute-start | bytes 147464 | tf_op jit(solution)/shard_map/ppermute | solution.py:319
  94.2 6.5 %collective-permute-start.9 = (f32[32,128]{1,0:T(8,128)S(1)}, f32[32,128]{1,0:T(8,128)S(1)}, u32[]{:S(2)}, u32[]{:S(2)}) collective-permute-start(f32[32,128]{1,0:T(8,128)S(1)} %get-tuple-element.43), channel_id=1, source_target_pairs={{8,0},{16,8},{24,16},{32,24},{40,32},{48,40},{56,48},{64,56},{72,6... | collective-permute-start | bytes 49160 | tf_op jit(solution)/shard_map/ppermute | solution.py:319
  101.3 5.6 %collective-permute-start.10 = (f32[8,128]{1,0:T(8,128)S(1)}, f32[8,128]{1,0:T(8,128)S(1)}, u32[]{:S(2)}, u32[]{:S(2)}) collective-permute-start(f32[8,128]{1,0:T(8,128)S(1)} %get-tuple-element.44), channel_id=1, source_target_pairs={{0,1},{1,0},{2,3},{3,2},{4,5},{5,4},{6,7},{7,6},{8,9},{9,8},{10,11... | collective-permute-start | bytes 12296 | tf_op jit(solution)/shard_map/ppermute | solution.py:327
  106.9 6.4 %collective-permute-start.11 = (f32[8,128]{1,0:T(8,128)S(1)}, f32[8,128]{1,0:T(8,128)S(1)}, u32[]{:S(2)}, u32[]{:S(2)}) collective-permute-start(f32[8,128]{1,0:T(8,128)S(1)} %add.25), channel_id=1, source_target_pairs={{0,2},{1,3},{2,0},{3,1},{4,6},{5,7},{6,4},{7,5},{8,10},{9,11},{10,... | collective-permute-start | bytes 12296 | tf_op jit(solution)/shard_map/ppermute | solution.py:327
  113.2 9.4 %collective-permute-start.12 = (f32[8,128]{1,0:T(8,128)S(1)}, f32[8,128]{1,0:T(8,128)S(1)}, u32[]{:S(2)}, u32[]{:S(2)}) collective-permute-start(f32[8,128]{1,0:T(8,128)S(1)} %add.26), channel_id=1, source_target_pairs={{0,4},{1,5},{2,6},{3,7},{4,0},{5,1},{6,2},{7,3},{8,12},{9,13},{10,... | collective-permute-start | bytes 12296 | tf_op jit(solution)/shard_map/ppermute | solution.py:327
where the time goes:
time: 145 us
  starting transfers between devices  54.3 us (37%)
  blocking collectives  42.3 us (29%)
  waiting for transfers between devices  37.8 us (26%)
  Pallas kernels  5.22 us (4%)
  local copies, waits for them, and re-layouts  4.01 us (3%)
    all_to_all x2, blocking collectives, gather(): return lax.all_to_all(copies, 'slab', 0, 0, tiled=True)  42.3 us
    ppermute x10, starting transfers between devices, shifted(): return lax.ppermute(value, axis, pairs)  30.8 us
    all_to_all x1, starting transfers between devices, gather(): return lax.all_to_all(copies, 'slab', 0, 0, tiled=True)  13.9 us
    ppermute x10, waiting for transfers between devices, shifted(): return lax.ppermute(value, axis, pairs)  13.8 us
    all_to_all x1, waiting for transfers between devices, gather(): return lax.all_to_all(copies, 'slab', 0, 0, tiled=True)  12.4 us
    ppermute x3, waiting for transfers between devices, add_up(): lax.ppermute(tile, 'cross', [(source, source ^ step) for source in range(...  11.7 us
    ppermute x3, starting transfers between devices, add_up(): lax.ppermute(tile, 'cross', [(source, source ^ step) for source in range(...  9.65 us
    pallas_call x9, Pallas kernels, call(): pl.pallas_call(kernel, out_shape=[jax.ShapeDtypeStruct(shape, F32) for sh...  5.22 us
  transfers between devices with their start and end apart: 14, of which 9 were waited for; matrix products, arithmetic and copies ran while one was open for 0% of the time, Pallas kernels for 0%

commit v1 on v0

--- a/solution.py
+++ b/solution.py
@@ -12,6 +12,7 @@
 COUPLING = 0.2
 SHARE = 0.1
 REACH = 3
+NEAR = REACH + 1
 
 
 F32 = jnp.float32
@@ -25,7 +26,7 @@
 
 def call(kernel, out_shapes, scratch, *operands, smem=(), away=()):
     specs = [
-        pl.BlockSpec(memory_space=pltpu.SMEM if index in smem else pl.ANY if index in away else pltpu.VMEM)
+        pl.BlockSpec(memory_space=pltpu.SMEM if index in smem else pltpu.HBM if index in away else pltpu.VMEM)
         for index in range(len(operands))
     ]
     return pl.pallas_call(
@@ -41,7 +42,7 @@
 def restrict(field, labels):
     rows = []
     for label in range(LABELS):
-        kept = jnp.sum(jnp.where(labels == float(label), field, 0.0), axis=0)
+        kept = jnp.sum(jnp.where(labels == label + 1.0, field, 0.0), axis=0)
         rows.append(jnp.sum(kept, axis=0, keepdims=True))
     sums = jnp.concatenate(rows, 0)
     even = lanes((8, 128)) % 2 == 0
@@ -49,9 +50,12 @@
 
 
 def prolong(coarse, labels):
+    row = lax.broadcasted_iota(jnp.int32, (16, 128), 0)
     field = jnp.zeros_like(labels)
     for label in range(LABELS):
-        field = jnp.where(labels == float(label), coarse[label : label + 1, :][None], field)
+        low, own, high = [coarse[step, label : label + 1, :] for step in range(3)]
+        values = jnp.where(row < 3, low, jnp.where(row < 9, own, high))
+        field = jnp.where(labels == label + 1.0, values[None], field)
     return field
 
 
@@ -100,26 +104,33 @@
         turned_ref[128 * piece : 128 * piece + 128, :] = rows_ref[:, 128 * piece : 128 * piece + 128].T
     r_ref[...] = jnp.zeros_like(r_ref)
     ionic_ref[...] = jnp.zeros_like(ionic_ref)
-    label_ref[...] = jnp.full_like(label_ref, -1.0)
+    label_ref[...] = jnp.zeros_like(label_ref)
     for c in range(3):
         split = turned_ref[pl.ds(c, 128, stride=3), :].T
         for y in range(6):
             r_ref[c * 6 + y, 0:6, :] = split[6 * y : 6 * y + 6]
             tangent = jnp.tanh(split[36 + 6 * y : 42 + 6 * y])
             ionic_ref[c * 6 + y, 0:6, :] = 1.0 + 2.0 * (1.0 - tangent * tangent)
-            label_ref[c * 6 + y, 0:6, :] = split[72 + 6 * y : 78 + 6 * y]
+            label_ref[c * 6 + y, 0:6, :] = split[72 + 6 * y : 78 + 6 * y] + 1.0
     coarse_ref[...] = restrict(r_ref[...], label_ref[...])
 
 
-def diagonal_kernel(own_ref, beside_ref, below_ref, table_ref, matrix_ref, ionic_ref, label_ref, coarse_ref,
-                    sigma_ref, diagonal_ref, message_ref, total_ref):
+def send_slab(field_ref, up_ref, down_ref, up_start, down_start):
+    for n in range(18):
+        up_ref[up_start + 3 * n : up_start + 3 * n + 3, :] = field_ref[n, 3:6, :]
+        down_ref[down_start + n : down_start + n + 1, :] = field_ref[n, 0:1, :]
+
+
+def diagonal_kernel(own_ref, beside_ref, below_ref, corner_ref, table_ref, matrix_ref, r_ref, ionic_ref, label_ref,
+                    coarse_ref, sigma_ref, diagonal_ref, scaled_ref, message_ref, up_ref, down_ref, total_ref):
     def conductance(region):
         value = jnp.zeros(region.shape, F32)
         for index in range(4):
             value = jnp.where(region == index + 1, table_ref[index], value)
         return value
 
-    sigma_ref[0:3, :] = conductance(below_ref[...])
+    sigma_ref[0:1, :] = conductance(corner_ref[...])
+    sigma_ref[1:3, :] = conductance(below_ref[...])
     for i in range(2):
         sigma_ref[3 + 3 * i : 4 + 3 * i, :] = conductance(beside_ref[i : i + 1, :])
         sigma_ref[4 + 3 * i : 6 + 3 * i, :] = conductance(own_ref[i] + 1)
@@ -128,12 +139,17 @@
     corner = jnp.sum(jnp.where(eye, matrix_ref[...], 0.0), axis=1, keepdims=True)
     assemble(lambda e: corner * sigma_ref[e : e + 1, :], total_ref)
     labels = label_ref[...]
-    diagonal = jnp.where(labels < 0.0, 1.0, total_ref[...] + ionic_ref[...])
+    diagonal = jnp.where(labels == 0.0, 1.0, total_ref[...] + ionic_ref[...])
     diagonal_ref[...] = diagonal
     coarse_diag = SHARE * restrict(diagonal, labels)
     even = lanes((8, 128)) % 2 == 0
     message = jnp.where(even, coarse_ref[...], coarse_diag)
     message_ref[...] = jnp.broadcast_to(message[None], message_ref.shape)
+    scaled_ref[...] = r_ref[...] / diagonal
+    up_ref[...] = jnp.zeros_like(up_ref)
+    down_ref[...] = jnp.zeros_like(down_ref)
+    send_slab(scaled_ref, up_ref, down_ref, 0, 0)
+    send_slab(label_ref, up_ref, down_ref, 56, 20)
 
 
 def along(values):
@@ -151,15 +167,15 @@
     level = start
     for sweep in range(REACH):
         beside = level[2:] + level[:-2] + along(level[1:-1])
-        here = slice(sweep + 1, 2 * REACH - sweep)
+        here = slice(sweep + 1, 2 * NEAR - sweep)
         level = start[here] + (1.0 - DAMPING) * level[1:-1] + (DAMPING * COUPLING) * beside
         level = level * valid[here]
-    return level[0]
+    return level
 
 
 def around(place_ref, count):
     rows, valid = [], []
-    for step in range(-REACH, REACH + 1):
+    for step in range(-NEAR, NEAR + 1):
         row = place_ref[0] + step
         inside = jnp.logical_and(row >= 0, row < count)
         rows.append(jnp.clip(row, 0, count - 1))
@@ -177,68 +193,69 @@
     return jnp.where(even, pltpu.roll(tiles, 127, tiles.ndim - 1), tiles)
 
 
-def send_cross(field_ref, up_ref, down_ref):
+def widen(field_ref, low_ref, high_ref, low_start, high_start, wide_ref):
+    wide_ref[...] = jnp.zeros_like(wide_ref)
+    for n in range(18):
+        wide_ref[n, 0:3, :] = low_ref[low_start + 3 * n : low_start + 3 * n + 3, :]
+        wide_ref[n, 3:9, :] = field_ref[n, 0:6, :]
+        wide_ref[n, 9:10, :] = high_ref[high_start + n : high_start + n + 1, :]
+
+
+def send_cross(wide_ref, own_ref, up_ref, down_ref):
+    own_ref[...] = jnp.zeros_like(own_ref)
+    for n in range(18):
+        own_ref[n, 0:6, :] = wide_ref[n, 3:9, :]
+    up_ref[90:96, :] = jnp.zeros((6, 128), F32)
+    down_ref[30:32, :] = jnp.zeros((2, 128), F32)
     for c in range(3):
-        up_ref[3 * c : 3 * c + 3] = field_ref[6 * c + 3 : 6 * c + 6]
-        down_ref[c : c + 1] = field_ref[6 * c : 6 * c + 1]
-
-
-def first_solve_kernel(place_ref, gathered_ref, r_ref, diagonal_ref, label_ref, z_ref, up_ref, down_ref, scale_ref):
-    count = gathered_ref.shape[0]
-    rows, valid = around(place_ref, count)
+        for y in range(3):
+            row = (3 * c + y) * 10
+            up_ref[row : row + 10, :] = wide_ref[6 * c + 3 + y, 0:10, :]
+        down_ref[10 * c : 10 * c + 10, :] = wide_ref[6 * c, 0:10, :]
+
+
+def first_solve_kernel(place_ref, gathered_ref, scaled_ref, label_ref, low_ref, high_ref,
+                       wide_ref, z_ref, up_ref, down_ref, scale_ref, wide_label_ref):
+    rows, valid = around(place_ref, gathered_ref.shape[0])
     near = jnp.concatenate([gathered_ref[pl.ds(row, 1)] for row in rows], 0)
     sums = jnp.sum(gathered_ref[...], axis=0)
     inverse = valid / jnp.sqrt(odd_part(near))
     share = 1.0 / odd_part(sums)
-    scale_ref[0 : 2 * REACH + 1] = inverse
-    scale_ref[2 * REACH + 1] = share
+    scale_ref[0 : 2 * NEAR + 1] = inverse
+    scale_ref[2 * NEAR + 1] = share
     level = smooth(DAMPING * even_part(near) * inverse, valid)
-    coarse = level * inverse[REACH] + even_part(sums) * share
-    z_ref[...] = r_ref[...] / diagonal_ref[...] + prolong(coarse, label_ref[...])
-    send_cross(z_ref, up_ref, down_ref)
-
-
-def next_solve_kernel(place_ref, gathered_ref, q_ref, diagonal_ref, label_ref, scale_ref, w_ref, up_ref, down_ref):
+    coarse = level * inverse[REACH : REACH + 3] + (even_part(sums) * share)[None]
+    widen(label_ref, low_ref, high_ref, 56, 20, wide_label_ref)
+    widen(scaled_ref, low_ref, high_ref, 0, 0, wide_ref)
+    wide_ref[...] += prolong(coarse, wide_label_ref[...])
+    send_cross(wide_ref, z_ref, up_ref, down_ref)
+
+
+def next_solve_kernel(place_ref, gathered_ref, scaled_ref, wide_label_ref, low_ref, high_ref, scale_ref,
+                      wide_ref, w_ref, up_ref, down_ref):
     rows, valid = around(place_ref, gathered_ref.shape[0])
     near = jnp.concatenate([gathered_ref[pl.ds(row, 1)] for row in rows], 0)
     sums = jnp.sum(gathered_ref[...], axis=0)
-    inverse = scale_ref[0 : 2 * REACH + 1]
+    inverse = scale_ref[0 : 2 * NEAR + 1]
     level = smooth(DAMPING * near * inverse, valid)
-    coarse = level * inverse[REACH] + sums * scale_ref[2 * REACH + 1]
-    w_ref[...] = q_ref[...] / diagonal_ref[...] + prolong(coarse, label_ref[...])
-    send_cross(w_ref, up_ref, down_ref)
-
-
-def send_slab_kernel(field_ref, above_ref, under_ref, up_ref, down_ref):
-    up_ref[90:96, :] = jnp.zeros((6, 128), F32)
-    down_ref[30:32, :] = jnp.zeros((2, 128), F32)
-    for c in range(3):
-        for y in range(10):
-            if y < 3:
-                tile = above_ref[3 * c + y]
-            elif y < 9:
-                tile = field_ref[6 * c + y - 3]
-            else:
-                tile = under_ref[c]
-            n = c * 10 + y
-            up_ref[3 * n : 3 * n + 3, :] = tile[3:6]
-            down_ref[n : n + 1, :] = tile[0:1]
-
-
-def operate(field_ref, above_ref, under_ref, low_ref, high_ref, sigma_ref, matrix_ref, ionic_ref,
+    coarse = level * inverse[REACH : REACH + 3] + (sums * scale_ref[2 * NEAR + 1])[None]
+    widen(scaled_ref, low_ref, high_ref, 0, 0, wide_ref)
+    wide_ref[...] += prolong(coarse, wide_label_ref[...])
+    send_cross(wide_ref, w_ref, up_ref, down_ref)
+
+
+def operate(wide_ref, field_ref, above_ref, under_ref, sigma_ref, matrix_ref, ionic_ref,
             grid_ref, local_ref, product_ref, total_ref):
     for c in range(3):
         for y in range(10):
             n = c * 10 + y
             if y < 3:
-                tile = above_ref[3 * c + y]
+                row = (3 * c + y) * 10
+                grid_ref[n, 0:10, :] = above_ref[row : row + 10, :]
             elif y < 9:
-                tile = field_ref[6 * c + y - 3]
+                grid_ref[n, 0:10, :] = wide_ref[6 * c + y - 3, 0:10, :]
             else:
-                tile = under_ref[c]
-            grid_ref[n, 3:9, :] = tile[0:6]
-            grid_ref[n, 0:3, :] = low_ref[3 * n : 3 * n + 3, :]
-            grid_ref[n, 9:10, :] = high_ref[n : n + 1, :]
+                grid_ref[n, 0:10, :] = under_ref[10 * c : 10 * c + 10, :]
     end = lanes((10, 128)) == 127
     for y in range(10):
         grid_ref[30 + y, 0:10, :] = jnp.where(end, 0.0, pltpu.roll(grid_ref[y, 0:10, :], 127, 1))
@@ -262,27 +279,31 @@
     return total_ref[...] + ionic_ref[...] * field_ref[...]
 
 
-def first_image_kernel(z_ref, above_ref, under_ref, low_ref, high_ref, sigma_ref, matrix_ref, ionic_ref, label_ref,
-                       q_ref, message_ref, *scratch):
-    image = operate(z_ref, above_ref, under_ref, low_ref, high_ref, sigma_ref, matrix_ref, ionic_ref, *scratch)
+def first_image_kernel(wide_ref, z_ref, above_ref, under_ref, sigma_ref, matrix_ref, ionic_ref, diagonal_ref, label_ref,
+                       q_ref, scaled_ref, message_ref, up_ref, down_ref, *scratch):
+    image = operate(wide_ref, z_ref, above_ref, under_ref, sigma_ref, matrix_ref, ionic_ref, *scratch)
     q_ref[...] = image
     message_ref[...] = jnp.broadcast_to(restrict(image, label_ref[...])[None], message_ref.shape)
-
-
-def next_image_kernel(w_ref, above_ref, under_ref, low_ref, high_ref, sigma_ref, matrix_ref, ionic_ref,
-                      r_ref, z_ref, q_ref, t_ref, tile_ref, *scratch):
-    image = operate(w_ref, above_ref, under_ref, low_ref, high_ref, sigma_ref, matrix_ref, ionic_ref, *scratch)
+    scaled_ref[...] = image / diagonal_ref[...]
+    up_ref[...] = jnp.zeros_like(up_ref)
+    down_ref[...] = jnp.zeros_like(down_ref)
+    send_slab(scaled_ref, up_ref, down_ref, 0, 0)
+
+
+def next_image_kernel(wide_ref, w_ref, above_ref, under_ref, sigma_ref, matrix_ref, ionic_ref,
+                      r_ref, z_ref, q_ref, t_ref, message_ref, *scratch):
+    image = operate(wide_ref, w_ref, above_ref, under_ref, sigma_ref, matrix_ref, ionic_ref, *scratch)
     t_ref[...] = image
     r, z, q, w = r_ref[...], z_ref[...], q_ref[...], w_ref[...]
     rows = []
     for left, right in ((r, z), (z, q), (r, w), (q, w), (z, image), (w, image)):
         rows.append(jnp.sum(jnp.sum(left * right, axis=0), axis=0, keepdims=True))
     rows.append(jnp.zeros((2, 128), F32))
-    tile_ref[...] = jnp.concatenate(rows, 0)
+    message_ref[...] = jnp.broadcast_to(jnp.concatenate(rows, 0)[None], message_ref.shape)
 
 
 def finish_kernel(dots_ref, r_ref, z_ref, q_ref, w_ref, t_ref, solution_ref, residual_ref, rows_ref, turned_ref):
-    dots = jnp.sum(jnp.sum(dots_ref[...], axis=0), axis=1, keepdims=True)
+    dots = dots_ref[...]
     rz, zq, rw, qw, zt, wt = [dots[index : index + 1] for index in range(6)]
     alpha = rz / zq
     rz_next = alpha * (alpha * qw - rw)
@@ -321,44 +342,49 @@
     def gather(copies):
         return lax.all_to_all(copies, "slab", 0, 0, tiled=True)
 
-    def add_up(tile):
-        step = 1
-        while step < n_cross:
-            tile = tile + lax.ppermute(tile, "cross", [(source, source ^ step) for source in range(n_cross)])
-            step *= 2
-        return gather(jnp.broadcast_to(tile[None], (n_slab, 8, 128)))
-
-    field, above, under = (18, 8, 128), (9, 8, 128), (3, 8, 128)
+    field, wide = (18, 8, 128), (18, 16, 128)
     space = [(40, 16, 128), (64, 1152), (64, 1152), field]
-    beside = shifted(region_labels[:, 1] + 1, "cross", 1)
-    below = shifted(jnp.concatenate([beside[1:2], region_labels[1] + 1], 0), "slab", 1)
+    regions = region_labels + 1
+    beside = shifted(regions[:, 1], "cross", 1)
+    below = shifted(regions[1], "slab", 1)
+    pairs = [
+        (slab * n_cross + cross, (slab + 1) * n_cross + cross + 1)
+        for slab in range(n_slab - 1)
+        for cross in range(n_cross - 1)
+    ]
+    corner = lax.ppermute(regions[1, 1:2], ("slab", "cross"), pairs)
     r, ionic, labels, coarse = call(
         unpack_kernel, [field] * 3 + [(8, 128)],
         [(128, 384), (384, 128), (6, 6, 384), (6, 6, 384), pltpu.VMEM((6, 6, 384), jnp.int32), pltpu.SemaphoreType.DMA((3,))],
         adjoint_source, potential, restriction_map, away=(0, 1, 2),
     )
-    sigma, diagonal, message = call(
-        diagonal_kernel, [(9, 128), field, (n_slab, 8, 128)], [field],
-        region_labels, beside, below, conductivity, element_matrix, ionic, labels, coarse, smem=(3,),
-    )
-
-    def with_halo(value, up, down):
-        over = shifted(up, "cross", 1)
-        low = shifted(down, "cross", -1)
-        up, down = call(send_slab_kernel, [(96, 128), (32, 128)], [], value, over, low)
-        return (value, over, low, shifted(up, "slab", 1), shifted(down, "slab", -1), sigma, element_matrix, ionic)
-
-    z, up, down, scale = call(
-        first_solve_kernel, [field, above, under, (8, 8, 128)], [], place, gather(message), r, diagonal, labels, smem=(0,)
-    )
-    q, message = call(first_image_kernel, [field, (n_slab, 8, 128)], space, *with_halo(z, up, down), labels)
-    w, up, down = call(
-        next_solve_kernel, [field, above, under], [], place, gather(message), q, diagonal, labels, scale, smem=(0,)
-    )
-    t, tile = call(next_image_kernel, [field, (8, 128)], space, *with_halo(w, up, down), r, z, q)
-    return tuple(
-        call(finish_kernel, [(6, 6, 384)] * 2, [(128, 128), (384, 128)], add_up(tile), r, z, q, w, t)
-    )
+    sigma, diagonal, scaled, message, up, down = call(
+        diagonal_kernel, [(9, 128), field, field, (n_slab, 8, 128), (112, 128), (40, 128)], [field],
+        region_labels, beside, below, corner, conductivity, element_matrix, r, ionic, labels, coarse, smem=(4,),
+    )
+
+    def beyond(up, down, axis):
+        return shifted(up, axis, 1), shifted(down, axis, -1)
+
+    faces = [(96, 128), (32, 128)]
+    wide_z, z, up, down, scale, wide_labels = call(
+        first_solve_kernel, [wide, field, *faces, (10, 8, 128), wide], [],
+        place, gather(message), scaled, labels, *beyond(up, down, "slab"), smem=(0,),
+    )
+    q, scaled, message, up, down = call(
+        first_image_kernel, [field, field, (n_slab, 8, 128), (56, 128), (24, 128)], space,
+        wide_z, z, *beyond(up, down, "cross"), sigma, element_matrix, ionic, diagonal, labels,
+    )
+    wide_w, w, up, down = call(
+        next_solve_kernel, [wide, field, *faces], [],
+        place, gather(message), scaled, wide_labels, *beyond(up, down, "slab"), scale, smem=(0,),
+    )
+    t, message = call(
+        next_image_kernel, [field, (n_slab, 8, 128)], space,
+        wide_w, w, *beyond(up, down, "cross"), sigma, element_matrix, ionic, r, z, q,
+    )
+    dots = lax.psum(jnp.sum(gather(message), (0, 2)), "cross").reshape(8, 1)
+    return tuple(call(finish_kernel, [(6, 6, 384)] * 2, [(128, 128), (384, 128)], dots, r, z, q, w, t))
 
 
 def solution(mesh):

time: 145 us -> 126 us (0.87)
  the two profiles are of different devices: /device:TPU:24 before, /device:TPU:40 now
where the time goes in v1:
time: 126 us; the launch traced here: 125 us
  starting transfers between devices  61.4 us (49%)
  blocking collectives  37.7 us (30%)
  waiting for transfers between devices  14.8 us (12%)
  Pallas kernels  5.9 us (5%)
  local copies, waits for them, and re-layouts  3.42 us (3%)
    ppermute x10, starting transfers between devices, shifted(): return lax.ppermute(value, axis, pairs)  34 us
    all_to_all x2, starting transfers between devices, gather(): return lax.all_to_all(copies, 'slab', 0, 0, tiled=True)  24.6 us
    all_to_all x1, blocking collectives, gather(): return lax.all_to_all(copies, 'slab', 0, 0, tiled=True)  21.1 us
    psum x1, blocking collectives, body(): dots = lax.psum(jnp.sum(gather(message), (0, 2)), 'cross').reshape(8, 1)  16.6 us
    ppermute x10, waiting for transfers between devices, shifted(): return lax.ppermute(value, axis, pairs)  11 us
    pallas_call x7, Pallas kernels, call(): pl.pallas_call(kernel, out_shape=[jax.ShapeDtypeStruct(shape, F32) for sh...  5.9 us
    unnamed x12, local copies, waits for them, and re-layouts  3.32 us
    ppermute x1, starting transfers between devices, body(): corner = lax.ppermute(regions[1, 1:2], ('slab', 'cross'), pairs)  2.8 us
  transfers between devices with their start and end apart: 13, of which 7 were waited for; matrix products, arithmetic and copies ran while one was open for 0% of the time, Pallas kernels for 1%

profile of v1, /device:TPU:40, one launch (start us, length us, event | category | flops | bytes accessed | tf_op | source)
XLA Modules:
  0.0 125.0 jit_solution(8513140262338675573)
XLA Ops:
  0.6 0.7 broadcast_add_fusion
  1.3 1.9 %collective-permute-start = (s32[2,128]{1,0:T(2,128)S(1)}, s32[2,128]{1,0:T(2,128)S(1)}, u32[]{:S(2)}, u32[]{:S(2)}) collective-permute-start(s32[2,128]{1,0:T(2,128)S(1)} %bitcast.8), channel_id=1, source_target_pairs={{0,1},{1,2},{2,3},{3,4},{4,5},{5,6},{6,7},{8,9},{9,10},{10,11},{11... | collective-permute-start | bytes 3080 | tf_op jit(solution)/shard_map/ppermute | solution.py:340
  3.2 5.1 %collective-permute-start.1 = (s32[2,128]{1,0:T(2,128)S(1)}, s32[2,128]{1,0:T(2,128)S(1)}, u32[]{:S(2)}, u32[]{:S(2)}) collective-permute-start(s32[2,128]{1,0:T(2,128)S(1)} %slice_bitcast_fusion), channel_id=1, source_target_pairs={{0,8},{8,16},{16,24},{24,32},{32,40},{40,48},{48,56},{56,64},{64,7... | collective-permute-start | bytes 3080 | tf_op jit(solution)/shard_map/ppermute | solution.py:340
  8.3 0.0 copy-start
  8.3 2.8 %collective-permute-start.2 = (s32[1,128]{1,0:T(1,128)S(1)}, s32[1,128]{1,0:T(1,128)S(1)}, u32[]{:S(2)}, u32[]{:S(2)}) collective-permute-start(s32[1,128]{1,0:T(1,128)S(1)} %slice_bitcast_fusion.1), channel_id=1, source_target_pairs={{0,9},{1,10},{2,11},{3,12},{4,13},{5,14},{6,15},{8,17},{9,18},{10,... | collective-permute-start | bytes 1544 | tf_op jit(solution)/shard_map/ppermute | solution.py:355
  11.2 0.0 copy-start.1
  11.2 0.9 copy-done.1
  12.0 0.0 copy-start.2
  12.0 0.9 copy-done.2
  12.9 0.0 copy-start.3
  12.9 0.9 copy-done.3
  13.8 0.7 shard_map.77
  14.5 1.7 %collective-permute-done.2.corner_ref = s32[1,128]{1,0:T(1,128)S(1)} collective-permute-done((s32[1,128]{1,0:T(1,128)S(1)}, s32[1,128]{1,0:T(1,128)S(1)}, u32[]{:S(2)}, u32[]{:S(2)}) %collective-permute-start.2) | collective-permute-done | bytes 544 | tf_op jit(solution)/shard_map/ppermute | solution.py:355
  16.2 0.0 collective-permute-done.beside_ref
  16.2 0.0 collective-permute-done.1.below_ref
  16.2 0.0 copy-start.4
  16.2 0.0 copy-start.5
  16.2 0.0 copy-done
  16.2 0.7 copy-done.4
  16.9 0.0 copy-done.5
  16.9 1.6 %shard_map.78 = (f32[9,128]{1,0:T(8,128)S(1)}, f32[18,8,128]{2,1,0:T(8,128)S(1)}, f32[18,8,128]{2,1,0:T(8,128)S(1)}, f32[64,8,128]{2,1,0:T(8,128)}, f32[112,128]{1,0:T(8,128)S(1)}, /*index=5*/f32[40,128]{1,0:T(8,128)S(1)}) custom-call(s32[2,2,128]{2,1,0:T(2,128)S(1)} %copy-done.4, s32[2,128]{1,0:T(2,128)S(1)} %collective-permute-done.beside_ref, ...), custom_call_target="tpu_custom_call" | custom-call | tf_op jit(solution)/shard_map/pallas_call | solution.py:32
  18.5 13.9 %all-to-all-start = ((f32[64,8,128]{2,1,0:T(8,128)}), f32[64,8,128]{2,1,0:T(8,128)S(1)}, u32[]{:S(2)}, u32[]{:S(2)}) async-start(f32[64,8,128]{2,1,0:T(8,128)} %get-tuple-element.33), calls=%async_computation | async-start | bytes 524288 | tf_op jit(solution)/shard_map/all_to_all | solution.py:343
  32.4 3.4 %collective-permute-start.3 = (f32[112,128]{1,0:T(8,128)S(1)}, f32[112,128]{1,0:T(8,128)S(1)}, u32[]{:S(2)}, u32[]{:S(2)}) collective-permute-start(f32[112,128]{1,0:T(8,128)S(1)} %get-tuple-element.35), channel_id=1, source_target_pairs={{0,8},{8,16},{16,24},{24,32},{32,40},{40,48},{48,56},{56,64},{64,7... | collective-permute-start | bytes 172040 | tf_op jit(solution)/shard_map/ppermute | solution.py:340
  35.8 2.5 %collective-permute-start.4 = (f32[40,128]{1,0:T(8,128)S(1)}, f32[40,128]{1,0:T(8,128)S(1)}, u32[]{:S(2)}, u32[]{:S(2)}) collective-permute-start(f32[40,128]{1,0:T(8,128)S(1)} %get-tuple-element.36), channel_id=1, source_target_pairs={{8,0},{16,8},{24,16},{32,24},{40,32},{48,40},{56,48},{64,56},{72,6... | collective-permute-start | bytes 61448 | tf_op jit(solution)/shard_map/ppermute | solution.py:340
  38.3 4.1 %collective-permute-done.4.high_ref = f32[40,128]{1,0:T(8,128)S(1)} collective-permute-done((f32[40,128]{1,0:T(8,128)S(1)}, f32[40,128]{1,0:T(8,128)S(1)}, u32[]{:S(2)}, u32[]{:S(2)}) %collective-permute-start.4) | collective-permute-done | bytes 20512 | tf_op jit(solution)/shard_map/ppermute | solution.py:340
  42.4 0.0 collective-permute-done.3.low_ref
  42.4 0.8 all-to-all-done.gathered_ref
  43.2 0.4 shard_map.79
  43.6 1.9 %collective-permute-start.5 = (f32[96,128]{1,0:T(8,128)S(1)}, f32[96,128]{1,0:T(8,128)S(1)}, u32[]{:S(2)}, u32[]{:S(2)}) collective-permute-start(f32[96,128]{1,0:T(8,128)S(1)} %get-tuple-element.39), channel_id=1, source_target_pairs={{0,1},{1,2},{2,3},{3,4},{4,5},{5,6},{6,7},{8,9},{9,10},{10,11},{11... | collective-permute-start | bytes 147464 | tf_op jit(solution)/shard_map/ppermute | solution.py:340
  45.6 5.8 %collective-permute-start.6 = (f32[32,128]{1,0:T(8,128)S(1)}, f32[32,128]{1,0:T(8,128)S(1)}, u32[]{:S(2)}, u32[]{:S(2)}) collective-permute-start(f32[32,128]{1,0:T(8,128)S(1)} %get-tuple-element.40), channel_id=1, source_target_pairs={{1,0},{2,1},{3,2},{4,3},{5,4},{6,5},{7,6},{9,8},{10,9},{11,10},{12... | collective-permute-start | bytes 49160 | tf_op jit(solution)/shard_map/ppermute | solution.py:340
  51.3 1.4 %collective-permute-done.6.under_ref = f32[32,128]{1,0:T(8,128)S(1)} collective-permute-done((f32[32,128]{1,0:T(8,128)S(1)}, f32[32,128]{1,0:T(8,128)S(1)}, u32[]{:S(2)}, u32[]{:S(2)}) %collective-permute-start.6) | collective-permute-done | bytes 16416 | tf_op jit(solution)/shard_map/ppermute | solution.py:340
  52.7 0.0 collective-permute-done.5.above_ref
  52.7 1.3 %shard_map.80 = (f32[18,8,128]{2,1,0:T(8,128)S(1)}, f32[18,8,128]{2,1,0:T(8,128)S(1)}, f32[64,8,128]{2,1,0:T(8,128)}, f32[56,128]{1,0:T(8,128)S(1)}, f32[24,128]{1,0:T(8,128)S(1)}) custom-call(f32[18,16,128]{2,1,0:T(8,128)S(1)} %get-tuple-element.37.wide_ref, f32[18,8,128]{2,1,0:T(8,128)S(1)} %get-tuple-element.38.z_ref, ...), custom_call_target="tpu_custom_call" | custom-call | tf_op jit(solution)/shard_map/pallas_call | solution.py:32
  54.0 10.7 %all-to-all-start.1 = ((f32[64,8,128]{2,1,0:T(8,128)}), f32[64,8,128]{2,1,0:T(8,128)S(1)}, u32[]{:S(2)}, u32[]{:S(2)}) async-start(f32[64,8,128]{2,1,0:T(8,128)} %get-tuple-element.43), calls=%async_computation.1 | async-start | bytes 524288 | tf_op jit(solution)/shard_map/all_to_all | solution.py:343
  64.8 3.4 %collective-permute-start.7 = (f32[56,128]{1,0:T(8,128)S(1)}, f32[56,128]{1,0:T(8,128)S(1)}, u32[]{:S(2)}, u32[]{:S(2)}) collective-permute-start(f32[56,128]{1,0:T(8,128)S(1)} %get-tuple-element.46), channel_id=1, source_target_pairs={{0,8},{8,16},{16,24},{24,32},{32,40},{40,48},{48,56},{56,64},{64,7... | collective-permute-start | bytes 86024 | tf_op jit(solution)/shard_map/ppermute | solution.py:340
  68.2 2.5 %collective-permute-start.8 = (f32[24,128]{1,0:T(8,128)S(1)}, f32[24,128]{1,0:T(8,128)S(1)}, u32[]{:S(2)}, u32[]{:S(2)}) collective-permute-start(f32[24,128]{1,0:T(8,128)S(1)} %get-tuple-element.47), channel_id=1, source_target_pairs={{8,0},{16,8},{24,16},{32,24},{40,32},{48,40},{56,48},{64,56},{72,6... | collective-permute-start | bytes 36872 | tf_op jit(solution)/shard_map/ppermute | solution.py:340
  70.6 4.0 %collective-permute-done.8.high_ref = f32[24,128]{1,0:T(8,128)S(1)} collective-permute-done((f32[24,128]{1,0:T(8,128)S(1)}, f32[24,128]{1,0:T(8,128)S(1)}, u32[]{:S(2)}, u32[]{:S(2)}) %collective-permute-start.8) | collective-permute-done | bytes 12320 | tf_op jit(solution)/shard_map/ppermute | solution.py:340
  74.6 0.0 collective-permute-done.7.low_ref
  74.6 1.4 %all-to-all-done.1.gathered_ref = f32[64,8,128]{2,1,0:T(8,128)S(1)} async-done(((f32[64,8,128]{2,1,0:T(8,128)}), f32[64,8,128]{2,1,0:T(8,128)S(1)}, u32[]{:S(2)}, u32[]{:S(2)}) %all-to-all-start.1) | async-done | bytes 262176 | tf_op jit(solution)/shard_map/all_to_all | solution.py:343
  76.0 0.3 shard_map.81
  76.4 1.9 %collective-permute-start.9 = (f32[96,128]{1,0:T(8,128)S(1)}, f32[96,128]{1,0:T(8,128)S(1)}, u32[]{:S(2)}, u32[]{:S(2)}) collective-permute-start(f32[96,128]{1,0:T(8,128)S(1)} %get-tuple-element.51), channel_id=1, source_target_pairs={{0,1},{1,2},{2,3},{3,4},{4,5},{5,6},{6,7},{8,9},{9,10},{10,11},{11... | collective-permute-start | bytes 147464 | tf_op jit(solution)/shard_map/ppermute | solution.py:340
  78.3 5.8 %collective-permute-start.10 = (f32[32,128]{1,0:T(8,128)S(1)}, f32[32,128]{1,0:T(8,128)S(1)}, u32[]{:S(2)}, u32[]{:S(2)}) collective-permute-start(f32[32,128]{1,0:T(8,128)S(1)} %get-tuple-element.52), channel_id=1, source_target_pairs={{1,0},{2,1},{3,2},{4,3},{5,4},{6,5},{7,6},{9,8},{10,9},{11,10},{12... | collective-permute-start | bytes 49160 | tf_op jit(solution)/shard_map/ppermute | solution.py:340
  84.1 1.4 %collective-permute-done.10.under_ref = f32[32,128]{1,0:T(8,128)S(1)} collective-permute-done((f32[32,128]{1,0:T(8,128)S(1)}, f32[32,128]{1,0:T(8,128)S(1)}, u32[]{:S(2)}, u32[]{:S(2)}) %collective-permute-start.10) | collective-permute-done | bytes 16416 | tf_op jit(solution)/shard_map/ppermute | solution.py:340
  85.5 0.0 collective-permute-done.9.above_ref
  85.5 0.5 shard_map.82
  86.0 21.1 %all_to_all.15 = f32[64,8,128]{2,1,0:T(8,128)S(1)} all-to-all(f32[64,8,128]{2,1,0:T(8,128)S(1)} %get-tuple-element.54), channel_id=1, replica_groups=mesh['slab'=64,'cross'=8] {'slab'}, dimensions={0} | all-to-all | bytes 524288 | tf_op jit(solution)/shard_map/all_to_all | solution.py:343
  107.1 0.2 reduce_sum.9
  107.3 0.1 copy.8
  107.4 16.6 %psum.7.dots_ref = f32[8,1]{1,0:T(8,128)S(1)} all-reduce(f32[8,1]{1,0:T(8,128)S(1)} %copy.8), channel_id=1, replica_groups=mesh['slab'=64,'cross'=8] {'cross'}, use_global_device_ids=true, to_apply=%region_1.0 | all-reduce | flops 8 | bytes 64 | tf_op jit(solution)/shard_map/psum | solution.py:386
  124.0 1.0 shard_map.83
  (3 shorter events, 0.0 us)
Async XLA Ops:
  1.3 14.9 %collective-permute-start = (s32[2,128]{1,0:T(2,128)S(1)}, s32[2,128]{1,0:T(2,128)S(1)}, u32[]{:S(2)}, u32[]{:S(2)}) collective-permute-start(s32[2,128]{1,0:T(2,128)S(1)} %bitcast.8), channel_id=1, source_target_pairs={{0,1},{1,2},{2,3},{3,4},{4,5},{5,6},{6,7},{8,9},{9,10},{10,11},{11... | collective-permute-start | bytes 3080 | tf_op jit(solution)/shard_map/ppermute | solution.py:340
  3.2 13.0 %collective-permute-start.1 = (s32[2,128]{1,0:T(2,128)S(1)}, s32[2,128]{1,0:T(2,128)S(1)}, u32[]{:S(2)}, u32[]{:S(2)}) collective-permute-start(s32[2,128]{1,0:T(2,128)S(1)} %slice_bitcast_fusion), channel_id=1, source_target_pairs={{0,8},{8,16},{16,24},{24,32},{32,40},{40,48},{48,56},{56,64},{64,7... | collective-permute-start | bytes 3080 | tf_op jit(solution)/shard_map/ppermute | solution.py:340
  8.3 7.9 %copy-start = (f32[64,64]{1,0:T(8,128)S(1)}, f32[64,64]{1,0:T(8,128)}, u32[]{:S(2)}) copy-start(f32[64,64]{1,0:T(8,128)} %matrix_ref.5) | copy-start | bytes 49156
  8.3 7.9 %collective-permute-start.2 = (s32[1,128]{1,0:T(1,128)S(1)}, s32[1,128]{1,0:T(1,128)S(1)}, u32[]{:S(2)}, u32[]{:S(2)}) collective-permute-start(s32[1,128]{1,0:T(1,128)S(1)} %slice_bitcast_fusion.1), channel_id=1, source_target_pairs={{0,9},{1,10},{2,11},{3,12},{4,13},{5,14},{6,15},{8,17},{9,18},{10,... | collective-permute-start | bytes 1544 | tf_op jit(solution)/shard_map/ppermute | solution.py:355
  11.2 0.9 copy-start.1
  12.0 0.9 copy-start.2
  12.9 0.9 copy-start.3
  16.2 0.7 copy-start.4
  16.2 0.7 copy-start.5
  18.5 24.7 %all-to-all-start = ((f32[64,8,128]{2,1,0:T(8,128)}), f32[64,8,128]{2,1,0:T(8,128)S(1)}, u32[]{:S(2)}, u32[]{:S(2)}) async-start(f32[64,8,128]{2,1,0:T(8,128)} %get-tuple-element.33), calls=%async_computation | async-start | bytes 524288 | tf_op jit(solution)/shard_map/all_to_all | solution.py:343
  32.4 10.0 %collective-permute-start.3 = (f32[112,128]{1,0:T(8,128)S(1)}, f32[112,128]{1,0:T(8,128)S(1)}, u32[]{:S(2)}, u32[]{:S(2)}) collective-permute-start(f32[112,128]{1,0:T(8,128)S(1)} %get-tuple-element.35), channel_id=1, source_target_pairs={{0,8},{8,16},{16,24},{24,32},{32,40},{40,48},{48,56},{56,64},{64,7... | collective-permute-start | bytes 172040 | tf_op jit(solution)/shard_map/ppermute | solution.py:340
  35.8 6.6 %collective-permute-start.4 = (f32[40,128]{1,0:T(8,128)S(1)}, f32[40,128]{1,0:T(8,128)S(1)}, u32[]{:S(2)}, u32[]{:S(2)}) collective-permute-start(f32[40,128]{1,0:T(8,128)S(1)} %get-tuple-element.36), channel_id=1, source_target_pairs={{8,0},{16,8},{24,16},{32,24},{40,32},{48,40},{56,48},{64,56},{72,6... | collective-permute-start | bytes 61448 | tf_op jit(solution)/shard_map/ppermute | solution.py:340
  43.6 9.1 %collective-permute-start.5 = (f32[96,128]{1,0:T(8,128)S(1)}, f32[96,128]{1,0:T(8,128)S(1)}, u32[]{:S(2)}, u32[]{:S(2)}) collective-permute-start(f32[96,128]{1,0:T(8,128)S(1)} %get-tuple-element.39), channel_id=1, source_target_pairs={{0,1},{1,2},{2,3},{3,4},{4,5},{5,6},{6,7},{8,9},{9,10},{10,11},{11... | collective-permute-start | bytes 147464 | tf_op jit(solution)/shard_map/ppermute | solution.py:340
  45.6 7.2 %collective-permute-start.6 = (f32[32,128]{1,0:T(8,128)S(1)}, f32[32,128]{1,0:T(8,128)S(1)}, u32[]{:S(2)}, u32[]{:S(2)}) collective-permute-start(f32[32,128]{1,0:T(8,128)S(1)} %get-tuple-element.40), channel_id=1, source_target_pairs={{1,0},{2,1},{3,2},{4,3},{5,4},{6,5},{7,6},{9,8},{10,9},{11,10},{12... | collective-permute-start | bytes 49160 | tf_op jit(solution)/shard_map/ppermute | solution.py:340
  54.0 22.0 %all-to-all-start.1 = ((f32[64,8,128]{2,1,0:T(8,128)}), f32[64,8,128]{2,1,0:T(8,128)S(1)}, u32[]{:S(2)}, u32[]{:S(2)}) async-start(f32[64,8,128]{2,1,0:T(8,128)} %get-tuple-element.43), calls=%async_computation.1 | async-start | bytes 524288 | tf_op jit(solution)/shard_map/all_to_all | solution.py:343
  64.8 9.9 %collective-permute-start.7 = (f32[56,128]{1,0:T(8,128)S(1)}, f32[56,128]{1,0:T(8,128)S(1)}, u32[]{:S(2)}, u32[]{:S(2)}) collective-permute-start(f32[56,128]{1,0:T(8,128)S(1)} %get-tuple-element.46), channel_id=1, source_target_pairs={{0,8},{8,16},{16,24},{24,32},{32,40},{40,48},{48,56},{56,64},{64,7... | collective-permute-start | bytes 86024 | tf_op jit(solution)/shard_map/ppermute | solution.py:340
  68.2 6.5 %collective-permute-start.8 = (f32[24,128]{1,0:T(8,128)S(1)}, f32[24,128]{1,0:T(8,128)S(1)}, u32[]{:S(2)}, u32[]{:S(2)}) collective-permute-start(f32[24,128]{1,0:T(8,128)S(1)} %get-tuple-element.47), channel_id=1, source_target_pairs={{8,0},{16,8},{24,16},{32,24},{40,32},{48,40},{56,48},{64,56},{72,6... | collective-permute-start | bytes 36872 | tf_op jit(solution)/shard_map/ppermute | solution.py:340
  76.4 9.1 %collective-permute-start.9 = (f32[96,128]{1,0:T(8,128)S(1)}, f32[96,128]{1,0:T(8,128)S(1)}, u32[]{:S(2)}, u32[]{:S(2)}) collective-permute-start(f32[96,128]{1,0:T(8,128)S(1)} %get-tuple-element.51), channel_id=1, source_target_pairs={{0,1},{1,2},{2,3},{3,4},{4,5},{5,6},{6,7},{8,9},{9,10},{10,11},{11... | collective-permute-start | bytes 147464 | tf_op jit(solution)/shard_map/ppermute | solution.py:340
  78.3 7.2 %collective-permute-start.10 = (f32[32,128]{1,0:T(8,128)S(1)}, f32[32,128]{1,0:T(8,128)S(1)}, u32[]{:S(2)}, u32[]{:S(2)}) collective-permute-start(f32[32,128]{1,0:T(8,128)S(1)} %get-tuple-element.52), channel_id=1, source_target_pairs={{1,0},{2,1},{3,2},{4,3},{5,4},{6,5},{7,6},{9,8},{10,9},{11,10},{12... | collective-permute-start | bytes 49160 | tf_op jit(solution)/shard_map/ppermute | solution.py:340

commit v2 on v1

--- a/solution.py
+++ b/solution.py
@@ -28,6 +28,10 @@
     specs = [
         pl.BlockSpec(memory_space=pltpu.SMEM if index in smem else pltpu.HBM if index in away else pltpu.VMEM)
         for index in range(len(operands))
+    ]
+    operands = [
+        pltpu.with_memory_space_constraint(operand, pltpu.HBM) if index in away else operand
+        for index, operand in enumerate(operands)
     ]
     return pl.pallas_call(
         kernel,
@@ -81,12 +85,19 @@
                         total_ref[c * 6 + y, x : x + high_a - low_a, :] += rows
 
 
-def unpack_kernel(source_hbm, potential_hbm, map_hbm, r_ref, ionic_ref, label_ref, coarse_ref,
-                  rows_ref, turned_ref, source_ref, potential_ref, map_ref, sems):
+def unpack_kernel(source_hbm, potential_hbm, map_hbm, region_hbm, table_hbm, r_ref, ionic_ref, label_ref, coarse_ref,
+                  own_ref, beside_ref, below_ref, corner_ref,
+                  rows_ref, turned_ref, source_ref, potential_ref, map_ref, region_ref, table_ref, sems):
     copies = [
         pltpu.make_async_copy(away, here, sems.at[index])
         for index, (away, here) in enumerate(
-            ((source_hbm, source_ref), (potential_hbm, potential_ref), (map_hbm, map_ref))
+            (
+                (source_hbm, source_ref),
+                (potential_hbm, potential_ref),
+                (map_hbm, map_ref),
+                (region_hbm, region_ref),
+                (table_hbm, table_ref),
+            )
         )
     ]
     for copy in copies:
@@ -94,6 +105,16 @@
     rows_ref[...] = jnp.zeros_like(rows_ref)
     for copy in copies:
         copy.wait()
+    for i in range(2):
+        region = region_ref[i]
+        sigma = jnp.zeros(region.shape, F32)
+        for index in range(4):
+            sigma = jnp.where(region == index, table_ref[index], sigma)
+        own_ref[2 * i : 2 * i + 2, :] = sigma
+    beside_ref[0:1, :] = own_ref[1:2, :]
+    beside_ref[1:2, :] = own_ref[3:4, :]
+    below_ref[...] = own_ref[2:4, :]
+    corner_ref[...] = own_ref[3:4, :]
     for y in range(6):
         for x in range(6):
             row = y * 6 + x
@@ -121,19 +142,13 @@
         down_ref[down_start + n : down_start + n + 1, :] = field_ref[n, 0:1, :]
 
 
-def diagonal_kernel(own_ref, beside_ref, below_ref, corner_ref, table_ref, matrix_ref, r_ref, ionic_ref, label_ref,
+def diagonal_kernel(own_ref, beside_ref, below_ref, corner_ref, matrix_ref, r_ref, ionic_ref, label_ref,
                     coarse_ref, sigma_ref, diagonal_ref, scaled_ref, message_ref, up_ref, down_ref, total_ref):
-    def conductance(region):
-        value = jnp.zeros(region.shape, F32)
-        for index in range(4):
-            value = jnp.where(region == index + 1, table_ref[index], value)
-        return value
-
-    sigma_ref[0:1, :] = conductance(corner_ref[...])
-    sigma_ref[1:3, :] = conductance(below_ref[...])
+    sigma_ref[0:1, :] = corner_ref[...]
+    sigma_ref[1:3, :] = below_ref[...]
     for i in range(2):
-        sigma_ref[3 + 3 * i : 4 + 3 * i, :] = conductance(beside_ref[i : i + 1, :])
-        sigma_ref[4 + 3 * i : 6 + 3 * i, :] = conductance(own_ref[i] + 1)
+        sigma_ref[3 + 3 * i : 4 + 3 * i, :] = beside_ref[i : i + 1, :]
+        sigma_ref[4 + 3 * i : 6 + 3 * i, :] = own_ref[2 * i : 2 * i + 2, :]
     square = (64, 64)
     eye = lax.broadcasted_iota(jnp.int32, square, 0) == lax.broadcasted_iota(jnp.int32, square, 1)
     corner = jnp.sum(jnp.where(eye, matrix_ref[...], 0.0), axis=1, keepdims=True)
@@ -201,61 +216,81 @@
         wide_ref[n, 9:10, :] = high_ref[high_start + n : high_start + n + 1, :]
 
 
-def send_cross(wide_ref, own_ref, up_ref, down_ref):
+def send_cross(even, wide_ref, own_ref, near_ref, far_ref):
     own_ref[...] = jnp.zeros_like(own_ref)
     for n in range(18):
         own_ref[n, 0:6, :] = wide_ref[n, 3:9, :]
-    up_ref[90:96, :] = jnp.zeros((6, 128), F32)
-    down_ref[30:32, :] = jnp.zeros((2, 128), F32)
-    for c in range(3):
-        for y in range(3):
-            row = (3 * c + y) * 10
-            up_ref[row : row + 10, :] = wide_ref[6 * c + 3 + y, 0:10, :]
-        down_ref[10 * c : 10 * c + 10, :] = wide_ref[6 * c, 0:10, :]
+    near_ref[...] = jnp.zeros_like(near_ref)
+    far_ref[...] = jnp.zeros_like(far_ref)
+
+    def fill(up_ref, down_ref):
+        for c in range(3):
+            for y in range(3):
+                row = (3 * c + y) * 10
+                up_ref[row : row + 10, :] = wide_ref[6 * c + 3 + y, 0:10, :]
+            down_ref[10 * c : 10 * c + 10, :] = wide_ref[6 * c, 0:10, :]
+
+    @pl.when(even)
+    def _():
+        fill(near_ref, far_ref)
+
+    @pl.when(jnp.logical_not(even))
+    def _():
+        fill(far_ref, near_ref)
 
 
 def first_solve_kernel(place_ref, gathered_ref, scaled_ref, label_ref, low_ref, high_ref,
-                       wide_ref, z_ref, up_ref, down_ref, scale_ref, wide_label_ref):
+                       wide_ref, z_ref, near_ref, far_ref, scale_ref, wide_label_ref):
     rows, valid = around(place_ref, gathered_ref.shape[0])
-    near = jnp.concatenate([gathered_ref[pl.ds(row, 1)] for row in rows], 0)
+    tiles = jnp.concatenate([gathered_ref[pl.ds(row, 1)] for row in rows], 0)
     sums = jnp.sum(gathered_ref[...], axis=0)
-    inverse = valid / jnp.sqrt(odd_part(near))
+    inverse = valid / jnp.sqrt(odd_part(tiles))
     share = 1.0 / odd_part(sums)
     scale_ref[0 : 2 * NEAR + 1] = inverse
     scale_ref[2 * NEAR + 1] = share
-    level = smooth(DAMPING * even_part(near) * inverse, valid)
+    level = smooth(DAMPING * even_part(tiles) * inverse, valid)
     coarse = level * inverse[REACH : REACH + 3] + (even_part(sums) * share)[None]
     widen(label_ref, low_ref, high_ref, 56, 20, wide_label_ref)
     widen(scaled_ref, low_ref, high_ref, 0, 0, wide_ref)
     wide_ref[...] += prolong(coarse, wide_label_ref[...])
-    send_cross(wide_ref, z_ref, up_ref, down_ref)
+    send_cross(place_ref[1] == 0, wide_ref, z_ref, near_ref, far_ref)
 
 
 def next_solve_kernel(place_ref, gathered_ref, scaled_ref, wide_label_ref, low_ref, high_ref, scale_ref,
-                      wide_ref, w_ref, up_ref, down_ref):
+                      wide_ref, w_ref, near_ref, far_ref):
     rows, valid = around(place_ref, gathered_ref.shape[0])
-    near = jnp.concatenate([gathered_ref[pl.ds(row, 1)] for row in rows], 0)
+    tiles = jnp.concatenate([gathered_ref[pl.ds(row, 1)] for row in rows], 0)
     sums = jnp.sum(gathered_ref[...], axis=0)
     inverse = scale_ref[0 : 2 * NEAR + 1]
-    level = smooth(DAMPING * near * inverse, valid)
+    level = smooth(DAMPING * tiles * inverse, valid)
     coarse = level * inverse[REACH : REACH + 3] + (sums * scale_ref[2 * NEAR + 1])[None]
     widen(scaled_ref, low_ref, high_ref, 0, 0, wide_ref)
     wide_ref[...] += prolong(coarse, wide_label_ref[...])
-    send_cross(wide_ref, w_ref, up_ref, down_ref)
-
-
-def operate(wide_ref, field_ref, above_ref, under_ref, sigma_ref, matrix_ref, ionic_ref,
+    send_cross(place_ref[1] == 0, wide_ref, w_ref, near_ref, far_ref)
+
+
+def operate(place_ref, wide_ref, field_ref, near_ref, far_ref, sigma_ref, matrix_ref, ionic_ref,
             grid_ref, local_ref, product_ref, total_ref):
-    for c in range(3):
-        for y in range(10):
-            n = c * 10 + y
-            if y < 3:
+    for n in range(18):
+        grid_ref[n // 6 * 10 + 3 + n % 6, 0:10, :] = wide_ref[n, 0:10, :]
+
+    def fill(above_ref, under_ref):
+        for c in range(3):
+            for y in range(3):
                 row = (3 * c + y) * 10
-                grid_ref[n, 0:10, :] = above_ref[row : row + 10, :]
-            elif y < 9:
-                grid_ref[n, 0:10, :] = wide_ref[6 * c + y - 3, 0:10, :]
-            else:
-                grid_ref[n, 0:10, :] = under_ref[10 * c : 10 * c + 10, :]
+                grid_ref[10 * c + y, 0:10, :] = above_ref[row : row + 10, :]
+            grid_ref[10 * c + 9, 0:10, :] = under_ref[10 * c : 10 * c + 10, :]
+
+    even = place_ref[1] == 0
+
+    @pl.when(even)
+    def _():
+        fill(far_ref, near_ref)
+
+    @pl.when(jnp.logical_not(even))
+    def _():
+        fill(near_ref, far_ref)
+
     end = lanes((10, 128)) == 127
     for y in range(10):
         grid_ref[30 + y, 0:10, :] = jnp.where(end, 0.0, pltpu.roll(grid_ref[y, 0:10, :], 127, 1))
@@ -279,9 +314,9 @@
     return total_ref[...] + ionic_ref[...] * field_ref[...]
 
 
-def first_image_kernel(wide_ref, z_ref, above_ref, under_ref, sigma_ref, matrix_ref, ionic_ref, diagonal_ref, label_ref,
+def first_image_kernel(place_ref, wide_ref, z_ref, near_ref, far_ref, sigma_ref, matrix_ref, ionic_ref, diagonal_ref, label_ref,
                        q_ref, scaled_ref, message_ref, up_ref, down_ref, *scratch):
-    image = operate(wide_ref, z_ref, above_ref, under_ref, sigma_ref, matrix_ref, ionic_ref, *scratch)
+    image = operate(place_ref, wide_ref, z_ref, near_ref, far_ref, sigma_ref, matrix_ref, ionic_ref, *scratch)
     q_ref[...] = image
     message_ref[...] = jnp.broadcast_to(restrict(image, label_ref[...])[None], message_ref.shape)
     scaled_ref[...] = image / diagonal_ref[...]
@@ -290,21 +325,21 @@
     send_slab(scaled_ref, up_ref, down_ref, 0, 0)
 
 
-def next_image_kernel(wide_ref, w_ref, above_ref, under_ref, sigma_ref, matrix_ref, ionic_ref,
+def next_image_kernel(place_ref, wide_ref, w_ref, near_ref, far_ref, sigma_ref, matrix_ref, ionic_ref,
                       r_ref, z_ref, q_ref, t_ref, message_ref, *scratch):
-    image = operate(wide_ref, w_ref, above_ref, under_ref, sigma_ref, matrix_ref, ionic_ref, *scratch)
+    image = operate(place_ref, wide_ref, w_ref, near_ref, far_ref, sigma_ref, matrix_ref, ionic_ref, *scratch)
     t_ref[...] = image
     r, z, q, w = r_ref[...], z_ref[...], q_ref[...], w_ref[...]
-    rows = []
-    for left, right in ((r, z), (z, q), (r, w), (q, w), (z, image), (w, image)):
-        rows.append(jnp.sum(jnp.sum(left * right, axis=0), axis=0, keepdims=True))
-    rows.append(jnp.zeros((2, 128), F32))
-    message_ref[...] = jnp.broadcast_to(jnp.concatenate(rows, 0)[None], message_ref.shape)
+    row = jnp.zeros((1, 128), F32)
+    for index, (left, right) in enumerate(((r, z), (z, q), (r, w), (q, w), (z, image), (w, image))):
+        part = jnp.sum(jnp.sum(left * right, axis=0), axis=0, keepdims=True)
+        row = jnp.where(lanes((1, 128)) == index, jnp.sum(part, axis=1, keepdims=True), row)
+    message_ref[...] = jnp.broadcast_to(row[None], message_ref.shape)
 
 
 def finish_kernel(dots_ref, r_ref, z_ref, q_ref, w_ref, t_ref, solution_ref, residual_ref, rows_ref, turned_ref):
-    dots = dots_ref[...]
-    rz, zq, rw, qw, zt, wt = [dots[index : index + 1] for index in range(6)]
+    dots = jnp.sum(dots_ref[...], axis=0)
+    rz, zq, rw, qw, zt, wt = [dots[:, index : index + 1] for index in range(6)]
     alpha = rz / zq
     rz_next = alpha * (alpha * qw - rw)
     beta = rz_next / rz
@@ -333,7 +368,13 @@
 def body(adjoint_source, potential, element_matrix, region_labels, conductivity, restriction_map):
     n_slab = lax.axis_size("slab")
     n_cross = lax.axis_size("cross")
-    place = lax.axis_index("slab").astype(jnp.int32).reshape(1)
+    slab, cross = lax.axis_index("slab"), lax.axis_index("cross")
+    place = jnp.stack([slab, cross % 2]).astype(jnp.int32)
+    columns = [
+        [slab * n_cross + cross for slab in (2 * pair, 2 * pair + 1) for cross in range(n_cross)]
+        for pair in range(n_slab // 2)
+    ]
+    planes = [[2 * pair + low for pair in range(n_slab // 2)] for low in range(2)]
     def shifted(value, axis, step):
         count = lax.axis_size(axis)
         pairs = [(source, source + step) for source in range(count) if 0 <= source + step < count]
@@ -344,46 +385,52 @@
 
     field, wide = (18, 8, 128), (18, 16, 128)
     space = [(40, 16, 128), (64, 1152), (64, 1152), field]
-    regions = region_labels + 1
-    beside = shifted(regions[:, 1], "cross", 1)
-    below = shifted(regions[1], "slab", 1)
     pairs = [
         (slab * n_cross + cross, (slab + 1) * n_cross + cross + 1)
         for slab in range(n_slab - 1)
         for cross in range(n_cross - 1)
     ]
-    corner = lax.ppermute(regions[1, 1:2], ("slab", "cross"), pairs)
-    r, ionic, labels, coarse = call(
-        unpack_kernel, [field] * 3 + [(8, 128)],
-        [(128, 384), (384, 128), (6, 6, 384), (6, 6, 384), pltpu.VMEM((6, 6, 384), jnp.int32), pltpu.SemaphoreType.DMA((3,))],
-        adjoint_source, potential, restriction_map, away=(0, 1, 2),
+    r, ionic, labels, coarse, own, beside, below, corner = call(
+        unpack_kernel, [field] * 3 + [(8, 128), (4, 128), (2, 128), (2, 128), (1, 128)],
+        [(128, 384), (384, 128), (6, 6, 384), (6, 6, 384), pltpu.VMEM((6, 6, 384), jnp.int32),
+         pltpu.VMEM((2, 2, 128), jnp.int32), pltpu.SMEM((4,), F32), pltpu.SemaphoreType.DMA((5,))],
+        adjoint_source, potential, restriction_map, region_labels, conductivity, away=(0, 1, 2, 3, 4),
     )
     sigma, diagonal, scaled, message, up, down = call(
         diagonal_kernel, [(9, 128), field, field, (n_slab, 8, 128), (112, 128), (40, 128)], [field],
-        region_labels, beside, below, corner, conductivity, element_matrix, r, ionic, labels, coarse, smem=(4,),
-    )
-
-    def beyond(up, down, axis):
-        return shifted(up, axis, 1), shifted(down, axis, -1)
-
-    faces = [(96, 128), (32, 128)]
-    wide_z, z, up, down, scale, wide_labels = call(
+        own, shifted(beside, "cross", 1), shifted(below, "slab", 1), lax.ppermute(corner, ("slab", "cross"), pairs),
+        element_matrix, r, ionic, labels, coarse,
+    )
+
+    def beyond(up, down):
+        return shifted(up, "slab", 1), shifted(down, "slab", -1)
+
+    def across(near, far):
+        far_pairs = [(c, c + 1) for c in range(1, n_cross - 1, 2)]
+        far_pairs += [(above, c) for c, above in far_pairs]
+        far = lax.ppermute(far, "cross", far_pairs)
+        return lax.ppermute(near, "cross", [(c, c ^ 1) for c in range(n_cross)]), far
+
+    faces = [(96, 128), (96, 128)]
+    wide_z, z, near, far, scale, wide_labels = call(
         first_solve_kernel, [wide, field, *faces, (10, 8, 128), wide], [],
-        place, gather(message), scaled, labels, *beyond(up, down, "slab"), smem=(0,),
+        place, gather(message), scaled, labels, *beyond(up, down), smem=(0,),
     )
     q, scaled, message, up, down = call(
         first_image_kernel, [field, field, (n_slab, 8, 128), (56, 128), (24, 128)], space,
-        wide_z, z, *beyond(up, down, "cross"), sigma, element_matrix, ionic, diagonal, labels,
-    )
-    wide_w, w, up, down = call(
+        place, wide_z, z, *across(near, far), sigma, element_matrix, ionic, diagonal, labels, smem=(0,),
+    )
+    wide_w, w, near, far = call(
         next_solve_kernel, [wide, field, *faces], [],
-        place, gather(message), scaled, wide_labels, *beyond(up, down, "slab"), scale, smem=(0,),
+        place, gather(message), scaled, wide_labels, *beyond(up, down), scale, smem=(0,),
     )
     t, message = call(
-        next_image_kernel, [field, (n_slab, 8, 128)], space,
-        wide_w, w, *beyond(up, down, "cross"), sigma, element_matrix, ionic, r, z, q,
-    )
-    dots = lax.psum(jnp.sum(gather(message), (0, 2)), "cross").reshape(8, 1)
+        next_image_kernel, [field, (n_slab // 2, 1, 128)], space,
+        place, wide_w, w, *across(near, far), sigma, element_matrix, ionic, r, z, q, smem=(0,),
+    )
+    parts = lax.all_to_all(message, "slab", 0, 0, axis_index_groups=planes, tiled=True)
+    parts = jnp.broadcast_to(jnp.sum(parts, 0)[None], (2 * n_cross, 1, 128))
+    dots = lax.all_to_all(parts, ("slab", "cross"), 0, 0, axis_index_groups=columns, tiled=True)
     return tuple(call(finish_kernel, [(6, 6, 384)] * 2, [(128, 128), (384, 128)], dots, r, z, q, w, t))
 
 

time: 126 us -> 123 us (0.976)
  the two profiles are of different devices: /device:TPU:40 before, /device:TPU:1 now
where the time goes in v2:
time: 123 us
  starting transfers between devices  64.4 us (52%)
  blocking collectives  31.9 us (26%)
  waiting for transfers between devices  17.1 us (14%)
  Pallas kernels  8.48 us (7%)
    all_to_all x2, starting transfers between devices, gather(): return lax.all_to_all(copies, 'slab', 0, 0, tiled=True)  24.1 us
    all_to_all x1, blocking collectives, body(): lax.all_to_all(parts, ('slab', 'cross'), 0, 0, axis_index_groups=columns,...  19 us
    ppermute x6, starting transfers between devices, shifted(): return lax.ppermute(value, axis, pairs)  18.3 us
    ppermute x2, starting transfers between devices, across(): far = lax.ppermute(far, 'cross', far_pairs)  14.3 us
    all_to_all x1, blocking collectives, body(): lax.all_to_all(message, 'slab', 0, 0, axis_index_groups=planes, tiled=True)  12.9 us
    pallas_call x7, Pallas kernels, call(): pl.pallas_call(kernel, out_shape=[jax.ShapeDtypeStruct(shape, F32) for sh...  8.48 us
    all_to_all x2, waiting for transfers between devices, gather(): return lax.all_to_all(copies, 'slab', 0, 0, tiled=True)  7.68 us
    ppermute x6, waiting for transfers between devices, shifted(): return lax.ppermute(value, axis, pairs)  4.53 us
  transfers between devices with their start and end apart: 13, of which 7 were waited for; matrix products, arithmetic and copies ran while one was open for 0% of the time, Pallas kernels for 0%

profile of v2, /device:TPU:1, one launch (start us, length us, event | category | flops | bytes accessed | tf_op | source)
XLA Modules:
  0.0 122.8 jit_solution(2298206251706816699)
XLA Ops:
  0.6 0.0 copy-start
  0.6 1.4 %shard_map.77 = (f32[18,8,128]{2,1,0:T(8,128)S(1)}, f32[18,8,128]{2,1,0:T(8,128)S(1)}, f32[18,8,128]{2,1,0:T(8,128)S(1)}, f32[8,128]{1,0:T(8,128)S(1)}, f32[4,12...) custom-call(f32[6,6,384]{2,1,0:T(8,128)} %source_hbm.1, ...), custom_call_target="tpu_custom_call" | custom-call | tf_op jit(solution)/shard_map/pallas_call | solution.py:36
  2.1 5.6 %collective-permute-start = (f32[2,128]{1,0:T(2,128)S(1)}, f32[2,128]{1,0:T(2,128)S(1)}, u32[]{:S(2)}, u32[]{:S(2)}) collective-permute-start(f32[2,128]{1,0:T(2,128)S(1)} %get-tuple-element.34), channel_id=1, source_target_pairs={{0,1},{1,2},{2,3},{3,4},{4,5},{5,6},{6,7},{8,9},{9,10},{10,11},{11... | collective-permute-start | bytes 3080 | tf_op jit(solution)/shard_map/ppermute | solution.py:381
  7.7 3.2 %collective-permute-start.1 = (f32[2,128]{1,0:T(2,128)S(1)}, f32[2,128]{1,0:T(2,128)S(1)}, u32[]{:S(2)}, u32[]{:S(2)}) collective-permute-start(f32[2,128]{1,0:T(2,128)S(1)} %get-tuple-element.35), channel_id=1, source_target_pairs={{0,8},{8,16},{16,24},{24,32},{32,40},{40,48},{48,56},{56,64},{64,7... | collective-permute-start | bytes 3080 | tf_op jit(solution)/shard_map/ppermute | solution.py:381
  10.9 3.9 %collective-permute-start.2 = (f32[1,128]{1,0:T(1,128)S(1)}, f32[1,128]{1,0:T(1,128)S(1)}, u32[]{:S(2)}, u32[]{:S(2)}) collective-permute-start(f32[1,128]{1,0:T(1,128)S(1)} %get-tuple-element.36), channel_id=1, source_target_pairs={{0,9},{1,10},{2,11},{3,12},{4,13},{5,14},{6,15},{8,17},{9,18},{10,... | collective-permute-start | bytes 1544 | tf_op jit(solution)/shard_map/ppermute | solution.py:401
  14.8 0.7 collective-permute-done.2.corner_ref
  15.5 0.0 collective-permute-done.beside_ref
  15.5 0.0 collective-permute-done.1.below_ref
  15.5 0.0 copy-done
  15.5 1.1 shard_map.78
  16.6 15.8 %all-to-all-start = ((f32[64,8,128]{2,1,0:T(8,128)}), f32[64,8,128]{2,1,0:T(8,128)S(1)}, u32[]{:S(2)}, u32[]{:S(2)}) async-start(f32[64,8,128]{2,1,0:T(8,128)} %get-tuple-element.41), calls=%async_computation | async-start | bytes 524288 | tf_op jit(solution)/shard_map/all_to_all | solution.py:384
  32.5 1.3 %collective-permute-start.4 = (f32[40,128]{1,0:T(8,128)S(1)}, f32[40,128]{1,0:T(8,128)S(1)}, u32[]{:S(2)}, u32[]{:S(2)}) collective-permute-start(f32[40,128]{1,0:T(8,128)S(1)} %get-tuple-element.44), channel_id=1, source_target_pairs={{8,0},{16,8},{24,16},{32,24},{40,32},{48,40},{56,48},{64,56},{72,6... | collective-permute-start | bytes 61448 | tf_op jit(solution)/shard_map/ppermute | solution.py:381
  33.8 4.0 %collective-permute-start.3 = (f32[112,128]{1,0:T(8,128)S(1)}, f32[112,128]{1,0:T(8,128)S(1)}, u32[]{:S(2)}, u32[]{:S(2)}) collective-permute-start(f32[112,128]{1,0:T(8,128)S(1)} %get-tuple-element.43), channel_id=1, source_target_pairs={{0,8},{8,16},{16,24},{24,32},{32,40},{40,48},{48,56},{56,64},{64,7... | collective-permute-start | bytes 172040 | tf_op jit(solution)/shard_map/ppermute | solution.py:381
  37.8 0.1 pad_add_fusion.place_ref
  37.9 0.0 collective-permute-done.4.high_ref
  37.9 1.4 %collective-permute-done.3.low_ref = f32[112,128]{1,0:T(8,128)S(1)} collective-permute-done((f32[112,128]{1,0:T(8,128)S(1)}, f32[112,128]{1,0:T(8,128)S(1)}, u32[]{:S(2)}, u32[]{:S(2)}) %collective-permute-start.3) | collective-permute-done | bytes 57376 | tf_op jit(solution)/shard_map/ppermute | solution.py:381
  39.2 5.3 %all-to-all-done.gathered_ref = f32[64,8,128]{2,1,0:T(8,128)S(1)} async-done(((f32[64,8,128]{2,1,0:T(8,128)}), f32[64,8,128]{2,1,0:T(8,128)S(1)}, u32[]{:S(2)}, u32[]{:S(2)}) %all-to-all-start) | async-done | bytes 262176 | tf_op jit(solution)/shard_map/all_to_all | solution.py:384
  44.5 1.0 shard_map.79
  45.5 1.9 %collective-permute-start.5 = (f32[96,128]{1,0:T(8,128)S(1)}, f32[96,128]{1,0:T(8,128)S(1)}, u32[]{:S(2)}, u32[]{:S(2)}) collective-permute-start(f32[96,128]{1,0:T(8,128)S(1)} %get-tuple-element.47), channel_id=1, source_target_pairs={{0,1},{1,0},{2,3},{3,2},{4,5},{5,4},{6,7},{7,6},{8,9},{9,8},{10,11... | collective-permute-start | bytes 147464 | tf_op jit(solution)/shard_map/ppermute | solution.py:412
  47.5 4.9 %collective-permute-start.6 = (f32[96,128]{1,0:T(8,128)S(1)}, f32[96,128]{1,0:T(8,128)S(1)}, u32[]{:S(2)}, u32[]{:S(2)}) collective-permute-start(f32[96,128]{1,0:T(8,128)S(1)} %get-tuple-element.48), channel_id=1, source_target_pairs={{1,2},{3,4},{5,6},{2,1},{4,3},{6,5},{9,10},{11,12},{13,14},{10,9},... | collective-permute-start | bytes 147464 | tf_op jit(solution)/shard_map/ppermute | solution.py:411
  52.4 0.0 collective-permute-done.5.near_ref
  52.4 2.3 %collective-permute-done.6.far_ref = f32[96,128]{1,0:T(8,128)S(1)} collective-permute-done((f32[96,128]{1,0:T(8,128)S(1)}, f32[96,128]{1,0:T(8,128)S(1)}, u32[]{:S(2)}, u32[]{:S(2)}) %collective-permute-start.6) | collective-permute-done | bytes 49184 | tf_op jit(solution)/shard_map/ppermute | solution.py:411
  54.7 1.8 %shard_map.80 = (f32[18,8,128]{2,1,0:T(8,128)S(1)}, f32[18,8,128]{2,1,0:T(8,128)S(1)}, f32[64,8,128]{2,1,0:T(8,128)}, f32[56,128]{1,0:T(8,128)S(1)}, f32[24,128]{1,0:T(8,128)S(1)}) custom-call(s32[2]{0:T(128)S(1)} %pad_add_fusion.place_ref, f32[18,16,128]{2,1,0:T(8,128)S(1)} %get-tuple-element.45.wide_ref, f32[18,8,128]{2,1,0:T(8,128)S(1)} %get-tuple-element.46.z_ref, ...), custom_call_target="tpu_custom_call" | custom-call | tf_op jit(solution)/shard_map/pallas_call | solution.py:36
  56.5 8.2 %all-to-all-start.1 = ((f32[64,8,128]{2,1,0:T(8,128)}), f32[64,8,128]{2,1,0:T(8,128)S(1)}, u32[]{:S(2)}, u32[]{:S(2)}) async-start(f32[64,8,128]{2,1,0:T(8,128)} %get-tuple-element.51), calls=%async_computation.1 | async-start | bytes 524288 | tf_op jit(solution)/shard_map/all_to_all | solution.py:384
  64.7 2.9 %collective-permute-start.7 = (f32[56,128]{1,0:T(8,128)S(1)}, f32[56,128]{1,0:T(8,128)S(1)}, u32[]{:S(2)}, u32[]{:S(2)}) collective-permute-start(f32[56,128]{1,0:T(8,128)S(1)} %get-tuple-element.54), channel_id=1, source_target_pairs={{0,8},{8,16},{16,24},{24,32},{32,40},{40,48},{48,56},{56,64},{64,7... | collective-permute-start | bytes 86024 | tf_op jit(solution)/shard_map/ppermute | solution.py:381
  67.7 1.3 %collective-permute-start.8 = (f32[24,128]{1,0:T(8,128)S(1)}, f32[24,128]{1,0:T(8,128)S(1)}, u32[]{:S(2)}, u32[]{:S(2)}) collective-permute-start(f32[24,128]{1,0:T(8,128)S(1)} %get-tuple-element.55), channel_id=1, source_target_pairs={{8,0},{16,8},{24,16},{32,24},{40,32},{48,40},{56,48},{64,56},{72,6... | collective-permute-start | bytes 36872 | tf_op jit(solution)/shard_map/ppermute | solution.py:381
  69.0 3.1 %collective-permute-done.8.high_ref = f32[24,128]{1,0:T(8,128)S(1)} collective-permute-done((f32[24,128]{1,0:T(8,128)S(1)}, f32[24,128]{1,0:T(8,128)S(1)}, u32[]{:S(2)}, u32[]{:S(2)}) %collective-permute-start.8) | collective-permute-done | bytes 12320 | tf_op jit(solution)/shard_map/ppermute | solution.py:381
  72.1 0.0 collective-permute-done.7.low_ref
  72.1 2.4 %all-to-all-done.1.gathered_ref = f32[64,8,128]{2,1,0:T(8,128)S(1)} async-done(((f32[64,8,128]{2,1,0:T(8,128)}), f32[64,8,128]{2,1,0:T(8,128)S(1)}, u32[]{:S(2)}, u32[]{:S(2)}) %all-to-all-start.1) | async-done | bytes 262176 | tf_op jit(solution)/shard_map/all_to_all | solution.py:384
  74.5 0.9 shard_map.81
  75.4 1.9 %collective-permute-start.9 = (f32[96,128]{1,0:T(8,128)S(1)}, f32[96,128]{1,0:T(8,128)S(1)}, u32[]{:S(2)}, u32[]{:S(2)}) collective-permute-start(f32[96,128]{1,0:T(8,128)S(1)} %get-tuple-element.59), channel_id=1, source_target_pairs={{0,1},{1,0},{2,3},{3,2},{4,5},{5,4},{6,7},{7,6},{8,9},{9,8},{10,11... | collective-permute-start | bytes 147464 | tf_op jit(solution)/shard_map/ppermute | solution.py:412
  77.3 9.4 %collective-permute-start.10 = (f32[96,128]{1,0:T(8,128)S(1)}, f32[96,128]{1,0:T(8,128)S(1)}, u32[]{:S(2)}, u32[]{:S(2)}) collective-permute-start(f32[96,128]{1,0:T(8,128)S(1)} %get-tuple-element.60), channel_id=1, source_target_pairs={{1,2},{3,4},{5,6},{2,1},{4,3},{6,5},{9,10},{11,12},{13,14},{10,9},... | collective-permute-start | bytes 147464 | tf_op jit(solution)/shard_map/ppermute | solution.py:411
  86.7 0.0 collective-permute-done.9.near_ref
  86.7 1.9 %collective-permute-done.10.far_ref = f32[96,128]{1,0:T(8,128)S(1)} collective-permute-done((f32[96,128]{1,0:T(8,128)S(1)}, f32[96,128]{1,0:T(8,128)S(1)}, u32[]{:S(2)}, u32[]{:S(2)}) %collective-permute-start.10) | collective-permute-done | bytes 49184 | tf_op jit(solution)/shard_map/ppermute | solution.py:411
  88.6 1.1 shard_map.82
  89.8 12.9 %all_to_all.20 = f32[32,1,128]{2,1,0:T(1,128)S(1)} all-to-all(f32[32,1,128]{2,1,0:T(1,128)S(1)} %get-tuple-element.62), channel_id=1, replica_groups={{0,16,32,48,64,80,96,112,128,144,160,176,192,208,224,240,256,272,288,30..., dimensions={0} | all-to-all | bytes 32768 | tf_op jit(solution)/shard_map/all_to_all | solution.py:431
  102.6 0.1 reduce_sum.9
  102.7 19.0 %all_to_all.21.dots_ref = f32[16,1,128]{2,1,0:T(1,128)S(1)} all-to-all(f32[16,1,128]{2,1,0:T(1,128)S(1)} %broadcast_in_dim.2), channel_id=1, replica_groups={{0,1,2,3,4,5,6,7,8,9,10,11,12,13,14,15},{16,17,18,19,20,21,22,23,24,25,..., dimensions={0} | all-to-all | bytes 16384 | tf_op jit(solution)/shard_map/all_to_all | solution.py:433
  121.7 1.1 shard_map.83
  (1 shorter events, 0.0 us)
Async XLA Ops:
  0.6 14.9 %copy-start = (f32[64,64]{1,0:T(8,128)S(1)}, f32[64,64]{1,0:T(8,128)}, u32[]{:S(2)}) copy-start(f32[64,64]{1,0:T(8,128)} %matrix_ref.5) | copy-start | bytes 49156
  2.1 13.4 %collective-permute-start = (f32[2,128]{1,0:T(2,128)S(1)}, f32[2,128]{1,0:T(2,128)S(1)}, u32[]{:S(2)}, u32[]{:S(2)}) collective-permute-start(f32[2,128]{1,0:T(2,128)S(1)} %get-tuple-element.34), channel_id=1, source_target_pairs={{0,1},{1,2},{2,3},{3,4},{4,5},{5,6},{6,7},{8,9},{9,10},{10,11},{11... | collective-permute-start | bytes 3080 | tf_op jit(solution)/shard_map/ppermute | solution.py:381
  7.7 7.8 %collective-permute-start.1 = (f32[2,128]{1,0:T(2,128)S(1)}, f32[2,128]{1,0:T(2,128)S(1)}, u32[]{:S(2)}, u32[]{:S(2)}) collective-permute-start(f32[2,128]{1,0:T(2,128)S(1)} %get-tuple-element.35), channel_id=1, source_target_pairs={{0,8},{8,16},{16,24},{24,32},{32,40},{40,48},{48,56},{56,64},{64,7... | collective-permute-start | bytes 3080 | tf_op jit(solution)/shard_map/ppermute | solution.py:381
  10.9 4.6 %collective-permute-start.2 = (f32[1,128]{1,0:T(1,128)S(1)}, f32[1,128]{1,0:T(1,128)S(1)}, u32[]{:S(2)}, u32[]{:S(2)}) collective-permute-start(f32[1,128]{1,0:T(1,128)S(1)} %get-tuple-element.36), channel_id=1, source_target_pairs={{0,9},{1,10},{2,11},{3,12},{4,13},{5,14},{6,15},{8,17},{9,18},{10,... | collective-permute-start | bytes 1544 | tf_op jit(solution)/shard_map/ppermute | solution.py:401
  16.6 27.9 %all-to-all-start = ((f32[64,8,128]{2,1,0:T(8,128)}), f32[64,8,128]{2,1,0:T(8,128)S(1)}, u32[]{:S(2)}, u32[]{:S(2)}) async-start(f32[64,8,128]{2,1,0:T(8,128)} %get-tuple-element.41), calls=%async_computation | async-start | bytes 524288 | tf_op jit(solution)/shard_map/all_to_all | solution.py:384
  32.5 5.4 %collective-permute-start.4 = (f32[40,128]{1,0:T(8,128)S(1)}, f32[40,128]{1,0:T(8,128)S(1)}, u32[]{:S(2)}, u32[]{:S(2)}) collective-permute-start(f32[40,128]{1,0:T(8,128)S(1)} %get-tuple-element.44), channel_id=1, source_target_pairs={{8,0},{16,8},{24,16},{32,24},{40,32},{48,40},{56,48},{64,56},{72,6... | collective-permute-start | bytes 61448 | tf_op jit(solution)/shard_map/ppermute | solution.py:381
  33.8 5.5 %collective-permute-start.3 = (f32[112,128]{1,0:T(8,128)S(1)}, f32[112,128]{1,0:T(8,128)S(1)}, u32[]{:S(2)}, u32[]{:S(2)}) collective-permute-start(f32[112,128]{1,0:T(8,128)S(1)} %get-tuple-element.43), channel_id=1, source_target_pairs={{0,8},{8,16},{16,24},{24,32},{32,40},{40,48},{48,56},{56,64},{64,7... | collective-permute-start | bytes 172040 | tf_op jit(solution)/shard_map/ppermute | solution.py:381
  45.5 6.9 %collective-permute-start.5 = (f32[96,128]{1,0:T(8,128)S(1)}, f32[96,128]{1,0:T(8,128)S(1)}, u32[]{:S(2)}, u32[]{:S(2)}) collective-permute-start(f32[96,128]{1,0:T(8,128)S(1)} %get-tuple-element.47), channel_id=1, source_target_pairs={{0,1},{1,0},{2,3},{3,2},{4,5},{5,4},{6,7},{7,6},{8,9},{9,8},{10,11... | collective-permute-start | bytes 147464 | tf_op jit(solution)/shard_map/ppermute | solution.py:412
  47.5 7.2 %collective-permute-start.6 = (f32[96,128]{1,0:T(8,128)S(1)}, f32[96,128]{1,0:T(8,128)S(1)}, u32[]{:S(2)}, u32[]{:S(2)}) collective-permute-start(f32[96,128]{1,0:T(8,128)S(1)} %get-tuple-element.48), channel_id=1, source_target_pairs={{1,2},{3,4},{5,6},{2,1},{4,3},{6,5},{9,10},{11,12},{13,14},{10,9},... | collective-permute-start | bytes 147464 | tf_op jit(solution)/shard_map/ppermute | solution.py:411
  56.5 18.0 %all-to-all-start.1 = ((f32[64,8,128]{2,1,0:T(8,128)}), f32[64,8,128]{2,1,0:T(8,128)S(1)}, u32[]{:S(2)}, u32[]{:S(2)}) async-start(f32[64,8,128]{2,1,0:T(8,128)} %get-tuple-element.51), calls=%async_computation.1 | async-start | bytes 524288 | tf_op jit(solution)/shard_map/all_to_all | solution.py:384
  64.7 7.4 %collective-permute-start.7 = (f32[56,128]{1,0:T(8,128)S(1)}, f32[56,128]{1,0:T(8,128)S(1)}, u32[]{:S(2)}, u32[]{:S(2)}) collective-permute-start(f32[56,128]{1,0:T(8,128)S(1)} %get-tuple-element.54), channel_id=1, source_target_pairs={{0,8},{8,16},{16,24},{24,32},{32,40},{40,48},{48,56},{56,64},{64,7... | collective-permute-start | bytes 86024 | tf_op jit(solution)/shard_map/ppermute | solution.py:381
  67.7 4.4 %collective-permute-start.8 = (f32[24,128]{1,0:T(8,128)S(1)}, f32[24,128]{1,0:T(8,128)S(1)}, u32[]{:S(2)}, u32[]{:S(2)}) collective-permute-start(f32[24,128]{1,0:T(8,128)S(1)} %get-tuple-element.55), channel_id=1, source_target_pairs={{8,0},{16,8},{24,16},{32,24},{40,32},{48,40},{56,48},{64,56},{72,6... | collective-permute-start | bytes 36872 | tf_op jit(solution)/shard_map/ppermute | solution.py:381
  75.4 11.3 %collective-permute-start.9 = (f32[96,128]{1,0:T(8,128)S(1)}, f32[96,128]{1,0:T(8,128)S(1)}, u32[]{:S(2)}, u32[]{:S(2)}) collective-permute-start(f32[96,128]{1,0:T(8,128)S(1)} %get-tuple-element.59), channel_id=1, source_target_pairs={{0,1},{1,0},{2,3},{3,2},{4,5},{5,4},{6,7},{7,6},{8,9},{9,8},{10,11... | collective-permute-start | bytes 147464 | tf_op jit(solution)/shard_map/ppermute | solution.py:412
  77.3 11.3 %collective-permute-start.10 = (f32[96,128]{1,0:T(8,128)S(1)}, f32[96,128]{1,0:T(8,128)S(1)}, u32[]{:S(2)}, u32[]{:S(2)}) collective-permute-start(f32[96,128]{1,0:T(8,128)S(1)} %get-tuple-element.60), channel_id=1, source_target_pairs={{1,2},{3,4},{5,6},{2,1},{4,3},{6,5},{9,10},{11,12},{13,14},{10,9},... | collective-permute-start | bytes 147464 | tf_op jit(solution)/shard_map/ppermute | solution.py:411

commit v3 on v2

--- a/solution.py
+++ b/solution.py
@@ -24,7 +24,7 @@
     return lax.broadcasted_iota(jnp.int32, shape, len(shape) - 1)
 
 
-def call(kernel, out_shapes, scratch, *operands, smem=(), away=()):
+def call(kernel, out_shapes, scratch, *operands, smem=(), away=(), sent=()):
     specs = [
         pl.BlockSpec(memory_space=pltpu.SMEM if index in smem else pltpu.HBM if index in away else pltpu.VMEM)
         for index in range(len(operands))
@@ -37,7 +37,9 @@
         kernel,
         out_shape=[jax.ShapeDtypeStruct(shape, F32) for shape in out_shapes],
         in_specs=specs,
-        out_specs=[pl.BlockSpec(memory_space=pltpu.VMEM)] * len(out_shapes),
+        out_specs=[
+            pl.BlockSpec(memory_space=pl.ANY if index in sent else pltpu.VMEM) for index in range(len(out_shapes))
+        ],
         scratch_shapes=[pltpu.VMEM(shape, F32) if isinstance(shape, tuple) else shape for shape in scratch],
         compiler_params=pltpu.CompilerParams(vmem_limit_bytes=24 << 20),
     )(*operands)
@@ -86,7 +88,7 @@
 
 
 def unpack_kernel(source_hbm, potential_hbm, map_hbm, region_hbm, table_hbm, r_ref, ionic_ref, label_ref, coarse_ref,
-                  own_ref, beside_ref, below_ref, corner_ref,
+                  own_ref, beside_ref,
                   rows_ref, turned_ref, source_ref, potential_ref, map_ref, region_ref, table_ref, sems):
     copies = [
         pltpu.make_async_copy(away, here, sems.at[index])
@@ -113,8 +115,6 @@
         own_ref[2 * i : 2 * i + 2, :] = sigma
     beside_ref[0:1, :] = own_ref[1:2, :]
     beside_ref[1:2, :] = own_ref[3:4, :]
-    below_ref[...] = own_ref[2:4, :]
-    corner_ref[...] = own_ref[3:4, :]
     for y in range(6):
         for x in range(6):
             row = y * 6 + x
@@ -136,16 +136,22 @@
     coarse_ref[...] = restrict(r_ref[...], label_ref[...])
 
 
-def send_slab(field_ref, up_ref, down_ref, up_start, down_start):
-    for n in range(18):
-        up_ref[up_start + 3 * n : up_start + 3 * n + 3, :] = field_ref[n, 3:6, :]
-        down_ref[down_start + n : down_start + n + 1, :] = field_ref[n, 0:1, :]
-
-
-def diagonal_kernel(own_ref, beside_ref, below_ref, corner_ref, matrix_ref, r_ref, ionic_ref, label_ref,
-                    coarse_ref, sigma_ref, diagonal_ref, scaled_ref, message_ref, up_ref, down_ref, total_ref):
-    sigma_ref[0:1, :] = corner_ref[...]
-    sigma_ref[1:3, :] = below_ref[...]
+def send_slab(even, fields, near_ref, far_ref, up_ref, down_ref):
+    up_ref[...] = jnp.zeros_like(up_ref)
+    down_ref[...] = jnp.zeros_like(down_ref)
+    for index, field_ref in enumerate(fields):
+        for n in range(18):
+            row = 56 * index + 3 * n
+            up_ref[row : row + 3, :] = field_ref[n, 3:6, :]
+            down_ref[56 * index + n : 56 * index + n + 1, :] = field_ref[n, 0:1, :]
+    near_ref[...] = jnp.where(even, up_ref[...], down_ref[...])
+    far_ref[...] = jnp.where(even, down_ref[...], up_ref[...])
+
+
+def diagonal_kernel(place_ref, own_ref, beside_ref, below_ref, matrix_ref, r_ref, ionic_ref, label_ref, coarse_ref,
+                    sigma_ref, diagonal_ref, scaled_ref, message_ref, near_ref, far_ref,
+                    total_ref, up_ref, down_ref, copies_ref, sem):
+    sigma_ref[0:3, :] = below_ref[...]
     for i in range(2):
         sigma_ref[3 + 3 * i : 4 + 3 * i, :] = beside_ref[i : i + 1, :]
         sigma_ref[4 + 3 * i : 6 + 3 * i, :] = own_ref[2 * i : 2 * i + 2, :]
@@ -159,12 +165,12 @@
     coarse_diag = SHARE * restrict(diagonal, labels)
     even = lanes((8, 128)) % 2 == 0
     message = jnp.where(even, coarse_ref[...], coarse_diag)
-    message_ref[...] = jnp.broadcast_to(message[None], message_ref.shape)
+    copies_ref[...] = jnp.broadcast_to(message[None], copies_ref.shape)
+    sending = pltpu.make_async_copy(copies_ref, message_ref, sem)
+    sending.start()
     scaled_ref[...] = r_ref[...] / diagonal
-    up_ref[...] = jnp.zeros_like(up_ref)
-    down_ref[...] = jnp.zeros_like(down_ref)
-    send_slab(scaled_ref, up_ref, down_ref, 0, 0)
-    send_slab(label_ref, up_ref, down_ref, 56, 20)
+    send_slab(place_ref[1] == 0, (scaled_ref, label_ref), near_ref, far_ref, up_ref, down_ref)
+    sending.wait()
 
 
 def along(values):
@@ -208,39 +214,36 @@
     return jnp.where(even, pltpu.roll(tiles, 127, tiles.ndim - 1), tiles)
 
 
-def widen(field_ref, low_ref, high_ref, low_start, high_start, wide_ref):
+def widen(field_ref, low, high, start, wide_ref):
     wide_ref[...] = jnp.zeros_like(wide_ref)
     for n in range(18):
-        wide_ref[n, 0:3, :] = low_ref[low_start + 3 * n : low_start + 3 * n + 3, :]
+        wide_ref[n, 0:3, :] = low[start + 3 * n : start + 3 * n + 3]
         wide_ref[n, 3:9, :] = field_ref[n, 0:6, :]
-        wide_ref[n, 9:10, :] = high_ref[high_start + n : high_start + n + 1, :]
-
-
-def send_cross(even, wide_ref, own_ref, near_ref, far_ref):
+        wide_ref[n, 9:10, :] = high[start + n : start + n + 1]
+
+
+def send_cross(even, wide_ref, own_ref, near_ref, far_ref, up_ref, down_ref):
     own_ref[...] = jnp.zeros_like(own_ref)
     for n in range(18):
         own_ref[n, 0:6, :] = wide_ref[n, 3:9, :]
-    near_ref[...] = jnp.zeros_like(near_ref)
-    far_ref[...] = jnp.zeros_like(far_ref)
-
-    def fill(up_ref, down_ref):
-        for c in range(3):
-            for y in range(3):
-                row = (3 * c + y) * 10
-                up_ref[row : row + 10, :] = wide_ref[6 * c + 3 + y, 0:10, :]
-            down_ref[10 * c : 10 * c + 10, :] = wide_ref[6 * c, 0:10, :]
-
-    @pl.when(even)
-    def _():
-        fill(near_ref, far_ref)
-
-    @pl.when(jnp.logical_not(even))
-    def _():
-        fill(far_ref, near_ref)
-
-
-def first_solve_kernel(place_ref, gathered_ref, scaled_ref, label_ref, low_ref, high_ref,
-                       wide_ref, z_ref, near_ref, far_ref, scale_ref, wide_label_ref):
+    up_ref[...] = jnp.zeros_like(up_ref)
+    down_ref[...] = jnp.zeros_like(down_ref)
+    for c in range(3):
+        for y in range(3):
+            row = (3 * c + y) * 10
+            up_ref[row : row + 10, :] = wide_ref[6 * c + 3 + y, 0:10, :]
+        down_ref[10 * c : 10 * c + 10, :] = wide_ref[6 * c, 0:10, :]
+    near_ref[...] = jnp.where(even, up_ref[...], down_ref[...])
+    far_ref[...] = jnp.where(even, down_ref[...], up_ref[...])
+
+
+def arrived(even, near_ref, far_ref):
+    return jnp.where(even, far_ref[...], near_ref[...]), jnp.where(even, near_ref[...], far_ref[...])
+
+
+def first_solve_kernel(place_ref, gathered_ref, scaled_ref, label_ref, left_ref, right_ref,
+                       wide_ref, z_ref, near_ref, far_ref, scale_ref, wide_label_ref, up_ref, down_ref):
+    low, high = arrived(place_ref[1] == 0, right_ref, left_ref)
     rows, valid = around(place_ref, gathered_ref.shape[0])
     tiles = jnp.concatenate([gathered_ref[pl.ds(row, 1)] for row in rows], 0)
     sums = jnp.sum(gathered_ref[...], axis=0)
@@ -250,23 +253,24 @@
     scale_ref[2 * NEAR + 1] = share
     level = smooth(DAMPING * even_part(tiles) * inverse, valid)
     coarse = level * inverse[REACH : REACH + 3] + (even_part(sums) * share)[None]
-    widen(label_ref, low_ref, high_ref, 56, 20, wide_label_ref)
-    widen(scaled_ref, low_ref, high_ref, 0, 0, wide_ref)
+    widen(label_ref, low, high, 56, wide_label_ref)
+    widen(scaled_ref, low, high, 0, wide_ref)
     wide_ref[...] += prolong(coarse, wide_label_ref[...])
-    send_cross(place_ref[1] == 0, wide_ref, z_ref, near_ref, far_ref)
-
-
-def next_solve_kernel(place_ref, gathered_ref, scaled_ref, wide_label_ref, low_ref, high_ref, scale_ref,
-                      wide_ref, w_ref, near_ref, far_ref):
+    send_cross(place_ref[2] == 0, wide_ref, z_ref, near_ref, far_ref, up_ref, down_ref)
+
+
+def next_solve_kernel(place_ref, gathered_ref, scaled_ref, wide_label_ref, left_ref, right_ref, scale_ref,
+                      wide_ref, w_ref, near_ref, far_ref, up_ref, down_ref):
+    low, high = arrived(place_ref[1] == 0, right_ref, left_ref)
     rows, valid = around(place_ref, gathered_ref.shape[0])
     tiles = jnp.concatenate([gathered_ref[pl.ds(row, 1)] for row in rows], 0)
     sums = jnp.sum(gathered_ref[...], axis=0)
     inverse = scale_ref[0 : 2 * NEAR + 1]
     level = smooth(DAMPING * tiles * inverse, valid)
     coarse = level * inverse[REACH : REACH + 3] + (sums * scale_ref[2 * NEAR + 1])[None]
-    widen(scaled_ref, low_ref, high_ref, 0, 0, wide_ref)
+    widen(scaled_ref, low, high, 0, wide_ref)
     wide_ref[...] += prolong(coarse, wide_label_ref[...])
-    send_cross(place_ref[1] == 0, wide_ref, w_ref, near_ref, far_ref)
+    send_cross(place_ref[2] == 0, wide_ref, w_ref, near_ref, far_ref, up_ref, down_ref)
 
 
 def operate(place_ref, wide_ref, field_ref, near_ref, far_ref, sigma_ref, matrix_ref, ionic_ref,
@@ -274,23 +278,12 @@
     for n in range(18):
         grid_ref[n // 6 * 10 + 3 + n % 6, 0:10, :] = wide_ref[n, 0:10, :]
 
-    def fill(above_ref, under_ref):
-        for c in range(3):
-            for y in range(3):
-                row = (3 * c + y) * 10
-                grid_ref[10 * c + y, 0:10, :] = above_ref[row : row + 10, :]
-            grid_ref[10 * c + 9, 0:10, :] = under_ref[10 * c : 10 * c + 10, :]
-
-    even = place_ref[1] == 0
-
-    @pl.when(even)
-    def _():
-        fill(far_ref, near_ref)
-
-    @pl.when(jnp.logical_not(even))
-    def _():
-        fill(near_ref, far_ref)
-
+    above, under = arrived(place_ref[2] == 0, near_ref, far_ref)
+    for c in range(3):
+        for y in range(3):
+            row = (3 * c + y) * 10
+            grid_ref[10 * c + y, 0:10, :] = above[row : row + 10]
+        grid_ref[10 * c + 9, 0:10, :] = under[10 * c : 10 * c + 10]
     end = lanes((10, 128)) == 127
     for y in range(10):
         grid_ref[30 + y, 0:10, :] = jnp.where(end, 0.0, pltpu.roll(grid_ref[y, 0:10, :], 127, 1))
@@ -314,18 +307,19 @@
     return total_ref[...] + ionic_ref[...] * field_ref[...]
 
 
-def first_image_kernel(place_ref, wide_ref, z_ref, near_ref, far_ref, sigma_ref, matrix_ref, ionic_ref, diagonal_ref, label_ref,
-                       q_ref, scaled_ref, message_ref, up_ref, down_ref, *scratch):
+def first_image_kernel(place_ref, wide_ref, z_ref, far_ref, near_ref, sigma_ref, matrix_ref, ionic_ref, diagonal_ref, label_ref,
+                       q_ref, scaled_ref, message_ref, left_ref, right_ref, up_ref, down_ref, copies_ref, sem, *scratch):
     image = operate(place_ref, wide_ref, z_ref, near_ref, far_ref, sigma_ref, matrix_ref, ionic_ref, *scratch)
     q_ref[...] = image
-    message_ref[...] = jnp.broadcast_to(restrict(image, label_ref[...])[None], message_ref.shape)
+    copies_ref[...] = jnp.broadcast_to(restrict(image, label_ref[...])[None], copies_ref.shape)
+    sending = pltpu.make_async_copy(copies_ref, message_ref, sem)
+    sending.start()
     scaled_ref[...] = image / diagonal_ref[...]
-    up_ref[...] = jnp.zeros_like(up_ref)
-    down_ref[...] = jnp.zeros_like(down_ref)
-    send_slab(scaled_ref, up_ref, down_ref, 0, 0)
-
-
-def next_image_kernel(place_ref, wide_ref, w_ref, near_ref, far_ref, sigma_ref, matrix_ref, ionic_ref,
+    send_slab(place_ref[1] == 0, (scaled_ref,), left_ref, right_ref, up_ref, down_ref)
+    sending.wait()
+
+
+def next_image_kernel(place_ref, wide_ref, w_ref, far_ref, near_ref, sigma_ref, matrix_ref, ionic_ref,
                       r_ref, z_ref, q_ref, t_ref, message_ref, *scratch):
     image = operate(place_ref, wide_ref, w_ref, near_ref, far_ref, sigma_ref, matrix_ref, ionic_ref, *scratch)
     t_ref[...] = image
@@ -369,7 +363,7 @@
     n_slab = lax.axis_size("slab")
     n_cross = lax.axis_size("cross")
     slab, cross = lax.axis_index("slab"), lax.axis_index("cross")
-    place = jnp.stack([slab, cross % 2]).astype(jnp.int32)
+    place = jnp.stack([slab, slab % 2, cross % 2]).astype(jnp.int32)
     columns = [
         [slab * n_cross + cross for slab in (2 * pair, 2 * pair + 1) for cross in range(n_cross)]
         for pair in range(n_slab // 2)
@@ -385,48 +379,46 @@
 
     field, wide = (18, 8, 128), (18, 16, 128)
     space = [(40, 16, 128), (64, 1152), (64, 1152), field]
-    pairs = [
-        (slab * n_cross + cross, (slab + 1) * n_cross + cross + 1)
-        for slab in range(n_slab - 1)
-        for cross in range(n_cross - 1)
-    ]
-    r, ionic, labels, coarse, own, beside, below, corner = call(
-        unpack_kernel, [field] * 3 + [(8, 128), (4, 128), (2, 128), (2, 128), (1, 128)],
+    r, ionic, labels, coarse, own, beside = call(
+        unpack_kernel, [field] * 3 + [(8, 128), (4, 128), (2, 128)],
         [(128, 384), (384, 128), (6, 6, 384), (6, 6, 384), pltpu.VMEM((6, 6, 384), jnp.int32),
          pltpu.VMEM((2, 2, 128), jnp.int32), pltpu.SMEM((4,), F32), pltpu.SemaphoreType.DMA((5,))],
         adjoint_source, potential, restriction_map, region_labels, conductivity, away=(0, 1, 2, 3, 4),
     )
-    sigma, diagonal, scaled, message, up, down = call(
-        diagonal_kernel, [(9, 128), field, field, (n_slab, 8, 128), (112, 128), (40, 128)], [field],
-        own, shifted(beside, "cross", 1), shifted(below, "slab", 1), lax.ppermute(corner, ("slab", "cross"), pairs),
-        element_matrix, r, ionic, labels, coarse,
-    )
-
-    def beyond(up, down):
-        return shifted(up, "slab", 1), shifted(down, "slab", -1)
-
-    def across(near, far):
-        far_pairs = [(c, c + 1) for c in range(1, n_cross - 1, 2)]
+    beside = shifted(beside, "cross", 1)
+    below = shifted(jnp.concatenate([beside[1:2], own[2:4]], 0), "slab", 1)
+    copies = [(n_slab, 8, 128), pltpu.SemaphoreType.DMA]
+    sigma, diagonal, scaled, message, near, far = call(
+        diagonal_kernel, [(9, 128), field, field, (n_slab, 8, 128), (112, 128), (112, 128)],
+        [field, (112, 128), (112, 128), *copies],
+        place, own, beside, below, element_matrix, r, ionic, labels, coarse, smem=(0,), sent=(3,),
+    )
+
+    def exchange(near, far, axis):
+        count = lax.axis_size(axis)
+        far_pairs = [(c, c + 1) for c in range(1, count - 1, 2)]
         far_pairs += [(above, c) for c, above in far_pairs]
-        far = lax.ppermute(far, "cross", far_pairs)
-        return lax.ppermute(near, "cross", [(c, c ^ 1) for c in range(n_cross)]), far
+        far = lax.ppermute(far, axis, far_pairs)
+        return far, lax.ppermute(near, axis, [(c, c ^ 1) for c in range(count)])
 
     faces = [(96, 128), (96, 128)]
     wide_z, z, near, far, scale, wide_labels = call(
-        first_solve_kernel, [wide, field, *faces, (10, 8, 128), wide], [],
-        place, gather(message), scaled, labels, *beyond(up, down), smem=(0,),
-    )
-    q, scaled, message, up, down = call(
-        first_image_kernel, [field, field, (n_slab, 8, 128), (56, 128), (24, 128)], space,
-        place, wide_z, z, *across(near, far), sigma, element_matrix, ionic, diagonal, labels, smem=(0,),
+        first_solve_kernel, [wide, field, *faces, (10, 8, 128), wide], faces,
+        place, gather(message), scaled, labels, *exchange(near, far, "slab"), smem=(0,),
+    )
+    q, scaled, message, near, far = call(
+        first_image_kernel, [field, field, (n_slab, 8, 128), (56, 128), (56, 128)],
+        [(56, 128), (56, 128), *copies, *space],
+        place, wide_z, z, *exchange(near, far, "cross"), sigma, element_matrix, ionic, diagonal, labels,
+        smem=(0,), sent=(2,),
     )
     wide_w, w, near, far = call(
-        next_solve_kernel, [wide, field, *faces], [],
-        place, gather(message), scaled, wide_labels, *beyond(up, down), scale, smem=(0,),
+        next_solve_kernel, [wide, field, *faces], faces,
+        place, gather(message), scaled, wide_labels, *exchange(near, far, "slab"), scale, smem=(0,),
     )
     t, message = call(
         next_image_kernel, [field, (n_slab // 2, 1, 128)], space,
-        place, wide_w, w, *across(near, far), sigma, element_matrix, ionic, r, z, q, smem=(0,),
+        place, wide_w, w, *exchange(near, far, "cross"), sigma, element_matrix, ionic, r, z, q, smem=(0,),
     )
     parts = lax.all_to_all(message, "slab", 0, 0, axis_index_groups=planes, tiled=True)
     parts = jnp.broadcast_to(jnp.sum(parts, 0)[None], (2 * n_cross, 1, 128))

time: 123 us -> 117 us (0.951)
  blocking collectives: 31.9 us -> 27.6 us
  starting transfers between devices: 64.4 us -> 60.3 us
  waiting for transfers between devices: 17.1 us -> 19 us
    ppermute x6 -> x2, starting transfers between devices: 18.3 us -> 6.9 us  [shifted(): return lax.ppermute(value, axis, pairs)]
    ppermute x5 -> x8, starting transfers between devices: 22 us -> 32.4 us  [the longest x4 17.9 us: exchange(): far = lax.ppermute(far, axis, far_pairs)]
    all_to_all x1, blocking collectives: 19 us -> 14.5 us  [body(): lax.all_to_all(parts, ('slab', 'cross'), 0, 0, axis_index_groups=columns,...]
    all_to_all x2, starting transfers between devices: 24.1 us -> 21 us  [gather(): return lax.all_to_all(copies, 'slab', 0, 0, tiled=True)]
    ppermute x5 -> x8, waiting for transfers between devices: 4.92 us -> 6.27 us  [the longest x4 6.25 us: exchange(): return (far, lax.ppermute(near, axis, [(c, c ^ 1) for c in range(count)]))]
    all_to_all x2, waiting for transfers between devices: 7.68 us -> 8.97 us  [gather(): return lax.all_to_all(copies, 'slab', 0, 0, tiled=True)]
    ppermute x6 -> x2, waiting for transfers between devices: 4.53 us -> 3.76 us  [shifted(): return lax.ppermute(value, axis, pairs)]
  transfers between devices with their start and end apart: 13 -> 12, of which waited for: 7 -> 8; matrix products, arithmetic and copies ran while one was open for 0% -> 0% of each run, Pallas kernels for 0% -> 0%
where the time goes in v3:
time: 117 us
  starting transfers between devices  60.3 us (52%)
  blocking collectives  27.6 us (24%)
  waiting for transfers between devices  19 us (16%)
  Pallas kernels  9.06 us (8%)
    all_to_all x2, starting transfers between devices, gather(): return lax.all_to_all(copies, 'slab', 0, 0, tiled=True)  21 us
    ppermute x4, starting transfers between devices, exchange(): far = lax.ppermute(far, axis, far_pairs)  17.9 us
    ppermute x4, starting transfers between devices, exchange(): return (far, lax.ppermute(near, axis, [(c, c ^ 1) for c in range(count)]))  14.5 us
    all_to_all x1, blocking collectives, body(): lax.all_to_all(parts, ('slab', 'cross'), 0, 0, axis_index_groups=columns,...  14.5 us
    all_to_all x1, blocking collectives, body(): lax.all_to_all(message, 'slab', 0, 0, axis_index_groups=planes, tiled=True)  13 us
    pallas_call x7, Pallas kernels, call(): pl.pallas_call(kernel, out_shape=[jax.ShapeDtypeStruct(shape, F32) for sh...  9.06 us
    all_to_all x2, waiting for transfers between devices, gather(): return lax.all_to_all(copies, 'slab', 0, 0, tiled=True)  8.97 us
    ppermute x2, starting transfers between devices, shifted(): return lax.ppermute(value, axis, pairs)  6.9 us
  transfers between devices with their start and end apart: 12, of which 8 were waited for; matrix products, arithmetic and copies ran while one was open for 0% of the time, Pallas kernels for 0%

profile of v3, /device:TPU:1, one launch (start us, length us, event | category | flops | bytes accessed | tf_op | source)
XLA Modules:
  0.0 116.9 jit_solution(6812770763556436363)
XLA Ops:
  0.6 1.4 %shard_map.77 = (f32[18,8,128]{2,1,0:T(8,128)S(1)}, f32[18,8,128]{2,1,0:T(8,128)S(1)}, f32[18,8,128]{2,1,0:T(8,128)S(1)}, f32[8,128]{1,0:T(8,128)S(1)}, f32[4,128]{1,0:T(4,128)S(1)}, /*index=5*/f32[2,128]{1,0:T(2,128)S(1)}) custom-call(f32[6,6,384]{2,1,0:T(8,128)} %source_hbm.1, f32[6,6,384]{2,1,0:T(8,128)} %potential_hbm.1, s32[6,6,384]{2,1,0:T(8,128)} %map_hbm.1, ...), custom_call_target="tpu_custom_call" | custom-call | tf_op jit(solution)/shard_map/pallas_call | solution.py:36
  2.1 5.6 %collective-permute-start = (f32[2,128]{1,0:T(2,128)S(1)}, f32[2,128]{1,0:T(2,128)S(1)}, u32[]{:S(2)}, u32[]{:S(2)}) collective-permute-start(f32[2,128]{1,0:T(2,128)S(1)} %get-tuple-element.32), channel_id=1, source_target_pairs={{0,1},{1,2},{2,3},{3,4},{4,5},{5,6},{6,7},{8,9},{9,10},{10,11},{11... | collective-permute-start | bytes 3080 | tf_op jit(solution)/shard_map/ppermute | solution.py:375
  7.7 0.0 copy-start
  7.7 3.1 %collective-permute-done.beside_ref = f32[2,128]{1,0:T(2,128)S(1)} collective-permute-done((f32[2,128]{1,0:T(2,128)S(1)}, f32[2,128]{1,0:T(2,128)S(1)}, u32[]{:S(2)}, u32[]{:S(2)}) %collective-permute-start) | collective-permute-done | bytes 1056 | tf_op jit(solution)/shard_map/ppermute | solution.py:375
  10.9 1.3 %collective-permute-start.1 = (f32[3,128]{1,0:T(4,128)S(1)}, f32[3,128]{1,0:T(4,128)S(1)}, u32[]{:S(2)}, u32[]{:S(2)}) collective-permute-start(f32[3,128]{1,0:T(4,128)S(1)} %pad_maximum_fusion), channel_id=1, source_target_pairs={{0,8},{8,16},{16,24},{24,32},{32,40},{40,48},{48,56},{56,64},{64,7... | collective-permute-start | bytes 4616 | tf_op jit(solution)/shard_map/ppermute | solution.py:375
  12.2 0.1 pad_add_fusion.place_ref
  12.3 0.6 collective-permute-done.1.below_ref
  12.9 0.0 copy-done
  12.9 1.7 %shard_map.78 = (f32[9,128]{1,0:T(8,128)S(1)}, f32[18,8,128]{2,1,0:T(8,128)S(1)}, f32[18,8,128]{2,1,0:T(8,128)S(1)}, f32[64,8,128]{2,1,0:T(8,128)}, f32[112,128]{1,0:T(8,128)S(1)}, /*index=5*/f32[112,128]{1,0:T(8,128)S(1)}) custom-call(s32[3]{0:T(128)S(1)} %pad_add_fusion.place_ref, f32[4,128]{1,0:T(4,128)S(1)} %get-tuple-element.31.own_ref, ...), custom_call_target="tpu_custom_call" | custom-call | tf_op jit(solution)/shard_map/pallas_call | solution.py:36
  14.6 15.4 %all-to-all-start = ((f32[64,8,128]{2,1,0:T(8,128)}), f32[64,8,128]{2,1,0:T(8,128)S(1)}, u32[]{:S(2)}, u32[]{:S(2)}) async-start(f32[64,8,128]{2,1,0:T(8,128)} %get-tuple-element.37), calls=%async_computation | async-start | bytes 524288 | tf_op jit(solution)/shard_map/all_to_all | solution.py:378
  30.0 0.7 collective-permute-start.2
  30.7 5.3 %collective-permute-start.3 = (f32[112,128]{1,0:T(8,128)S(1)}, f32[112,128]{1,0:T(8,128)S(1)}, u32[]{:S(2)}, u32[]{:S(2)}) collective-permute-start(f32[112,128]{1,0:T(8,128)S(1)} %get-tuple-element.40), channel_id=1, source_target_pairs={{0,8},{8,0},{16,24},{24,16},{32,40},{40,32},{48,56},{56,48},{64,72... | collective-permute-start | bytes 172040 | tf_op jit(solution)/shard_map/ppermute | solution.py:402
  36.0 0.0 collective-permute-done.2.left_ref
  36.0 2.4 %collective-permute-done.3.right_ref = f32[112,128]{1,0:T(8,128)S(1)} collective-permute-done((f32[112,128]{1,0:T(8,128)S(1)}, f32[112,128]{1,0:T(8,128)S(1)}, u32[]{:S(2)}, u32[]{:S(2)}) %collective-permute-start.3) | collective-permute-done | bytes 57376 | tf_op jit(solution)/shard_map/ppermute | solution.py:402
  38.4 5.2 %all-to-all-done.gathered_ref = f32[64,8,128]{2,1,0:T(8,128)S(1)} async-done(((f32[64,8,128]{2,1,0:T(8,128)}), f32[64,8,128]{2,1,0:T(8,128)S(1)}, u32[]{:S(2)}, u32[]{:S(2)}) %all-to-all-start) | async-done | bytes 262176 | tf_op jit(solution)/shard_map/all_to_all | solution.py:378
  43.6 1.0 shard_map.79
  44.6 6.9 %collective-permute-start.4 = (f32[96,128]{1,0:T(8,128)S(1)}, f32[96,128]{1,0:T(8,128)S(1)}, u32[]{:S(2)}, u32[]{:S(2)}) collective-permute-start(f32[96,128]{1,0:T(8,128)S(1)} %get-tuple-element.43), channel_id=1, source_target_pairs={{1,2},{3,4},{5,6},{2,1},{4,3},{6,5},{9,10},{11,12},{13,14},{10,9},... | collective-permute-start | bytes 147464 | tf_op jit(solution)/shard_map/ppermute | solution.py:401
  51.5 1.9 %collective-permute-start.5 = (f32[96,128]{1,0:T(8,128)S(1)}, f32[96,128]{1,0:T(8,128)S(1)}, u32[]{:S(2)}, u32[]{:S(2)}) collective-permute-start(f32[96,128]{1,0:T(8,128)S(1)} %get-tuple-element.44), channel_id=1, source_target_pairs={{0,1},{1,0},{2,3},{3,2},{4,5},{5,4},{6,7},{7,6},{8,9},{9,8},{10,11... | collective-permute-start | bytes 147464 | tf_op jit(solution)/shard_map/ppermute | solution.py:402
  53.4 0.0 collective-permute-done.4.far_ref
  53.4 1.2 %collective-permute-done.5.near_ref = f32[96,128]{1,0:T(8,128)S(1)} collective-permute-done((f32[96,128]{1,0:T(8,128)S(1)}, f32[96,128]{1,0:T(8,128)S(1)}, u32[]{:S(2)}, u32[]{:S(2)}) %collective-permute-start.5) | collective-permute-done | bytes 49184 | tf_op jit(solution)/shard_map/ppermute | solution.py:402
  54.6 1.9 %shard_map.80 = (f32[18,8,128]{2,1,0:T(8,128)S(1)}, f32[18,8,128]{2,1,0:T(8,128)S(1)}, f32[64,8,128]{2,1,0:T(8,128)}, f32[56,128]{1,0:T(8,128)S(1)}, f32[56,128]{1,0:T(8,128)S(1)}) custom-call(s32[3]{0:T(128)S(1)} %pad_add_fusion.place_ref, f32[18,16,128]{2,1,0:T(8,128)S(1)} %get-tuple-element.41.wide_ref, f32[18,8,128]{2,1,0:T(8,128)S(1)} %get-tuple-element.42.z_ref, ...), custom_call_target="tpu_custom_call" | custom-call | tf_op jit(solution)/shard_map/pallas_call | solution.py:36
  56.5 5.5 %all-to-all-start.1 = ((f32[64,8,128]{2,1,0:T(8,128)}), f32[64,8,128]{2,1,0:T(8,128)S(1)}, u32[]{:S(2)}, u32[]{:S(2)}) async-start(f32[64,8,128]{2,1,0:T(8,128)} %get-tuple-element.47), calls=%async_computation.1 | async-start | bytes 524288 | tf_op jit(solution)/shard_map/all_to_all | solution.py:378
  62.0 0.7 collective-permute-start.6
  62.7 5.3 %collective-permute-start.7 = (f32[56,128]{1,0:T(8,128)S(1)}, f32[56,128]{1,0:T(8,128)S(1)}, u32[]{:S(2)}, u32[]{:S(2)}) collective-permute-start(f32[56,128]{1,0:T(8,128)S(1)} %get-tuple-element.51), channel_id=1, source_target_pairs={{0,8},{8,0},{16,24},{24,16},{32,40},{40,32},{48,56},{56,48},{64,72... | collective-permute-start | bytes 86024 | tf_op jit(solution)/shard_map/ppermute | solution.py:402
  68.1 0.0 collective-permute-done.6.left_ref
  68.1 1.5 %collective-permute-done.7.right_ref = f32[56,128]{1,0:T(8,128)S(1)} collective-permute-done((f32[56,128]{1,0:T(8,128)S(1)}, f32[56,128]{1,0:T(8,128)S(1)}, u32[]{:S(2)}, u32[]{:S(2)}) %collective-permute-start.7) | collective-permute-done | bytes 28704 | tf_op jit(solution)/shard_map/ppermute | solution.py:402
  69.6 3.8 %all-to-all-done.1.gathered_ref = f32[64,8,128]{2,1,0:T(8,128)S(1)} async-done(((f32[64,8,128]{2,1,0:T(8,128)}), f32[64,8,128]{2,1,0:T(8,128)S(1)}, u32[]{:S(2)}, u32[]{:S(2)}) %all-to-all-start.1) | async-done | bytes 262176 | tf_op jit(solution)/shard_map/all_to_all | solution.py:378
  73.4 0.9 shard_map.81
  74.3 9.6 %collective-permute-start.8 = (f32[96,128]{1,0:T(8,128)S(1)}, f32[96,128]{1,0:T(8,128)S(1)}, u32[]{:S(2)}, u32[]{:S(2)}) collective-permute-start(f32[96,128]{1,0:T(8,128)S(1)} %get-tuple-element.55), channel_id=1, source_target_pairs={{1,2},{3,4},{5,6},{2,1},{4,3},{6,5},{9,10},{11,12},{13,14},{10,9},... | collective-permute-start | bytes 147464 | tf_op jit(solution)/shard_map/ppermute | solution.py:401
  83.9 1.9 %collective-permute-start.9 = (f32[96,128]{1,0:T(8,128)S(1)}, f32[96,128]{1,0:T(8,128)S(1)}, u32[]{:S(2)}, u32[]{:S(2)}) collective-permute-start(f32[96,128]{1,0:T(8,128)S(1)} %get-tuple-element.56), channel_id=1, source_target_pairs={{0,1},{1,0},{2,3},{3,2},{4,5},{5,4},{6,7},{7,6},{8,9},{9,8},{10,11... | collective-permute-start | bytes 147464 | tf_op jit(solution)/shard_map/ppermute | solution.py:402
  85.8 0.0 collective-permute-done.8.far_ref
  85.8 1.2 %collective-permute-done.9.near_ref = f32[96,128]{1,0:T(8,128)S(1)} collective-permute-done((f32[96,128]{1,0:T(8,128)S(1)}, f32[96,128]{1,0:T(8,128)S(1)}, u32[]{:S(2)}, u32[]{:S(2)}) %collective-permute-start.9) | collective-permute-done | bytes 49184 | tf_op jit(solution)/shard_map/ppermute | solution.py:402
  87.0 1.1 shard_map.82
  88.2 13.0 %all_to_all.20 = f32[32,1,128]{2,1,0:T(1,128)S(1)} all-to-all(f32[32,1,128]{2,1,0:T(1,128)S(1)} %get-tuple-element.58), channel_id=1, replica_groups={{0,16,32,48,64,80,96,112,128,144,160,176,192,208,224,240,256,272,288,30..., dimensions={0} | all-to-all | bytes 32768 | tf_op jit(solution)/shard_map/all_to_all | solution.py:423
  101.2 0.1 reduce_sum.9
  101.3 14.5 %all_to_all.21.dots_ref = f32[16,1,128]{2,1,0:T(1,128)S(1)} all-to-all(f32[16,1,128]{2,1,0:T(1,128)S(1)} %broadcast_in_dim.2), channel_id=1, replica_groups={{0,1,2,3,4,5,6,7,8,9,10,11,12,13,14,15},{16,17,18,19,20,21,22,23,24,25,..., dimensions={0} | all-to-all | bytes 16384 | tf_op jit(solution)/shard_map/all_to_all | solution.py:425
  115.8 1.1 shard_map.83
  (4 shorter events, 0.0 us)
Async XLA Ops:
  2.1 8.8 %collective-permute-start = (f32[2,128]{1,0:T(2,128)S(1)}, f32[2,128]{1,0:T(2,128)S(1)}, u32[]{:S(2)}, u32[]{:S(2)}) collective-permute-start(f32[2,128]{1,0:T(2,128)S(1)} %get-tuple-element.32), channel_id=1, source_target_pairs={{0,1},{1,2},{2,3},{3,4},{4,5},{5,6},{6,7},{8,9},{9,10},{10,11},{11... | collective-permute-start | bytes 3080 | tf_op jit(solution)/shard_map/ppermute | solution.py:375
  7.7 5.2 %copy-start = (f32[64,64]{1,0:T(8,128)S(1)}, f32[64,64]{1,0:T(8,128)}, u32[]{:S(2)}) copy-start(f32[64,64]{1,0:T(8,128)} %matrix_ref.5) | copy-start | bytes 49156
  10.9 2.0 %collective-permute-start.1 = (f32[3,128]{1,0:T(4,128)S(1)}, f32[3,128]{1,0:T(4,128)S(1)}, u32[]{:S(2)}, u32[]{:S(2)}) collective-permute-start(f32[3,128]{1,0:T(4,128)S(1)} %pad_maximum_fusion), channel_id=1, source_target_pairs={{0,8},{8,16},{16,24},{24,32},{32,40},{40,48},{48,56},{56,64},{64,7... | collective-permute-start | bytes 4616 | tf_op jit(solution)/shard_map/ppermute | solution.py:375
  14.6 29.0 %all-to-all-start = ((f32[64,8,128]{2,1,0:T(8,128)}), f32[64,8,128]{2,1,0:T(8,128)S(1)}, u32[]{:S(2)}, u32[]{:S(2)}) async-start(f32[64,8,128]{2,1,0:T(8,128)} %get-tuple-element.37), calls=%async_computation | async-start | bytes 524288 | tf_op jit(solution)/shard_map/all_to_all | solution.py:378
  30.0 6.0 %collective-permute-start.2 = (f32[112,128]{1,0:T(8,128)S(1)}, f32[112,128]{1,0:T(8,128)S(1)}, u32[]{:S(2)}, u32[]{:S(2)}) collective-permute-start(f32[112,128]{1,0:T(8,128)S(1)} %get-tuple-element.39), channel_id=1, source_target_pairs={{8,16},{24,32},{40,48},{56,64},{72,80},{88,96},{104,112},{120,128}... | collective-permute-start | bytes 172040 | tf_op jit(solution)/shard_map/ppermute | solution.py:401
  30.7 7.7 %collective-permute-start.3 = (f32[112,128]{1,0:T(8,128)S(1)}, f32[112,128]{1,0:T(8,128)S(1)}, u32[]{:S(2)}, u32[]{:S(2)}) collective-permute-start(f32[112,128]{1,0:T(8,128)S(1)} %get-tuple-element.40), channel_id=1, source_target_pairs={{0,8},{8,0},{16,24},{24,16},{32,40},{40,32},{48,56},{56,48},{64,72... | collective-permute-start | bytes 172040 | tf_op jit(solution)/shard_map/ppermute | solution.py:402
  44.6 8.9 %collective-permute-start.4 = (f32[96,128]{1,0:T(8,128)S(1)}, f32[96,128]{1,0:T(8,128)S(1)}, u32[]{:S(2)}, u32[]{:S(2)}) collective-permute-start(f32[96,128]{1,0:T(8,128)S(1)} %get-tuple-element.43), channel_id=1, source_target_pairs={{1,2},{3,4},{5,6},{2,1},{4,3},{6,5},{9,10},{11,12},{13,14},{10,9},... | collective-permute-start | bytes 147464 | tf_op jit(solution)/shard_map/ppermute | solution.py:401
  51.5 3.1 %collective-permute-start.5 = (f32[96,128]{1,0:T(8,128)S(1)}, f32[96,128]{1,0:T(8,128)S(1)}, u32[]{:S(2)}, u32[]{:S(2)}) collective-permute-start(f32[96,128]{1,0:T(8,128)S(1)} %get-tuple-element.44), channel_id=1, source_target_pairs={{0,1},{1,0},{2,3},{3,2},{4,5},{5,4},{6,7},{7,6},{8,9},{9,8},{10,11... | collective-permute-start | bytes 147464 | tf_op jit(solution)/shard_map/ppermute | solution.py:402
  56.5 16.9 %all-to-all-start.1 = ((f32[64,8,128]{2,1,0:T(8,128)}), f32[64,8,128]{2,1,0:T(8,128)S(1)}, u32[]{:S(2)}, u32[]{:S(2)}) async-start(f32[64,8,128]{2,1,0:T(8,128)} %get-tuple-element.47), calls=%async_computation.1 | async-start | bytes 524288 | tf_op jit(solution)/shard_map/all_to_all | solution.py:378
  62.0 6.0 %collective-permute-start.6 = (f32[56,128]{1,0:T(8,128)S(1)}, f32[56,128]{1,0:T(8,128)S(1)}, u32[]{:S(2)}, u32[]{:S(2)}) collective-permute-start(f32[56,128]{1,0:T(8,128)S(1)} %get-tuple-element.50), channel_id=1, source_target_pairs={{8,16},{24,32},{40,48},{56,64},{72,80},{88,96},{104,112},{120,128}... | collective-permute-start | bytes 86024 | tf_op jit(solution)/shard_map/ppermute | solution.py:401
  62.7 6.9 %collective-permute-start.7 = (f32[56,128]{1,0:T(8,128)S(1)}, f32[56,128]{1,0:T(8,128)S(1)}, u32[]{:S(2)}, u32[]{:S(2)}) collective-permute-start(f32[56,128]{1,0:T(8,128)S(1)} %get-tuple-element.51), channel_id=1, source_target_pairs={{0,8},{8,0},{16,24},{24,16},{32,40},{40,32},{48,56},{56,48},{64,72... | collective-permute-start | bytes 86024 | tf_op jit(solution)/shard_map/ppermute | solution.py:402
  74.3 11.6 %collective-permute-start.8 = (f32[96,128]{1,0:T(8,128)S(1)}, f32[96,128]{1,0:T(8,128)S(1)}, u32[]{:S(2)}, u32[]{:S(2)}) collective-permute-start(f32[96,128]{1,0:T(8,128)S(1)} %get-tuple-element.55), channel_id=1, source_target_pairs={{1,2},{3,4},{5,6},{2,1},{4,3},{6,5},{9,10},{11,12},{13,14},{10,9},... | collective-permute-start | bytes 147464 | tf_op jit(solution)/shard_map/ppermute | solution.py:401
  83.9 3.1 %collective-permute-start.9 = (f32[96,128]{1,0:T(8,128)S(1)}, f32[96,128]{1,0:T(8,128)S(1)}, u32[]{:S(2)}, u32[]{:S(2)}) collective-permute-start(f32[96,128]{1,0:T(8,128)S(1)} %get-tuple-element.56), channel_id=1, source_target_pairs={{0,1},{1,0},{2,3},{3,2},{4,5},{5,4},{6,7},{7,6},{8,9},{9,8},{10,11... | collective-permute-start | bytes 147464 | tf_op jit(solution)/shard_map/ppermute | solution.py:402

commit v4 on v3

--- a/solution.py
+++ b/solution.py
@@ -24,7 +24,7 @@
     return lax.broadcasted_iota(jnp.int32, shape, len(shape) - 1)
 
 
-def call(kernel, out_shapes, scratch, *operands, smem=(), away=(), sent=()):
+def call(kernel, out_shapes, scratch, *operands, smem=(), away=()):
     specs = [
         pl.BlockSpec(memory_space=pltpu.SMEM if index in smem else pltpu.HBM if index in away else pltpu.VMEM)
         for index in range(len(operands))
@@ -37,9 +37,7 @@
         kernel,
         out_shape=[jax.ShapeDtypeStruct(shape, F32) for shape in out_shapes],
         in_specs=specs,
-        out_specs=[
-            pl.BlockSpec(memory_space=pl.ANY if index in sent else pltpu.VMEM) for index in range(len(out_shapes))
-        ],
+        out_specs=[pl.BlockSpec(memory_space=pltpu.VMEM)] * len(out_shapes),
         scratch_shapes=[pltpu.VMEM(shape, F32) if isinstance(shape, tuple) else shape for shape in scratch],
         compiler_params=pltpu.CompilerParams(vmem_limit_bytes=24 << 20),
     )(*operands)
@@ -87,9 +85,16 @@
                         total_ref[c * 6 + y, x : x + high_a - low_a, :] += rows
 
 
+def conductance(region, table_ref):
+    value = jnp.zeros(region.shape, F32)
+    for index in range(4):
+        value = jnp.where(region == index + 1, table_ref[index : index + 1, :], value)
+    return value
+
+
 def unpack_kernel(source_hbm, potential_hbm, map_hbm, region_hbm, table_hbm, r_ref, ionic_ref, label_ref, coarse_ref,
-                  own_ref, beside_ref,
-                  rows_ref, turned_ref, source_ref, potential_ref, map_ref, region_ref, table_ref, sems):
+                  own_ref, table_ref,
+                  rows_ref, turned_ref, source_ref, potential_ref, map_ref, region_ref, values_ref, sems):
     copies = [
         pltpu.make_async_copy(away, here, sems.at[index])
         for index, (away, here) in enumerate(
@@ -98,7 +103,7 @@
                 (potential_hbm, potential_ref),
                 (map_hbm, map_ref),
                 (region_hbm, region_ref),
-                (table_hbm, table_ref),
+                (table_hbm, values_ref),
             )
         )
     ]
@@ -107,14 +112,10 @@
     rows_ref[...] = jnp.zeros_like(rows_ref)
     for copy in copies:
         copy.wait()
+    for index in range(4):
+        table_ref[index : index + 1, :] = jnp.full((1, 128), values_ref[index])
     for i in range(2):
-        region = region_ref[i]
-        sigma = jnp.zeros(region.shape, F32)
-        for index in range(4):
-            sigma = jnp.where(region == index, table_ref[index], sigma)
-        own_ref[2 * i : 2 * i + 2, :] = sigma
-    beside_ref[0:1, :] = own_ref[1:2, :]
-    beside_ref[1:2, :] = own_ref[3:4, :]
+        own_ref[2 * i : 2 * i + 2, :] = conductance(region_ref[i] + 1, table_ref)
     for y in range(6):
         for x in range(6):
             row = y * 6 + x
@@ -148,12 +149,13 @@
     far_ref[...] = jnp.where(even, down_ref[...], up_ref[...])
 
 
-def diagonal_kernel(place_ref, own_ref, beside_ref, below_ref, matrix_ref, r_ref, ionic_ref, label_ref, coarse_ref,
+def diagonal_kernel(place_ref, corner_ref, below_ref, beside_ref, own_ref, table_ref, matrix_ref, r_ref, ionic_ref, label_ref, coarse_ref,
                     sigma_ref, diagonal_ref, scaled_ref, message_ref, near_ref, far_ref,
-                    total_ref, up_ref, down_ref, copies_ref, sem):
-    sigma_ref[0:3, :] = below_ref[...]
+                    total_ref, up_ref, down_ref):
+    sigma_ref[0:1, :] = conductance(corner_ref[...], table_ref)
+    sigma_ref[1:3, :] = conductance(below_ref[...], table_ref)
     for i in range(2):
-        sigma_ref[3 + 3 * i : 4 + 3 * i, :] = beside_ref[i : i + 1, :]
+        sigma_ref[3 + 3 * i : 4 + 3 * i, :] = conductance(beside_ref[i : i + 1, :], table_ref)
         sigma_ref[4 + 3 * i : 6 + 3 * i, :] = own_ref[2 * i : 2 * i + 2, :]
     square = (64, 64)
     eye = lax.broadcasted_iota(jnp.int32, square, 0) == lax.broadcasted_iota(jnp.int32, square, 1)
@@ -165,12 +167,9 @@
     coarse_diag = SHARE * restrict(diagonal, labels)
     even = lanes((8, 128)) % 2 == 0
     message = jnp.where(even, coarse_ref[...], coarse_diag)
-    copies_ref[...] = jnp.broadcast_to(message[None], copies_ref.shape)
-    sending = pltpu.make_async_copy(copies_ref, message_ref, sem)
-    sending.start()
+    message_ref[...] = jnp.broadcast_to(message[None], message_ref.shape)
     scaled_ref[...] = r_ref[...] / diagonal
     send_slab(place_ref[1] == 0, (scaled_ref, label_ref), near_ref, far_ref, up_ref, down_ref)
-    sending.wait()
 
 
 def along(values):
@@ -243,7 +242,7 @@
 
 def first_solve_kernel(place_ref, gathered_ref, scaled_ref, label_ref, left_ref, right_ref,
                        wide_ref, z_ref, near_ref, far_ref, scale_ref, wide_label_ref, up_ref, down_ref):
-    low, high = arrived(place_ref[1] == 0, right_ref, left_ref)
+    low, high = arrived(place_ref[1] == 0, left_ref, right_ref)
     rows, valid = around(place_ref, gathered_ref.shape[0])
     tiles = jnp.concatenate([gathered_ref[pl.ds(row, 1)] for row in rows], 0)
     sums = jnp.sum(gathered_ref[...], axis=0)
@@ -261,7 +260,7 @@
 
 def next_solve_kernel(place_ref, gathered_ref, scaled_ref, wide_label_ref, left_ref, right_ref, scale_ref,
                       wide_ref, w_ref, near_ref, far_ref, up_ref, down_ref):
-    low, high = arrived(place_ref[1] == 0, right_ref, left_ref)
+    low, high = arrived(place_ref[1] == 0, left_ref, right_ref)
     rows, valid = around(place_ref, gathered_ref.shape[0])
     tiles = jnp.concatenate([gathered_ref[pl.ds(row, 1)] for row in rows], 0)
     sums = jnp.sum(gathered_ref[...], axis=0)
@@ -308,15 +307,12 @@
 
 
 def first_image_kernel(place_ref, wide_ref, z_ref, far_ref, near_ref, sigma_ref, matrix_ref, ionic_ref, diagonal_ref, label_ref,
-                       q_ref, scaled_ref, message_ref, left_ref, right_ref, up_ref, down_ref, copies_ref, sem, *scratch):
+                       q_ref, scaled_ref, message_ref, left_ref, right_ref, up_ref, down_ref, *scratch):
     image = operate(place_ref, wide_ref, z_ref, near_ref, far_ref, sigma_ref, matrix_ref, ionic_ref, *scratch)
     q_ref[...] = image
-    copies_ref[...] = jnp.broadcast_to(restrict(image, label_ref[...])[None], copies_ref.shape)
-    sending = pltpu.make_async_copy(copies_ref, message_ref, sem)
-    sending.start()
+    message_ref[...] = jnp.broadcast_to(restrict(image, label_ref[...])[None], message_ref.shape)
     scaled_ref[...] = image / diagonal_ref[...]
     send_slab(place_ref[1] == 0, (scaled_ref,), left_ref, right_ref, up_ref, down_ref)
-    sending.wait()
 
 
 def next_image_kernel(place_ref, wide_ref, w_ref, far_ref, near_ref, sigma_ref, matrix_ref, ionic_ref,
@@ -379,27 +375,32 @@
 
     field, wide = (18, 8, 128), (18, 16, 128)
     space = [(40, 16, 128), (64, 1152), (64, 1152), field]
-    r, ionic, labels, coarse, own, beside = call(
-        unpack_kernel, [field] * 3 + [(8, 128), (4, 128), (2, 128)],
+    regions = region_labels + 1
+    pairs = [
+        (here * n_cross + beside, (here + 1) * n_cross + beside + 1)
+        for here in range(n_slab - 1)
+        for beside in range(n_cross - 1)
+    ]
+    corner = lax.ppermute(regions[1, 1:2], ("slab", "cross"), pairs)
+    below = shifted(regions[1], "slab", 1)
+    beside = shifted(regions[:, 1], "cross", 1)
+    r, ionic, labels, coarse, own, table = call(
+        unpack_kernel, [field] * 3 + [(8, 128), (4, 128), (4, 128)],
         [(128, 384), (384, 128), (6, 6, 384), (6, 6, 384), pltpu.VMEM((6, 6, 384), jnp.int32),
          pltpu.VMEM((2, 2, 128), jnp.int32), pltpu.SMEM((4,), F32), pltpu.SemaphoreType.DMA((5,))],
         adjoint_source, potential, restriction_map, region_labels, conductivity, away=(0, 1, 2, 3, 4),
     )
-    beside = shifted(beside, "cross", 1)
-    below = shifted(jnp.concatenate([beside[1:2], own[2:4]], 0), "slab", 1)
-    copies = [(n_slab, 8, 128), pltpu.SemaphoreType.DMA]
     sigma, diagonal, scaled, message, near, far = call(
         diagonal_kernel, [(9, 128), field, field, (n_slab, 8, 128), (112, 128), (112, 128)],
-        [field, (112, 128), (112, 128), *copies],
-        place, own, beside, below, element_matrix, r, ionic, labels, coarse, smem=(0,), sent=(3,),
+        [field, (112, 128), (112, 128)],
+        place, corner, below, beside, own, table, element_matrix, r, ionic, labels, coarse, smem=(0,),
     )
 
     def exchange(near, far, axis):
         count = lax.axis_size(axis)
         far_pairs = [(c, c + 1) for c in range(1, count - 1, 2)]
         far_pairs += [(above, c) for c, above in far_pairs]
-        far = lax.ppermute(far, axis, far_pairs)
-        return far, lax.ppermute(near, axis, [(c, c ^ 1) for c in range(count)])
+        return lax.ppermute(near, axis, [(c, c ^ 1) for c in range(count)]), lax.ppermute(far, axis, far_pairs)
 
     faces = [(96, 128), (96, 128)]
     wide_z, z, near, far, scale, wide_labels = call(
@@ -408,9 +409,9 @@
     )
     q, scaled, message, near, far = call(
         first_image_kernel, [field, field, (n_slab, 8, 128), (56, 128), (56, 128)],
-        [(56, 128), (56, 128), *copies, *space],
-        place, wide_z, z, *exchange(near, far, "cross"), sigma, element_matrix, ionic, diagonal, labels,
-        smem=(0,), sent=(2,),
+        [(56, 128), (56, 128), *space],
+        place, wide_z, z, *exchange(near, far, "cross")[::-1], sigma, element_matrix, ionic, diagonal, labels,
+        smem=(0,),
     )
     wide_w, w, near, far = call(
         next_solve_kernel, [wide, field, *faces], faces,
@@ -418,7 +419,7 @@
     )
     t, message = call(
         next_image_kernel, [field, (n_slab // 2, 1, 128)], space,
-        place, wide_w, w, *exchange(near, far, "cross"), sigma, element_matrix, ionic, r, z, q, smem=(0,),
+        place, wide_w, w, *exchange(near, far, "cross")[::-1], sigma, element_matrix, ionic, r, z, q, smem=(0,),
     )
     parts = lax.all_to_all(message, "slab", 0, 0, axis_index_groups=planes, tiled=True)
     parts = jnp.broadcast_to(jnp.sum(parts, 0)[None], (2 * n_cross, 1, 128))

time: 117 us -> 120 us (1.026)
  waiting for transfers between devices: 19 us -> 15.5 us
  blocking collectives: 27.6 us -> 30.6 us
  starting transfers between devices: 60.3 us -> 62.1 us
    ppermute x2, waiting for transfers between devices: 3.76 us -> 0.01 us  [shifted(): return lax.ppermute(value, axis, pairs)]
    all_to_all x1, blocking collectives: 13 us -> 16.1 us  [body(): lax.all_to_all(message, 'slab', 0, 0, axis_index_groups=planes, tiled=True)]
    ppermute x8 -> x9, starting transfers between devices: 32.4 us -> 33.8 us  [the longest x4 17.5 us: exchange(): lax.ppermute(far, axis, far_pairs)]
    all_to_all x2, starting transfers between devices: 21 us -> 22.3 us  [gather(): return lax.all_to_all(copies, 'slab', 0, 0, tiled=True)]
    ppermute x8 -> x9, waiting for transfers between devices: 6.27 us -> 5.94 us  [the longest x4 5.49 us: exchange(): lax.ppermute(near, axis, [(c, c ^ 1) for c in range(count)])]
  transfers between devices with their start and end apart: 12 -> 13, of which waited for: 8 -> 8; matrix products, arithmetic and copies ran while one was open for 0% -> 0% of each run, Pallas kernels for 0% -> 1%
where the time goes in v4:
time: 120 us; the launch traced here: 119 us
  starting transfers between devices  62.1 us (52%)
  blocking collectives  30.6 us (26%)
  waiting for transfers between devices  15.5 us (13%)
  Pallas kernels  9.03 us (8%)
    all_to_all x2, starting transfers between devices, gather(): return lax.all_to_all(copies, 'slab', 0, 0, tiled=True)  22.3 us
    ppermute x4, starting transfers between devices, exchange(): lax.ppermute(far, axis, far_pairs)  17.5 us
    all_to_all x1, blocking collectives, body(): lax.all_to_all(message, 'slab', 0, 0, axis_index_groups=planes, tiled=True)  16.1 us
    all_to_all x1, blocking collectives, body(): lax.all_to_all(parts, ('slab', 'cross'), 0, 0, axis_index_groups=columns,...  14.5 us
    ppermute x4, starting transfers between devices, exchange(): lax.ppermute(near, axis, [(c, c ^ 1) for c in range(count)])  9.68 us
    all_to_all x2, waiting for transfers between devices, gather(): return lax.all_to_all(copies, 'slab', 0, 0, tiled=True)  9.6 us
    pallas_call x7, Pallas kernels, call(): pl.pallas_call(kernel, out_shape=[jax.ShapeDtypeStruct(shape, F32) for sh...  9.03 us
    ppermute x1, starting transfers between devices, body(): corner = lax.ppermute(regions[1, 1:2], ('slab', 'cross'), pairs)  6.6 us
  transfers between devices with their start and end apart: 13, of which 8 were waited for; matrix products, arithmetic and copies ran while one was open for 0% of the time, Pallas kernels for 1%

profile of v4, /device:TPU:1, one launch (start us, length us, event | category | flops | bytes accessed | tf_op | source)
XLA Modules:
  0.0 119.0 jit_solution(7439907499237728856)
XLA Ops:
  0.6 0.7 copy_add_fusion
  1.3 6.6 %collective-permute-start = (s32[1,128]{1,0:T(1,128)S(1)}, s32[1,128]{1,0:T(1,128)S(1)}, u32[]{:S(2)}, u32[]{:S(2)}) collective-permute-start(s32[1,128]{1,0:T(1,128)S(1)} %slice_bitcast_fusion.1), channel_id=1, source_target_pairs={{0,9},{1,10},{2,11},{3,12},{4,13},{5,14},{6,15},{8,17},{9,18},{10,... | collective-permute-start | bytes 1544 | tf_op jit(solution)/shard_map/ppermute | solution.py:384
  7.9 3.0 %collective-permute-start.1 = (s32[2,128]{1,0:T(2,128)S(1)}, s32[2,128]{1,0:T(2,128)S(1)}, u32[]{:S(2)}, u32[]{:S(2)}) collective-permute-start(s32[2,128]{1,0:T(2,128)S(1)} %bitcast.8), channel_id=1, source_target_pairs={{0,8},{8,16},{16,24},{24,32},{32,40},{40,48},{48,56},{56,64},{64,7... | collective-permute-start | bytes 3080 | tf_op jit(solution)/shard_map/ppermute | solution.py:371
  11.0 3.1 %collective-permute-start.2 = (s32[2,128]{1,0:T(2,128)S(1)}, s32[2,128]{1,0:T(2,128)S(1)}, u32[]{:S(2)}, u32[]{:S(2)}) collective-permute-start(s32[2,128]{1,0:T(2,128)S(1)} %slice_bitcast_fusion), channel_id=1, source_target_pairs={{0,1},{1,2},{2,3},{3,4},{4,5},{5,6},{6,7},{8,9},{9,10},{10,11},{11... | collective-permute-start | bytes 3080 | tf_op jit(solution)/shard_map/ppermute | solution.py:371
  14.1 0.1 pad_add_fusion.place_ref
  14.1 0.0 copy-start
  14.1 1.4 %shard_map.77 = (f32[18,8,128]{2,1,0:T(8,128)S(1)}, f32[18,8,128]{2,1,0:T(8,128)S(1)}, f32[18,8,128]{2,1,0:T(8,128)S(1)}, f32[8,128]{1,0:T(8,128)S(1)}, f32[4,128]{1,0:T(4,128)S(1)}, /*index=5*/f32[4,128]{1,0:T(4,128)S(1)}) custom-call(f32[6,6,384]{2,1,0:T(8,128)} %source_hbm.1, f32[6,6,384]{2,1,0:T(8,128)} %potential_hbm.1, s32[6,6,384]{2,1,0:T(8,128)} %map_hbm.1, ...), custom_call_target="tpu_custom_call" | custom-call | tf_op jit(solution)/shard_map/pallas_call | solution.py:36
  15.6 0.0 collective-permute-done.corner_ref
  15.6 0.0 collective-permute-done.1.below_ref
  15.6 0.0 collective-permute-done.2.beside_ref
  15.6 0.0 copy-done
  15.6 1.6 %shard_map.78 = (f32[9,128]{1,0:T(8,128)S(1)}, f32[18,8,128]{2,1,0:T(8,128)S(1)}, f32[18,8,128]{2,1,0:T(8,128)S(1)}, f32[64,8,128]{2,1,0:T(8,128)}, f32[112,128]{1,0:T(8,128)S(1)}, /*index=5*/f32[112,128]{1,0:T(8,128)S(1)}) custom-call(s32[3]{0:T(128)S(1)} %pad_add_fusion.place_ref, s32[1,128]{1,0:T(1,128)S(1)} %collective-permute-done.corner_ref, ...), custom_call_target="tpu_custom_call" | custom-call | tf_op jit(solution)/shard_map/pallas_call | solution.py:36
  17.3 13.6 %all-to-all-start = ((f32[64,8,128]{2,1,0:T(8,128)}), f32[64,8,128]{2,1,0:T(8,128)S(1)}, u32[]{:S(2)}, u32[]{:S(2)}) async-start(f32[64,8,128]{2,1,0:T(8,128)} %get-tuple-element.37), calls=%async_computation | async-start | bytes 524288 | tf_op jit(solution)/shard_map/all_to_all | solution.py:374
  30.9 2.9 %collective-permute-start.3 = (f32[112,128]{1,0:T(8,128)S(1)}, f32[112,128]{1,0:T(8,128)S(1)}, u32[]{:S(2)}, u32[]{:S(2)}) collective-permute-start(f32[112,128]{1,0:T(8,128)S(1)} %get-tuple-element.39), channel_id=1, source_target_pairs={{0,8},{8,0},{16,24},{24,16},{32,40},{40,32},{48,56},{56,48},{64,72... | collective-permute-start | bytes 172040 | tf_op jit(solution)/shard_map/ppermute | solution.py:403
  33.8 0.7 collective-permute-start.4
  34.5 1.9 %collective-permute-done.3.left_ref = f32[112,128]{1,0:T(8,128)S(1)} collective-permute-done((f32[112,128]{1,0:T(8,128)S(1)}, f32[112,128]{1,0:T(8,128)S(1)}, u32[]{:S(2)}, u32[]{:S(2)}) %collective-permute-start.3) | collective-permute-done | bytes 57376 | tf_op jit(solution)/shard_map/ppermute | solution.py:403
  36.4 0.0 collective-permute-done.4.right_ref
  36.4 4.6 %all-to-all-done.gathered_ref = f32[64,8,128]{2,1,0:T(8,128)S(1)} async-done(((f32[64,8,128]{2,1,0:T(8,128)}), f32[64,8,128]{2,1,0:T(8,128)S(1)}, u32[]{:S(2)}, u32[]{:S(2)}) %all-to-all-start) | async-done | bytes 262176 | tf_op jit(solution)/shard_map/all_to_all | solution.py:374
  41.1 1.0 shard_map.79
  42.1 7.7 %collective-permute-start.5 = (f32[96,128]{1,0:T(8,128)S(1)}, f32[96,128]{1,0:T(8,128)S(1)}, u32[]{:S(2)}, u32[]{:S(2)}) collective-permute-start(f32[96,128]{1,0:T(8,128)S(1)} %get-tuple-element.43), channel_id=1, source_target_pairs={{1,2},{3,4},{5,6},{2,1},{4,3},{6,5},{9,10},{11,12},{13,14},{10,9},... | collective-permute-start | bytes 147464 | tf_op jit(solution)/shard_map/ppermute | solution.py:403
  49.8 1.9 %collective-permute-start.6 = (f32[96,128]{1,0:T(8,128)S(1)}, f32[96,128]{1,0:T(8,128)S(1)}, u32[]{:S(2)}, u32[]{:S(2)}) collective-permute-start(f32[96,128]{1,0:T(8,128)S(1)} %get-tuple-element.44), channel_id=1, source_target_pairs={{0,1},{1,0},{2,3},{3,2},{4,5},{5,4},{6,7},{7,6},{8,9},{9,8},{10,11... | collective-permute-start | bytes 147464 | tf_op jit(solution)/shard_map/ppermute | solution.py:403
  51.7 0.4 collective-permute-done.5.far_ref
  52.1 0.8 collective-permute-done.6.near_ref
  52.9 1.8 %shard_map.80 = (f32[18,8,128]{2,1,0:T(8,128)S(1)}, f32[18,8,128]{2,1,0:T(8,128)S(1)}, f32[64,8,128]{2,1,0:T(8,128)}, f32[56,128]{1,0:T(8,128)S(1)}, f32[56,128]{1,0:T(8,128)S(1)}) custom-call(s32[3]{0:T(128)S(1)} %pad_add_fusion.place_ref, f32[18,16,128]{2,1,0:T(8,128)S(1)} %get-tuple-element.41.wide_ref, f32[18,8,128]{2,1,0:T(8,128)S(1)} %get-tuple-element.42.z_ref, ...), custom_call_target="tpu_custom_call" | custom-call | tf_op jit(solution)/shard_map/pallas_call | solution.py:36
  54.7 8.6 %all-to-all-start.1 = ((f32[64,8,128]{2,1,0:T(8,128)}), f32[64,8,128]{2,1,0:T(8,128)S(1)}, u32[]{:S(2)}, u32[]{:S(2)}) async-start(f32[64,8,128]{2,1,0:T(8,128)} %get-tuple-element.47), calls=%async_computation.1 | async-start | bytes 524288 | tf_op jit(solution)/shard_map/all_to_all | solution.py:374
  63.4 2.9 %collective-permute-start.7 = (f32[56,128]{1,0:T(8,128)S(1)}, f32[56,128]{1,0:T(8,128)S(1)}, u32[]{:S(2)}, u32[]{:S(2)}) collective-permute-start(f32[56,128]{1,0:T(8,128)S(1)} %get-tuple-element.50), channel_id=1, source_target_pairs={{0,8},{8,0},{16,24},{24,16},{32,40},{40,32},{48,56},{56,48},{64,72... | collective-permute-start | bytes 86024 | tf_op jit(solution)/shard_map/ppermute | solution.py:403
  66.3 0.7 collective-permute-start.8
  67.0 1.6 %collective-permute-done.7.left_ref = f32[56,128]{1,0:T(8,128)S(1)} collective-permute-done((f32[56,128]{1,0:T(8,128)S(1)}, f32[56,128]{1,0:T(8,128)S(1)}, u32[]{:S(2)}, u32[]{:S(2)}) %collective-permute-start.7) | collective-permute-done | bytes 28704 | tf_op jit(solution)/shard_map/ppermute | solution.py:403
  68.6 0.0 collective-permute-done.8.right_ref
  68.6 5.0 %all-to-all-done.1.gathered_ref = f32[64,8,128]{2,1,0:T(8,128)S(1)} async-done(((f32[64,8,128]{2,1,0:T(8,128)}), f32[64,8,128]{2,1,0:T(8,128)S(1)}, u32[]{:S(2)}, u32[]{:S(2)}) %all-to-all-start.1) | async-done | bytes 262176 | tf_op jit(solution)/shard_map/all_to_all | solution.py:374
  73.6 0.9 shard_map.81
  74.5 8.5 %collective-permute-start.9 = (f32[96,128]{1,0:T(8,128)S(1)}, f32[96,128]{1,0:T(8,128)S(1)}, u32[]{:S(2)}, u32[]{:S(2)}) collective-permute-start(f32[96,128]{1,0:T(8,128)S(1)} %get-tuple-element.55), channel_id=1, source_target_pairs={{1,2},{3,4},{5,6},{2,1},{4,3},{6,5},{9,10},{11,12},{13,14},{10,9},... | collective-permute-start | bytes 147464 | tf_op jit(solution)/shard_map/ppermute | solution.py:403
  83.0 1.9 %collective-permute-start.10 = (f32[96,128]{1,0:T(8,128)S(1)}, f32[96,128]{1,0:T(8,128)S(1)}, u32[]{:S(2)}, u32[]{:S(2)}) collective-permute-start(f32[96,128]{1,0:T(8,128)S(1)} %get-tuple-element.56), channel_id=1, source_target_pairs={{0,1},{1,0},{2,3},{3,2},{4,5},{5,4},{6,7},{7,6},{8,9},{9,8},{10,11... | collective-permute-start | bytes 147464 | tf_op jit(solution)/shard_map/ppermute | solution.py:403
  84.9 0.1 collective-permute-done.9.far_ref
  85.0 1.1 collective-permute-done.10.near_ref
  86.1 1.1 shard_map.82
  87.2 16.1 %all_to_all.20 = f32[32,1,128]{2,1,0:T(1,128)S(1)} all-to-all(f32[32,1,128]{2,1,0:T(1,128)S(1)} %get-tuple-element.58), channel_id=1, replica_groups={{0,16,32,48,64,80,96,112,128,144,160,176,192,208,224,240,256,272,288,30..., dimensions={0} | all-to-all | bytes 32768 | tf_op jit(solution)/shard_map/all_to_all | solution.py:424
  103.3 0.1 reduce_sum.9
  103.4 14.5 %all_to_all.21.dots_ref = f32[16,1,128]{2,1,0:T(1,128)S(1)} all-to-all(f32[16,1,128]{2,1,0:T(1,128)S(1)} %broadcast_in_dim.2), channel_id=1, replica_groups={{0,1,2,3,4,5,6,7,8,9,10,11,12,13,14,15},{16,17,18,19,20,21,22,23,24,25,..., dimensions={0} | all-to-all | bytes 16384 | tf_op jit(solution)/shard_map/all_to_all | solution.py:426
  117.9 1.1 shard_map.83
  (4 shorter events, 0.0 us)
Async XLA Ops:
  1.3 14.3 %collective-permute-start = (s32[1,128]{1,0:T(1,128)S(1)}, s32[1,128]{1,0:T(1,128)S(1)}, u32[]{:S(2)}, u32[]{:S(2)}) collective-permute-start(s32[1,128]{1,0:T(1,128)S(1)} %slice_bitcast_fusion.1), channel_id=1, source_target_pairs={{0,9},{1,10},{2,11},{3,12},{4,13},{5,14},{6,15},{8,17},{9,18},{10,... | collective-permute-start | bytes 1544 | tf_op jit(solution)/shard_map/ppermute | solution.py:384
  7.9 7.7 %collective-permute-start.1 = (s32[2,128]{1,0:T(2,128)S(1)}, s32[2,128]{1,0:T(2,128)S(1)}, u32[]{:S(2)}, u32[]{:S(2)}) collective-permute-start(s32[2,128]{1,0:T(2,128)S(1)} %bitcast.8), channel_id=1, source_target_pairs={{0,8},{8,16},{16,24},{24,32},{32,40},{40,48},{48,56},{56,64},{64,7... | collective-permute-start | bytes 3080 | tf_op jit(solution)/shard_map/ppermute | solution.py:371
  11.0 4.7 %collective-permute-start.2 = (s32[2,128]{1,0:T(2,128)S(1)}, s32[2,128]{1,0:T(2,128)S(1)}, u32[]{:S(2)}, u32[]{:S(2)}) collective-permute-start(s32[2,128]{1,0:T(2,128)S(1)} %slice_bitcast_fusion), channel_id=1, source_target_pairs={{0,1},{1,2},{2,3},{3,4},{4,5},{5,6},{6,7},{8,9},{9,10},{10,11},{11... | collective-permute-start | bytes 3080 | tf_op jit(solution)/shard_map/ppermute | solution.py:371
  14.1 1.5 %copy-start = (f32[64,64]{1,0:T(8,128)S(1)}, f32[64,64]{1,0:T(8,128)}, u32[]{:S(2)}) copy-start(f32[64,64]{1,0:T(8,128)} %matrix_ref.5) | copy-start | bytes 49156
  17.3 23.8 %all-to-all-start = ((f32[64,8,128]{2,1,0:T(8,128)}), f32[64,8,128]{2,1,0:T(8,128)S(1)}, u32[]{:S(2)}, u32[]{:S(2)}) async-start(f32[64,8,128]{2,1,0:T(8,128)} %get-tuple-element.37), calls=%async_computation | async-start | bytes 524288 | tf_op jit(solution)/shard_map/all_to_all | solution.py:374
  30.9 5.5 %collective-permute-start.3 = (f32[112,128]{1,0:T(8,128)S(1)}, f32[112,128]{1,0:T(8,128)S(1)}, u32[]{:S(2)}, u32[]{:S(2)}) collective-permute-start(f32[112,128]{1,0:T(8,128)S(1)} %get-tuple-element.39), channel_id=1, source_target_pairs={{0,8},{8,0},{16,24},{24,16},{32,40},{40,32},{48,56},{56,48},{64,72... | collective-permute-start | bytes 172040 | tf_op jit(solution)/shard_map/ppermute | solution.py:403
  33.8 2.6 %collective-permute-start.4 = (f32[112,128]{1,0:T(8,128)S(1)}, f32[112,128]{1,0:T(8,128)S(1)}, u32[]{:S(2)}, u32[]{:S(2)}) collective-permute-start(f32[112,128]{1,0:T(8,128)S(1)} %get-tuple-element.40), channel_id=1, source_target_pairs={{8,16},{24,32},{40,48},{56,64},{72,80},{88,96},{104,112},{120,128}... | collective-permute-start | bytes 172040 | tf_op jit(solution)/shard_map/ppermute | solution.py:403
  42.1 10.0 %collective-permute-start.5 = (f32[96,128]{1,0:T(8,128)S(1)}, f32[96,128]{1,0:T(8,128)S(1)}, u32[]{:S(2)}, u32[]{:S(2)}) collective-permute-start(f32[96,128]{1,0:T(8,128)S(1)} %get-tuple-element.43), channel_id=1, source_target_pairs={{1,2},{3,4},{5,6},{2,1},{4,3},{6,5},{9,10},{11,12},{13,14},{10,9},... | collective-permute-start | bytes 147464 | tf_op jit(solution)/shard_map/ppermute | solution.py:403
  49.8 3.1 %collective-permute-start.6 = (f32[96,128]{1,0:T(8,128)S(1)}, f32[96,128]{1,0:T(8,128)S(1)}, u32[]{:S(2)}, u32[]{:S(2)}) collective-permute-start(f32[96,128]{1,0:T(8,128)S(1)} %get-tuple-element.44), channel_id=1, source_target_pairs={{0,1},{1,0},{2,3},{3,2},{4,5},{5,4},{6,7},{7,6},{8,9},{9,8},{10,11... | collective-permute-start | bytes 147464 | tf_op jit(solution)/shard_map/ppermute | solution.py:403
  54.7 18.8 %all-to-all-start.1 = ((f32[64,8,128]{2,1,0:T(8,128)}), f32[64,8,128]{2,1,0:T(8,128)S(1)}, u32[]{:S(2)}, u32[]{:S(2)}) async-start(f32[64,8,128]{2,1,0:T(8,128)} %get-tuple-element.47), calls=%async_computation.1 | async-start | bytes 524288 | tf_op jit(solution)/shard_map/all_to_all | solution.py:374
  63.4 5.2 %collective-permute-start.7 = (f32[56,128]{1,0:T(8,128)S(1)}, f32[56,128]{1,0:T(8,128)S(1)}, u32[]{:S(2)}, u32[]{:S(2)}) collective-permute-start(f32[56,128]{1,0:T(8,128)S(1)} %get-tuple-element.50), channel_id=1, source_target_pairs={{0,8},{8,0},{16,24},{24,16},{32,40},{40,32},{48,56},{56,48},{64,72... | collective-permute-start | bytes 86024 | tf_op jit(solution)/shard_map/ppermute | solution.py:403
  66.3 2.3 %collective-permute-start.8 = (f32[56,128]{1,0:T(8,128)S(1)}, f32[56,128]{1,0:T(8,128)S(1)}, u32[]{:S(2)}, u32[]{:S(2)}) collective-permute-start(f32[56,128]{1,0:T(8,128)S(1)} %get-tuple-element.51), channel_id=1, source_target_pairs={{8,16},{24,32},{40,48},{56,64},{72,80},{88,96},{104,112},{120,128}... | collective-permute-start | bytes 86024 | tf_op jit(solution)/shard_map/ppermute | solution.py:403
  74.5 10.5 %collective-permute-start.9 = (f32[96,128]{1,0:T(8,128)S(1)}, f32[96,128]{1,0:T(8,128)S(1)}, u32[]{:S(2)}, u32[]{:S(2)}) collective-permute-start(f32[96,128]{1,0:T(8,128)S(1)} %get-tuple-element.55), channel_id=1, source_target_pairs={{1,2},{3,4},{5,6},{2,1},{4,3},{6,5},{9,10},{11,12},{13,14},{10,9},... | collective-permute-start | bytes 147464 | tf_op jit(solution)/shard_map/ppermute | solution.py:403
  83.0 3.1 %collective-permute-start.10 = (f32[96,128]{1,0:T(8,128)S(1)}, f32[96,128]{1,0:T(8,128)S(1)}, u32[]{:S(2)}, u32[]{:S(2)}) collective-permute-start(f32[96,128]{1,0:T(8,128)S(1)} %get-tuple-element.56), channel_id=1, source_target_pairs={{0,1},{1,0},{2,3},{3,2},{4,5},{5,4},{6,7},{7,6},{8,9},{9,8},{10,11... | collective-permute-start | bytes 147464 | tf_op jit(solution)/shard_map/ppermute | solution.py:403

commit v5 on v4

--- a/solution.py
+++ b/solution.py
@@ -137,21 +137,29 @@
     coarse_ref[...] = restrict(r_ref[...], label_ref[...])
 
 
-def send_slab(even, fields, near_ref, far_ref, up_ref, down_ref):
-    up_ref[...] = jnp.zeros_like(up_ref)
-    down_ref[...] = jnp.zeros_like(down_ref)
+def send(odd, both_ref, near_ref, far_ref):
+    near_ref[...] = both_ref[odd]
+    far_ref[...] = both_ref[1 - odd]
+
+
+def receive(odd, near_ref, far_ref, both_ref):
+    both_ref[odd] = near_ref[...]
+    both_ref[1 - odd] = far_ref[...]
+
+
+def send_slab(odd, fields, near_ref, far_ref, both_ref):
+    both_ref[...] = jnp.zeros_like(both_ref)
     for index, field_ref in enumerate(fields):
         for n in range(18):
             row = 56 * index + 3 * n
-            up_ref[row : row + 3, :] = field_ref[n, 3:6, :]
-            down_ref[56 * index + n : 56 * index + n + 1, :] = field_ref[n, 0:1, :]
-    near_ref[...] = jnp.where(even, up_ref[...], down_ref[...])
-    far_ref[...] = jnp.where(even, down_ref[...], up_ref[...])
+            both_ref[0, row : row + 3, :] = field_ref[n, 3:6, :]
+            both_ref[1, 56 * index + n : 56 * index + n + 1, :] = field_ref[n, 0:1, :]
+    send(odd, both_ref, near_ref, far_ref)
 
 
 def diagonal_kernel(place_ref, corner_ref, below_ref, beside_ref, own_ref, table_ref, matrix_ref, r_ref, ionic_ref, label_ref, coarse_ref,
                     sigma_ref, diagonal_ref, scaled_ref, message_ref, near_ref, far_ref,
-                    total_ref, up_ref, down_ref):
+                    total_ref, both_ref):
     sigma_ref[0:1, :] = conductance(corner_ref[...], table_ref)
     sigma_ref[1:3, :] = conductance(below_ref[...], table_ref)
     for i in range(2):
@@ -169,7 +177,7 @@
     message = jnp.where(even, coarse_ref[...], coarse_diag)
     message_ref[...] = jnp.broadcast_to(message[None], message_ref.shape)
     scaled_ref[...] = r_ref[...] / diagonal
-    send_slab(place_ref[1] == 0, (scaled_ref, label_ref), near_ref, far_ref, up_ref, down_ref)
+    send_slab(place_ref[1], (scaled_ref, label_ref), near_ref, far_ref, both_ref)
 
 
 def along(values):
@@ -213,36 +221,30 @@
     return jnp.where(even, pltpu.roll(tiles, 127, tiles.ndim - 1), tiles)
 
 
-def widen(field_ref, low, high, start, wide_ref):
+def widen(field_ref, both_ref, start, wide_ref):
     wide_ref[...] = jnp.zeros_like(wide_ref)
     for n in range(18):
-        wide_ref[n, 0:3, :] = low[start + 3 * n : start + 3 * n + 3]
+        wide_ref[n, 0:3, :] = both_ref[1, start + 3 * n : start + 3 * n + 3, :]
         wide_ref[n, 3:9, :] = field_ref[n, 0:6, :]
-        wide_ref[n, 9:10, :] = high[start + n : start + n + 1]
-
-
-def send_cross(even, wide_ref, own_ref, near_ref, far_ref, up_ref, down_ref):
+        wide_ref[n, 9:10, :] = both_ref[0, start + n : start + n + 1, :]
+
+
+def send_cross(odd, wide_ref, own_ref, near_ref, far_ref, both_ref):
     own_ref[...] = jnp.zeros_like(own_ref)
     for n in range(18):
         own_ref[n, 0:6, :] = wide_ref[n, 3:9, :]
-    up_ref[...] = jnp.zeros_like(up_ref)
-    down_ref[...] = jnp.zeros_like(down_ref)
+    both_ref[...] = jnp.zeros_like(both_ref)
     for c in range(3):
         for y in range(3):
             row = (3 * c + y) * 10
-            up_ref[row : row + 10, :] = wide_ref[6 * c + 3 + y, 0:10, :]
-        down_ref[10 * c : 10 * c + 10, :] = wide_ref[6 * c, 0:10, :]
-    near_ref[...] = jnp.where(even, up_ref[...], down_ref[...])
-    far_ref[...] = jnp.where(even, down_ref[...], up_ref[...])
-
-
-def arrived(even, near_ref, far_ref):
-    return jnp.where(even, far_ref[...], near_ref[...]), jnp.where(even, near_ref[...], far_ref[...])
+            both_ref[0, row : row + 10, :] = wide_ref[6 * c + 3 + y, 0:10, :]
+        both_ref[1, 10 * c : 10 * c + 10, :] = wide_ref[6 * c, 0:10, :]
+    send(odd, both_ref, near_ref, far_ref)
 
 
 def first_solve_kernel(place_ref, gathered_ref, scaled_ref, label_ref, left_ref, right_ref,
-                       wide_ref, z_ref, near_ref, far_ref, scale_ref, wide_label_ref, up_ref, down_ref):
-    low, high = arrived(place_ref[1] == 0, left_ref, right_ref)
+                       wide_ref, z_ref, near_ref, far_ref, scale_ref, wide_label_ref, slab_ref, cross_ref):
+    receive(place_ref[1], right_ref, left_ref, slab_ref)
     rows, valid = around(place_ref, gathered_ref.shape[0])
     tiles = jnp.concatenate([gathered_ref[pl.ds(row, 1)] for row in rows], 0)
     sums = jnp.sum(gathered_ref[...], axis=0)
@@ -252,37 +254,37 @@
     scale_ref[2 * NEAR + 1] = share
     level = smooth(DAMPING * even_part(tiles) * inverse, valid)
     coarse = level * inverse[REACH : REACH + 3] + (even_part(sums) * share)[None]
-    widen(label_ref, low, high, 56, wide_label_ref)
-    widen(scaled_ref, low, high, 0, wide_ref)
+    widen(label_ref, slab_ref, 56, wide_label_ref)
+    widen(scaled_ref, slab_ref, 0, wide_ref)
     wide_ref[...] += prolong(coarse, wide_label_ref[...])
-    send_cross(place_ref[2] == 0, wide_ref, z_ref, near_ref, far_ref, up_ref, down_ref)
+    send_cross(place_ref[2], wide_ref, z_ref, near_ref, far_ref, cross_ref)
 
 
 def next_solve_kernel(place_ref, gathered_ref, scaled_ref, wide_label_ref, left_ref, right_ref, scale_ref,
-                      wide_ref, w_ref, near_ref, far_ref, up_ref, down_ref):
-    low, high = arrived(place_ref[1] == 0, left_ref, right_ref)
+                      wide_ref, w_ref, near_ref, far_ref, slab_ref, cross_ref):
+    receive(place_ref[1], right_ref, left_ref, slab_ref)
     rows, valid = around(place_ref, gathered_ref.shape[0])
     tiles = jnp.concatenate([gathered_ref[pl.ds(row, 1)] for row in rows], 0)
     sums = jnp.sum(gathered_ref[...], axis=0)
     inverse = scale_ref[0 : 2 * NEAR + 1]
     level = smooth(DAMPING * tiles * inverse, valid)
     coarse = level * inverse[REACH : REACH + 3] + (sums * scale_ref[2 * NEAR + 1])[None]
-    widen(scaled_ref, low, high, 0, wide_ref)
+    widen(scaled_ref, slab_ref, 0, wide_ref)
     wide_ref[...] += prolong(coarse, wide_label_ref[...])
-    send_cross(place_ref[2] == 0, wide_ref, w_ref, near_ref, far_ref, up_ref, down_ref)
+    send_cross(place_ref[2], wide_ref, w_ref, near_ref, far_ref, cross_ref)
 
 
 def operate(place_ref, wide_ref, field_ref, near_ref, far_ref, sigma_ref, matrix_ref, ionic_ref,
-            grid_ref, local_ref, product_ref, total_ref):
+            cross_ref, grid_ref, local_ref, product_ref, total_ref):
     for n in range(18):
         grid_ref[n // 6 * 10 + 3 + n % 6, 0:10, :] = wide_ref[n, 0:10, :]
 
-    above, under = arrived(place_ref[2] == 0, near_ref, far_ref)
+    receive(place_ref[2], near_ref, far_ref, cross_ref)
     for c in range(3):
         for y in range(3):
             row = (3 * c + y) * 10
-            grid_ref[10 * c + y, 0:10, :] = above[row : row + 10]
-        grid_ref[10 * c + 9, 0:10, :] = under[10 * c : 10 * c + 10]
+            grid_ref[10 * c + y, 0:10, :] = cross_ref[1, row : row + 10, :]
+        grid_ref[10 * c + 9, 0:10, :] = cross_ref[0, 10 * c : 10 * c + 10, :]
     end = lanes((10, 128)) == 127
     for y in range(10):
         grid_ref[30 + y, 0:10, :] = jnp.where(end, 0.0, pltpu.roll(grid_ref[y, 0:10, :], 127, 1))
@@ -307,12 +309,12 @@
 
 
 def first_image_kernel(place_ref, wide_ref, z_ref, far_ref, near_ref, sigma_ref, matrix_ref, ionic_ref, diagonal_ref, label_ref,
-                       q_ref, scaled_ref, message_ref, left_ref, right_ref, up_ref, down_ref, *scratch):
+                       q_ref, scaled_ref, message_ref, left_ref, right_ref, both_ref, *scratch):
     image = operate(place_ref, wide_ref, z_ref, near_ref, far_ref, sigma_ref, matrix_ref, ionic_ref, *scratch)
     q_ref[...] = image
     message_ref[...] = jnp.broadcast_to(restrict(image, label_ref[...])[None], message_ref.shape)
     scaled_ref[...] = image / diagonal_ref[...]
-    send_slab(place_ref[1] == 0, (scaled_ref,), left_ref, right_ref, up_ref, down_ref)
+    send_slab(place_ref[1], (scaled_ref,), left_ref, right_ref, both_ref)
 
 
 def next_image_kernel(place_ref, wide_ref, w_ref, far_ref, near_ref, sigma_ref, matrix_ref, ionic_ref,
@@ -374,7 +376,7 @@
         return lax.all_to_all(copies, "slab", 0, 0, tiled=True)
 
     field, wide = (18, 8, 128), (18, 16, 128)
-    space = [(40, 16, 128), (64, 1152), (64, 1152), field]
+    space = [(2, 96, 128), (40, 16, 128), (64, 1152), (64, 1152), field]
     regions = region_labels + 1
     pairs = [
         (here * n_cross + beside, (here + 1) * n_cross + beside + 1)
@@ -392,7 +394,7 @@
     )
     sigma, diagonal, scaled, message, near, far = call(
         diagonal_kernel, [(9, 128), field, field, (n_slab, 8, 128), (112, 128), (112, 128)],
-        [field, (112, 128), (112, 128)],
+        [field, (2, 112, 128)],
         place, corner, below, beside, own, table, element_matrix, r, ionic, labels, coarse, smem=(0,),
     )
 
@@ -400,26 +402,27 @@
         count = lax.axis_size(axis)
         far_pairs = [(c, c + 1) for c in range(1, count - 1, 2)]
         far_pairs += [(above, c) for c, above in far_pairs]
-        return lax.ppermute(near, axis, [(c, c ^ 1) for c in range(count)]), lax.ppermute(far, axis, far_pairs)
+        far = lax.ppermute(far, axis, far_pairs)
+        return far, lax.ppermute(near, axis, [(c, c ^ 1) for c in range(count)])
 
     faces = [(96, 128), (96, 128)]
     wide_z, z, near, far, scale, wide_labels = call(
-        first_solve_kernel, [wide, field, *faces, (10, 8, 128), wide], faces,
+        first_solve_kernel, [wide, field, *faces, (10, 8, 128), wide], [(2, 112, 128), (2, 96, 128)],
         place, gather(message), scaled, labels, *exchange(near, far, "slab"), smem=(0,),
     )
     q, scaled, message, near, far = call(
         first_image_kernel, [field, field, (n_slab, 8, 128), (56, 128), (56, 128)],
-        [(56, 128), (56, 128), *space],
-        place, wide_z, z, *exchange(near, far, "cross")[::-1], sigma, element_matrix, ionic, diagonal, labels,
+        [(2, 56, 128), *space],
+        place, wide_z, z, *exchange(near, far, "cross"), sigma, element_matrix, ionic, diagonal, labels,
         smem=(0,),
     )
     wide_w, w, near, far = call(
-        next_solve_kernel, [wide, field, *faces], faces,
+        next_solve_kernel, [wide, field, *faces], [(2, 56, 128), (2, 96, 128)],
         place, gather(message), scaled, wide_labels, *exchange(near, far, "slab"), scale, smem=(0,),
     )
     t, message = call(
         next_image_kernel, [field, (n_slab // 2, 1, 128)], space,
-        place, wide_w, w, *exchange(near, far, "cross")[::-1], sigma, element_matrix, ionic, r, z, q, smem=(0,),
+        place, wide_w, w, *exchange(near, far, "cross"), sigma, element_matrix, ionic, r, z, q, smem=(0,),
     )
     parts = lax.all_to_all(message, "slab", 0, 0, axis_index_groups=planes, tiled=True)
     parts = jnp.broadcast_to(jnp.sum(parts, 0)[None], (2 * n_cross, 1, 128))

time: 120 us -> 115 us (0.958)
  blocking collectives: 30.6 us -> 27.6 us
  waiting for transfers between devices: 15.5 us -> 13.5 us
    ppermute x8, starting transfers between devices: 27.2 us -> 31.7 us  [the longest x4 17.2 us: exchange(): far = lax.ppermute(far, axis, far_pairs)]
    all_to_all x2, starting transfers between devices: 22.3 us -> 18.6 us  [gather(): return lax.all_to_all(copies, 'slab', 0, 0, tiled=True)]
    all_to_all x1, blocking collectives: 16.1 us -> 13 us  [body(): lax.all_to_all(message, 'slab', 0, 0, axis_index_groups=planes, tiled=True)]
    all_to_all x2, waiting for transfers between devices: 9.6 us -> 7.79 us  [gather(): return lax.all_to_all(copies, 'slab', 0, 0, tiled=True)]
  transfers between devices with their start and end apart: 13 -> 13, of which waited for: 8 -> 6; matrix products, arithmetic and copies ran while one was open for 0% -> 0% of each run, Pallas kernels for 1% -> 1%
where the time goes in v5:
time: 115 us
  starting transfers between devices  63 us (55%)
  blocking collectives  27.6 us (24%)
  waiting for transfers between devices  13.5 us (12%)
  Pallas kernels  9.02 us (8%)
    all_to_all x2, starting transfers between devices, gather(): return lax.all_to_all(copies, 'slab', 0, 0, tiled=True)  18.6 us
    ppermute x4, starting transfers between devices, exchange(): far = lax.ppermute(far, axis, far_pairs)  17.2 us
    ppermute x4, starting transfers between devices, exchange(): return (far, lax.ppermute(near, axis, [(c, c ^ 1) for c in range(count)]))  14.5 us
    all_to_all x1, blocking collectives, body(): lax.all_to_all(parts, ('slab', 'cross'), 0, 0, axis_index_groups=columns,...  14.5 us
    all_to_all x1, blocking collectives, body(): lax.all_to_all(message, 'slab', 0, 0, axis_index_groups=planes, tiled=True)  13 us
    pallas_call x7, Pallas kernels, call(): pl.pallas_call(kernel, out_shape=[jax.ShapeDtypeStruct(shape, F32) for sh...  9.02 us
    all_to_all x2, waiting for transfers between devices, gather(): return lax.all_to_all(copies, 'slab', 0, 0, tiled=True)  7.79 us
    ppermute x1, starting transfers between devices, body(): corner = lax.ppermute(regions[1, 1:2], ('slab', 'cross'), pairs)  6.6 us
  transfers between devices with their start and end apart: 13, of which 6 were waited for; matrix products, arithmetic and copies ran while one was open for 0% of the time, Pallas kernels for 1%

profile of v5, /device:TPU:1, one launch (start us, length us, event | category | flops | bytes accessed | tf_op | source)
XLA Modules:
  0.0 114.8 jit_solution(4631425566770327712)
XLA Ops:
  0.6 0.7 copy_add_fusion
  1.3 6.6 %collective-permute-start = (s32[1,128]{1,0:T(1,128)S(1)}, s32[1,128]{1,0:T(1,128)S(1)}, u32[]{:S(2)}, u32[]{:S(2)}) collective-permute-start(s32[1,128]{1,0:T(1,128)S(1)} %slice_bitcast_fusion.1), channel_id=1, source_target_pairs={{0,9},{1,10},{2,11},{3,12},{4,13},{5,14},{6,15},{8,17},{9,18},{10,... | collective-permute-start | bytes 1544 | tf_op jit(solution)/shard_map/ppermute | solution.py:386
  7.9 3.0 %collective-permute-start.1 = (s32[2,128]{1,0:T(2,128)S(1)}, s32[2,128]{1,0:T(2,128)S(1)}, u32[]{:S(2)}, u32[]{:S(2)}) collective-permute-start(s32[2,128]{1,0:T(2,128)S(1)} %bitcast.8), channel_id=1, source_target_pairs={{0,8},{8,16},{16,24},{24,32},{32,40},{40,48},{48,56},{56,64},{64,7... | collective-permute-start | bytes 3080 | tf_op jit(solution)/shard_map/ppermute | solution.py:373
  11.0 3.1 %collective-permute-start.2 = (s32[2,128]{1,0:T(2,128)S(1)}, s32[2,128]{1,0:T(2,128)S(1)}, u32[]{:S(2)}, u32[]{:S(2)}) collective-permute-start(s32[2,128]{1,0:T(2,128)S(1)} %slice_bitcast_fusion), channel_id=1, source_target_pairs={{0,1},{1,2},{2,3},{3,4},{4,5},{5,6},{6,7},{8,9},{9,10},{10,11},{11... | collective-permute-start | bytes 3080 | tf_op jit(solution)/shard_map/ppermute | solution.py:373
  14.1 0.1 pad_add_fusion.place_ref
  14.1 0.0 copy-start
  14.1 1.4 %shard_map.77 = (f32[18,8,128]{2,1,0:T(8,128)S(1)}, f32[18,8,128]{2,1,0:T(8,128)S(1)}, f32[18,8,128]{2,1,0:T(8,128)S(1)}, f32[8,128]{1,0:T(8,128)S(1)}, f32[4,128]{1,0:T(4,128)S(1)}, /*index=5*/f32[4,128]{1,0:T(4,128)S(1)}) custom-call(f32[6,6,384]{2,1,0:T(8,128)} %source_hbm.1, f32[6,6,384]{2,1,0:T(8,128)} %potential_hbm.1, s32[6,6,384]{2,1,0:T(8,128)} %map_hbm.1, ...), custom_call_target="tpu_custom_call" | custom-call | tf_op jit(solution)/shard_map/pallas_call | solution.py:36
  15.6 0.0 collective-permute-done.corner_ref
  15.6 0.0 collective-permute-done.1.below_ref
  15.6 0.0 collective-permute-done.2.beside_ref
  15.6 0.0 copy-done
  15.6 1.6 %shard_map.78 = (f32[9,128]{1,0:T(8,128)S(1)}, f32[18,8,128]{2,1,0:T(8,128)S(1)}, f32[18,8,128]{2,1,0:T(8,128)S(1)}, f32[64,8,128]{2,1,0:T(8,128)}, f32[112,128]{1,0:T(8,128)S(1)}, /*index=5*/f32[112,128]{1,0:T(8,128)S(1)}) custom-call(s32[3]{0:T(128)S(1)} %pad_add_fusion.place_ref, s32[1,128]{1,0:T(1,128)S(1)} %collective-permute-done.corner_ref, ...), custom_call_target="tpu_custom_call" | custom-call | tf_op jit(solution)/shard_map/pallas_call | solution.py:36
  17.3 13.6 %all-to-all-start = ((f32[64,8,128]{2,1,0:T(8,128)}), f32[64,8,128]{2,1,0:T(8,128)S(1)}, u32[]{:S(2)}, u32[]{:S(2)}) async-start(f32[64,8,128]{2,1,0:T(8,128)} %get-tuple-element.37), calls=%async_computation | async-start | bytes 524288 | tf_op jit(solution)/shard_map/all_to_all | solution.py:376
  30.9 0.7 collective-permute-start.3
  31.6 5.3 %collective-permute-start.4 = (f32[112,128]{1,0:T(8,128)S(1)}, f32[112,128]{1,0:T(8,128)S(1)}, u32[]{:S(2)}, u32[]{:S(2)}) collective-permute-start(f32[112,128]{1,0:T(8,128)S(1)} %get-tuple-element.40), channel_id=1, source_target_pairs={{0,8},{8,0},{16,24},{24,16},{32,40},{40,32},{48,56},{56,48},{64,72... | collective-permute-start | bytes 172040 | tf_op jit(solution)/shard_map/ppermute | solution.py:406
  36.9 0.0 collective-permute-done.3.left_ref
  36.9 1.8 %collective-permute-done.4.right_ref = f32[112,128]{1,0:T(8,128)S(1)} collective-permute-done((f32[112,128]{1,0:T(8,128)S(1)}, f32[112,128]{1,0:T(8,128)S(1)}, u32[]{:S(2)}, u32[]{:S(2)}) %collective-permute-start.4) | collective-permute-done | bytes 57376 | tf_op jit(solution)/shard_map/ppermute | solution.py:406
  38.8 4.0 %all-to-all-done.gathered_ref = f32[64,8,128]{2,1,0:T(8,128)S(1)} async-done(((f32[64,8,128]{2,1,0:T(8,128)}), f32[64,8,128]{2,1,0:T(8,128)S(1)}, u32[]{:S(2)}, u32[]{:S(2)}) %all-to-all-start) | async-done | bytes 262176 | tf_op jit(solution)/shard_map/all_to_all | solution.py:376
  42.8 1.0 shard_map.79
  43.8 7.6 %collective-permute-start.5 = (f32[96,128]{1,0:T(8,128)S(1)}, f32[96,128]{1,0:T(8,128)S(1)}, u32[]{:S(2)}, u32[]{:S(2)}) collective-permute-start(f32[96,128]{1,0:T(8,128)S(1)} %get-tuple-element.43), channel_id=1, source_target_pairs={{1,2},{3,4},{5,6},{2,1},{4,3},{6,5},{9,10},{11,12},{13,14},{10,9},... | collective-permute-start | bytes 147464 | tf_op jit(solution)/shard_map/ppermute | solution.py:405
  51.4 1.9 %collective-permute-start.6 = (f32[96,128]{1,0:T(8,128)S(1)}, f32[96,128]{1,0:T(8,128)S(1)}, u32[]{:S(2)}, u32[]{:S(2)}) collective-permute-start(f32[96,128]{1,0:T(8,128)S(1)} %get-tuple-element.44), channel_id=1, source_target_pairs={{0,1},{1,0},{2,3},{3,2},{4,5},{5,4},{6,7},{7,6},{8,9},{9,8},{10,11... | collective-permute-start | bytes 147464 | tf_op jit(solution)/shard_map/ppermute | solution.py:406
  53.3 0.0 collective-permute-done.5.far_ref
  53.3 1.2 %collective-permute-done.6.near_ref = f32[96,128]{1,0:T(8,128)S(1)} collective-permute-done((f32[96,128]{1,0:T(8,128)S(1)}, f32[96,128]{1,0:T(8,128)S(1)}, u32[]{:S(2)}, u32[]{:S(2)}) %collective-permute-start.6) | collective-permute-done | bytes 49184 | tf_op jit(solution)/shard_map/ppermute | solution.py:406
  54.5 1.8 %shard_map.80 = (f32[18,8,128]{2,1,0:T(8,128)S(1)}, f32[18,8,128]{2,1,0:T(8,128)S(1)}, f32[64,8,128]{2,1,0:T(8,128)}, f32[56,128]{1,0:T(8,128)S(1)}, f32[56,128]{1,0:T(8,128)S(1)}) custom-call(s32[3]{0:T(128)S(1)} %pad_add_fusion.place_ref, f32[18,16,128]{2,1,0:T(8,128)S(1)} %get-tuple-element.41.wide_ref, f32[18,8,128]{2,1,0:T(8,128)S(1)} %get-tuple-element.42.z_ref, ...), custom_call_target="tpu_custom_call" | custom-call | tf_op jit(solution)/shard_map/pallas_call | solution.py:36
  56.3 5.0 %all-to-all-start.1 = ((f32[64,8,128]{2,1,0:T(8,128)}), f32[64,8,128]{2,1,0:T(8,128)S(1)}, u32[]{:S(2)}, u32[]{:S(2)}) async-start(f32[64,8,128]{2,1,0:T(8,128)} %get-tuple-element.47), calls=%async_computation.1 | async-start | bytes 524288 | tf_op jit(solution)/shard_map/all_to_all | solution.py:376
  61.3 0.7 collective-permute-start.7
  62.0 5.3 %collective-permute-start.8 = (f32[56,128]{1,0:T(8,128)S(1)}, f32[56,128]{1,0:T(8,128)S(1)}, u32[]{:S(2)}, u32[]{:S(2)}) collective-permute-start(f32[56,128]{1,0:T(8,128)S(1)} %get-tuple-element.51), channel_id=1, source_target_pairs={{0,8},{8,0},{16,24},{24,16},{32,40},{40,32},{48,56},{56,48},{64,72... | collective-permute-start | bytes 86024 | tf_op jit(solution)/shard_map/ppermute | solution.py:406
  67.3 0.0 collective-permute-done.7.left_ref
  67.3 1.5 %collective-permute-done.8.right_ref = f32[56,128]{1,0:T(8,128)S(1)} collective-permute-done((f32[56,128]{1,0:T(8,128)S(1)}, f32[56,128]{1,0:T(8,128)S(1)}, u32[]{:S(2)}, u32[]{:S(2)}) %collective-permute-start.8) | collective-permute-done | bytes 28704 | tf_op jit(solution)/shard_map/ppermute | solution.py:406
  68.9 3.8 %all-to-all-done.1.gathered_ref = f32[64,8,128]{2,1,0:T(8,128)S(1)} async-done(((f32[64,8,128]{2,1,0:T(8,128)}), f32[64,8,128]{2,1,0:T(8,128)S(1)}, u32[]{:S(2)}, u32[]{:S(2)}) %all-to-all-start.1) | async-done | bytes 262176 | tf_op jit(solution)/shard_map/all_to_all | solution.py:376
  72.6 0.9 shard_map.81
  73.5 8.3 %collective-permute-start.9 = (f32[96,128]{1,0:T(8,128)S(1)}, f32[96,128]{1,0:T(8,128)S(1)}, u32[]{:S(2)}, u32[]{:S(2)}) collective-permute-start(f32[96,128]{1,0:T(8,128)S(1)} %get-tuple-element.55), channel_id=1, source_target_pairs={{1,2},{3,4},{5,6},{2,1},{4,3},{6,5},{9,10},{11,12},{13,14},{10,9},... | collective-permute-start | bytes 147464 | tf_op jit(solution)/shard_map/ppermute | solution.py:405
  81.8 1.9 %collective-permute-start.10 = (f32[96,128]{1,0:T(8,128)S(1)}, f32[96,128]{1,0:T(8,128)S(1)}, u32[]{:S(2)}, u32[]{:S(2)}) collective-permute-start(f32[96,128]{1,0:T(8,128)S(1)} %get-tuple-element.56), channel_id=1, source_target_pairs={{0,1},{1,0},{2,3},{3,2},{4,5},{5,4},{6,7},{7,6},{8,9},{9,8},{10,11... | collective-permute-start | bytes 147464 | tf_op jit(solution)/shard_map/ppermute | solution.py:406
  83.7 0.0 collective-permute-done.9.far_ref
  83.7 1.2 %collective-permute-done.10.near_ref = f32[96,128]{1,0:T(8,128)S(1)} collective-permute-done((f32[96,128]{1,0:T(8,128)S(1)}, f32[96,128]{1,0:T(8,128)S(1)}, u32[]{:S(2)}, u32[]{:S(2)}) %collective-permute-start.10) | collective-permute-done | bytes 49184 | tf_op jit(solution)/shard_map/ppermute | solution.py:406
  84.9 1.1 shard_map.82
  86.1 13.0 %all_to_all.20 = f32[32,1,128]{2,1,0:T(1,128)S(1)} all-to-all(f32[32,1,128]{2,1,0:T(1,128)S(1)} %get-tuple-element.58), channel_id=1, replica_groups={{0,16,32,48,64,80,96,112,128,144,160,176,192,208,224,240,256,272,288,30..., dimensions={0} | all-to-all | bytes 32768 | tf_op jit(solution)/shard_map/all_to_all | solution.py:427
  99.1 0.1 reduce_sum.9
  99.2 14.5 %all_to_all.21.dots_ref = f32[16,1,128]{2,1,0:T(1,128)S(1)} all-to-all(f32[16,1,128]{2,1,0:T(1,128)S(1)} %broadcast_in_dim.2), channel_id=1, replica_groups={{0,1,2,3,4,5,6,7,8,9,10,11,12,13,14,15},{16,17,18,19,20,21,22,23,24,25,..., dimensions={0} | all-to-all | bytes 16384 | tf_op jit(solution)/shard_map/all_to_all | solution.py:429
  113.7 1.1 shard_map.83
  (4 shorter events, 0.0 us)
Async XLA Ops:
  1.3 14.3 %collective-permute-start = (s32[1,128]{1,0:T(1,128)S(1)}, s32[1,128]{1,0:T(1,128)S(1)}, u32[]{:S(2)}, u32[]{:S(2)}) collective-permute-start(s32[1,128]{1,0:T(1,128)S(1)} %slice_bitcast_fusion.1), channel_id=1, source_target_pairs={{0,9},{1,10},{2,11},{3,12},{4,13},{5,14},{6,15},{8,17},{9,18},{10,... | collective-permute-start | bytes 1544 | tf_op jit(solution)/shard_map/ppermute | solution.py:386
  7.9 7.7 %collective-permute-start.1 = (s32[2,128]{1,0:T(2,128)S(1)}, s32[2,128]{1,0:T(2,128)S(1)}, u32[]{:S(2)}, u32[]{:S(2)}) collective-permute-start(s32[2,128]{1,0:T(2,128)S(1)} %bitcast.8), channel_id=1, source_target_pairs={{0,8},{8,16},{16,24},{24,32},{32,40},{40,48},{48,56},{56,64},{64,7... | collective-permute-start | bytes 3080 | tf_op jit(solution)/shard_map/ppermute | solution.py:373
  11.0 4.7 %collective-permute-start.2 = (s32[2,128]{1,0:T(2,128)S(1)}, s32[2,128]{1,0:T(2,128)S(1)}, u32[]{:S(2)}, u32[]{:S(2)}) collective-permute-start(s32[2,128]{1,0:T(2,128)S(1)} %slice_bitcast_fusion), channel_id=1, source_target_pairs={{0,1},{1,2},{2,3},{3,4},{4,5},{5,6},{6,7},{8,9},{9,10},{10,11},{11... | collective-permute-start | bytes 3080 | tf_op jit(solution)/shard_map/ppermute | solution.py:373
  14.1 1.5 %copy-start = (f32[64,64]{1,0:T(8,128)S(1)}, f32[64,64]{1,0:T(8,128)}, u32[]{:S(2)}) copy-start(f32[64,64]{1,0:T(8,128)} %matrix_ref.5) | copy-start | bytes 49156
  17.3 25.5 %all-to-all-start = ((f32[64,8,128]{2,1,0:T(8,128)}), f32[64,8,128]{2,1,0:T(8,128)S(1)}, u32[]{:S(2)}, u32[]{:S(2)}) async-start(f32[64,8,128]{2,1,0:T(8,128)} %get-tuple-element.37), calls=%async_computation | async-start | bytes 524288 | tf_op jit(solution)/shard_map/all_to_all | solution.py:376
  30.9 6.0 %collective-permute-start.3 = (f32[112,128]{1,0:T(8,128)S(1)}, f32[112,128]{1,0:T(8,128)S(1)}, u32[]{:S(2)}, u32[]{:S(2)}) collective-permute-start(f32[112,128]{1,0:T(8,128)S(1)} %get-tuple-element.39), channel_id=1, source_target_pairs={{8,16},{24,32},{40,48},{56,64},{72,80},{88,96},{104,112},{120,128}... | collective-permute-start | bytes 172040 | tf_op jit(solution)/shard_map/ppermute | solution.py:405
  31.6 7.2 %collective-permute-start.4 = (f32[112,128]{1,0:T(8,128)S(1)}, f32[112,128]{1,0:T(8,128)S(1)}, u32[]{:S(2)}, u32[]{:S(2)}) collective-permute-start(f32[112,128]{1,0:T(8,128)S(1)} %get-tuple-element.40), channel_id=1, source_target_pairs={{0,8},{8,0},{16,24},{24,16},{32,40},{40,32},{48,56},{56,48},{64,72... | collective-permute-start | bytes 172040 | tf_op jit(solution)/shard_map/ppermute | solution.py:406
  43.8 9.5 %collective-permute-start.5 = (f32[96,128]{1,0:T(8,128)S(1)}, f32[96,128]{1,0:T(8,128)S(1)}, u32[]{:S(2)}, u32[]{:S(2)}) collective-permute-start(f32[96,128]{1,0:T(8,128)S(1)} %get-tuple-element.43), channel_id=1, source_target_pairs={{1,2},{3,4},{5,6},{2,1},{4,3},{6,5},{9,10},{11,12},{13,14},{10,9},... | collective-permute-start | bytes 147464 | tf_op jit(solution)/shard_map/ppermute | solution.py:405
  51.4 3.1 %collective-permute-start.6 = (f32[96,128]{1,0:T(8,128)S(1)}, f32[96,128]{1,0:T(8,128)S(1)}, u32[]{:S(2)}, u32[]{:S(2)}) collective-permute-start(f32[96,128]{1,0:T(8,128)S(1)} %get-tuple-element.44), channel_id=1, source_target_pairs={{0,1},{1,0},{2,3},{3,2},{4,5},{5,4},{6,7},{7,6},{8,9},{9,8},{10,11... | collective-permute-start | bytes 147464 | tf_op jit(solution)/shard_map/ppermute | solution.py:406
  56.3 16.3 %all-to-all-start.1 = ((f32[64,8,128]{2,1,0:T(8,128)}), f32[64,8,128]{2,1,0:T(8,128)S(1)}, u32[]{:S(2)}, u32[]{:S(2)}) async-start(f32[64,8,128]{2,1,0:T(8,128)} %get-tuple-element.47), calls=%async_computation.1 | async-start | bytes 524288 | tf_op jit(solution)/shard_map/all_to_all | solution.py:376
  61.3 6.0 %collective-permute-start.7 = (f32[56,128]{1,0:T(8,128)S(1)}, f32[56,128]{1,0:T(8,128)S(1)}, u32[]{:S(2)}, u32[]{:S(2)}) collective-permute-start(f32[56,128]{1,0:T(8,128)S(1)} %get-tuple-element.50), channel_id=1, source_target_pairs={{8,16},{24,32},{40,48},{56,64},{72,80},{88,96},{104,112},{120,128}... | collective-permute-start | bytes 86024 | tf_op jit(solution)/shard_map/ppermute | solution.py:405
  62.0 6.9 %collective-permute-start.8 = (f32[56,128]{1,0:T(8,128)S(1)}, f32[56,128]{1,0:T(8,128)S(1)}, u32[]{:S(2)}, u32[]{:S(2)}) collective-permute-start(f32[56,128]{1,0:T(8,128)S(1)} %get-tuple-element.51), channel_id=1, source_target_pairs={{0,8},{8,0},{16,24},{24,16},{32,40},{40,32},{48,56},{56,48},{64,72... | collective-permute-start | bytes 86024 | tf_op jit(solution)/shard_map/ppermute | solution.py:406
  73.5 10.2 %collective-permute-start.9 = (f32[96,128]{1,0:T(8,128)S(1)}, f32[96,128]{1,0:T(8,128)S(1)}, u32[]{:S(2)}, u32[]{:S(2)}) collective-permute-start(f32[96,128]{1,0:T(8,128)S(1)} %get-tuple-element.55), channel_id=1, source_target_pairs={{1,2},{3,4},{5,6},{2,1},{4,3},{6,5},{9,10},{11,12},{13,14},{10,9},... | collective-permute-start | bytes 147464 | tf_op jit(solution)/shard_map/ppermute | solution.py:405
  81.8 3.1 %collective-permute-start.10 = (f32[96,128]{1,0:T(8,128)S(1)}, f32[96,128]{1,0:T(8,128)S(1)}, u32[]{:S(2)}, u32[]{:S(2)}) collective-permute-start(f32[96,128]{1,0:T(8,128)S(1)} %get-tuple-element.56), channel_id=1, source_target_pairs={{0,1},{1,0},{2,3},{3,2},{4,5},{5,4},{6,7},{7,6},{8,9},{9,8},{10,11... | collective-permute-start | bytes 147464 | tf_op jit(solution)/shard_map/ppermute | solution.py:406

commit v6 on v5

--- a/solution.py
+++ b/solution.py
@@ -20,13 +20,17 @@
 SPAN = (-1, 0, 1)
 
 
+def parity(axis):
+    return lax.rem(lax.axis_index(axis), 2)
+
+
 def lanes(shape):
     return lax.broadcasted_iota(jnp.int32, shape, len(shape) - 1)
 
 
-def call(kernel, out_shapes, scratch, *operands, smem=(), away=()):
+def call(kernel, out_shapes, scratch, *operands, away=()):
     specs = [
-        pl.BlockSpec(memory_space=pltpu.SMEM if index in smem else pltpu.HBM if index in away else pltpu.VMEM)
+        pl.BlockSpec(memory_space=pltpu.HBM if index in away else pltpu.VMEM)
         for index in range(len(operands))
     ]
     operands = [
@@ -157,8 +161,8 @@
     send(odd, both_ref, near_ref, far_ref)
 
 
-def diagonal_kernel(place_ref, corner_ref, below_ref, beside_ref, own_ref, table_ref, matrix_ref, r_ref, ionic_ref, label_ref, coarse_ref,
-                    sigma_ref, diagonal_ref, scaled_ref, message_ref, near_ref, far_ref,
+def diagonal_kernel(corner_ref, below_ref, beside_ref, own_ref, table_ref, matrix_ref, r_ref, ionic_ref, label_ref,
+                    sigma_ref, diagonal_ref, scaled_ref, near_ref, far_ref,
                     total_ref, both_ref):
     sigma_ref[0:1, :] = conductance(corner_ref[...], table_ref)
     sigma_ref[1:3, :] = conductance(below_ref[...], table_ref)
@@ -172,12 +176,22 @@
     labels = label_ref[...]
     diagonal = jnp.where(labels == 0.0, 1.0, total_ref[...] + ionic_ref[...])
     diagonal_ref[...] = diagonal
-    coarse_diag = SHARE * restrict(diagonal, labels)
+    scaled_ref[...] = r_ref[...] / diagonal
+    send_slab(parity("slab"), (scaled_ref, label_ref), near_ref, far_ref, both_ref)
+
+
+def first_message_kernel(diagonal_ref, label_ref, coarse_ref, held_ref, message_ref, near_ref):
+    labels = label_ref[...]
+    coarse_diag = SHARE * restrict(diagonal_ref[...], labels)
     even = lanes((8, 128)) % 2 == 0
     message = jnp.where(even, coarse_ref[...], coarse_diag)
     message_ref[...] = jnp.broadcast_to(message[None], message_ref.shape)
-    scaled_ref[...] = r_ref[...] / diagonal
-    send_slab(place_ref[1], (scaled_ref, label_ref), near_ref, far_ref, both_ref)
+    near_ref[...] = held_ref[...]
+
+
+def next_message_kernel(q_ref, label_ref, held_ref, message_ref, near_ref):
+    message_ref[...] = jnp.broadcast_to(restrict(q_ref[...], label_ref[...])[None], message_ref.shape)
+    near_ref[...] = held_ref[...]
 
 
 def along(values):
@@ -201,10 +215,10 @@
     return level
 
 
-def around(place_ref, count):
+def around(count):
     rows, valid = [], []
     for step in range(-NEAR, NEAR + 1):
-        row = place_ref[0] + step
+        row = lax.axis_index("slab") + step
         inside = jnp.logical_and(row >= 0, row < count)
         rows.append(jnp.clip(row, 0, count - 1))
         valid.append(jnp.where(inside, jnp.ones((1, 8, 128), F32), 0.0))
@@ -242,10 +256,10 @@
     send(odd, both_ref, near_ref, far_ref)
 
 
-def first_solve_kernel(place_ref, gathered_ref, scaled_ref, label_ref, left_ref, right_ref,
+def first_solve_kernel(gathered_ref, scaled_ref, label_ref, left_ref, right_ref,
                        wide_ref, z_ref, near_ref, far_ref, scale_ref, wide_label_ref, slab_ref, cross_ref):
-    receive(place_ref[1], right_ref, left_ref, slab_ref)
-    rows, valid = around(place_ref, gathered_ref.shape[0])
+    receive(parity("slab"), right_ref, left_ref, slab_ref)
+    rows, valid = around(gathered_ref.shape[0])
     tiles = jnp.concatenate([gathered_ref[pl.ds(row, 1)] for row in rows], 0)
     sums = jnp.sum(gathered_ref[...], axis=0)
     inverse = valid / jnp.sqrt(odd_part(tiles))
@@ -257,13 +271,13 @@
     widen(label_ref, slab_ref, 56, wide_label_ref)
     widen(scaled_ref, slab_ref, 0, wide_ref)
     wide_ref[...] += prolong(coarse, wide_label_ref[...])
-    send_cross(place_ref[2], wide_ref, z_ref, near_ref, far_ref, cross_ref)
-
-
-def next_solve_kernel(place_ref, gathered_ref, scaled_ref, wide_label_ref, left_ref, right_ref, scale_ref,
+    send_cross(parity("cross"), wide_ref, z_ref, near_ref, far_ref, cross_ref)
+
+
+def next_solve_kernel(gathered_ref, scaled_ref, wide_label_ref, left_ref, right_ref, scale_ref,
                       wide_ref, w_ref, near_ref, far_ref, slab_ref, cross_ref):
-    receive(place_ref[1], right_ref, left_ref, slab_ref)
-    rows, valid = around(place_ref, gathered_ref.shape[0])
+    receive(parity("slab"), right_ref, left_ref, slab_ref)
+    rows, valid = around(gathered_ref.shape[0])
     tiles = jnp.concatenate([gathered_ref[pl.ds(row, 1)] for row in rows], 0)
     sums = jnp.sum(gathered_ref[...], axis=0)
     inverse = scale_ref[0 : 2 * NEAR + 1]
@@ -271,15 +285,15 @@
     coarse = level * inverse[REACH : REACH + 3] + (sums * scale_ref[2 * NEAR + 1])[None]
     widen(scaled_ref, slab_ref, 0, wide_ref)
     wide_ref[...] += prolong(coarse, wide_label_ref[...])
-    send_cross(place_ref[2], wide_ref, w_ref, near_ref, far_ref, cross_ref)
-
-
-def operate(place_ref, wide_ref, field_ref, near_ref, far_ref, sigma_ref, matrix_ref, ionic_ref,
+    send_cross(parity("cross"), wide_ref, w_ref, near_ref, far_ref, cross_ref)
+
+
+def operate(wide_ref, field_ref, near_ref, far_ref, sigma_ref, matrix_ref, ionic_ref,
             cross_ref, grid_ref, local_ref, product_ref, total_ref):
     for n in range(18):
         grid_ref[n // 6 * 10 + 3 + n % 6, 0:10, :] = wide_ref[n, 0:10, :]
 
-    receive(place_ref[2], near_ref, far_ref, cross_ref)
+    receive(parity("cross"), near_ref, far_ref, cross_ref)
     for c in range(3):
         for y in range(3):
             row = (3 * c + y) * 10
@@ -308,18 +322,17 @@
     return total_ref[...] + ionic_ref[...] * field_ref[...]
 
 
-def first_image_kernel(place_ref, wide_ref, z_ref, far_ref, near_ref, sigma_ref, matrix_ref, ionic_ref, diagonal_ref, label_ref,
-                       q_ref, scaled_ref, message_ref, left_ref, right_ref, both_ref, *scratch):
-    image = operate(place_ref, wide_ref, z_ref, near_ref, far_ref, sigma_ref, matrix_ref, ionic_ref, *scratch)
+def first_image_kernel(wide_ref, z_ref, far_ref, near_ref, sigma_ref, matrix_ref, ionic_ref, diagonal_ref,
+                       q_ref, scaled_ref, left_ref, right_ref, both_ref, *scratch):
+    image = operate(wide_ref, z_ref, near_ref, far_ref, sigma_ref, matrix_ref, ionic_ref, *scratch)
     q_ref[...] = image
-    message_ref[...] = jnp.broadcast_to(restrict(image, label_ref[...])[None], message_ref.shape)
     scaled_ref[...] = image / diagonal_ref[...]
-    send_slab(place_ref[1], (scaled_ref,), left_ref, right_ref, both_ref)
-
-
-def next_image_kernel(place_ref, wide_ref, w_ref, far_ref, near_ref, sigma_ref, matrix_ref, ionic_ref,
+    send_slab(parity("slab"), (scaled_ref,), left_ref, right_ref, both_ref)
+
+
+def next_image_kernel(wide_ref, w_ref, far_ref, near_ref, sigma_ref, matrix_ref, ionic_ref,
                       r_ref, z_ref, q_ref, t_ref, message_ref, *scratch):
-    image = operate(place_ref, wide_ref, w_ref, near_ref, far_ref, sigma_ref, matrix_ref, ionic_ref, *scratch)
+    image = operate(wide_ref, w_ref, near_ref, far_ref, sigma_ref, matrix_ref, ionic_ref, *scratch)
     t_ref[...] = image
     r, z, q, w = r_ref[...], z_ref[...], q_ref[...], w_ref[...]
     row = jnp.zeros((1, 128), F32)
@@ -360,8 +373,6 @@
 def body(adjoint_source, potential, element_matrix, region_labels, conductivity, restriction_map):
     n_slab = lax.axis_size("slab")
     n_cross = lax.axis_size("cross")
-    slab, cross = lax.axis_index("slab"), lax.axis_index("cross")
-    place = jnp.stack([slab, slab % 2, cross % 2]).astype(jnp.int32)
     columns = [
         [slab * n_cross + cross for slab in (2 * pair, 2 * pair + 1) for cross in range(n_cross)]
         for pair in range(n_slab // 2)
@@ -392,10 +403,13 @@
          pltpu.VMEM((2, 2, 128), jnp.int32), pltpu.SMEM((4,), F32), pltpu.SemaphoreType.DMA((5,))],
         adjoint_source, potential, restriction_map, region_labels, conductivity, away=(0, 1, 2, 3, 4),
     )
-    sigma, diagonal, scaled, message, near, far = call(
-        diagonal_kernel, [(9, 128), field, field, (n_slab, 8, 128), (112, 128), (112, 128)],
+    sigma, diagonal, scaled, near, far = call(
+        diagonal_kernel, [(9, 128), field, field, (112, 128), (112, 128)],
         [field, (2, 112, 128)],
-        place, corner, below, beside, own, table, element_matrix, r, ionic, labels, coarse, smem=(0,),
+        corner, below, beside, own, table, element_matrix, r, ionic, labels,
+    )
+    message, near = call(
+        first_message_kernel, [(n_slab, 8, 128), (112, 128)], [], diagonal, labels, coarse, near
     )
 
     def exchange(near, far, axis):
@@ -408,21 +422,21 @@
     faces = [(96, 128), (96, 128)]
     wide_z, z, near, far, scale, wide_labels = call(
         first_solve_kernel, [wide, field, *faces, (10, 8, 128), wide], [(2, 112, 128), (2, 96, 128)],
-        place, gather(message), scaled, labels, *exchange(near, far, "slab"), smem=(0,),
-    )
-    q, scaled, message, near, far = call(
-        first_image_kernel, [field, field, (n_slab, 8, 128), (56, 128), (56, 128)],
+        gather(message), scaled, labels, *exchange(near, far, "slab"),
+    )
+    q, scaled, near, far = call(
+        first_image_kernel, [field, field, (56, 128), (56, 128)],
         [(2, 56, 128), *space],
-        place, wide_z, z, *exchange(near, far, "cross"), sigma, element_matrix, ionic, diagonal, labels,
-        smem=(0,),
-    )
+        wide_z, z, *exchange(near, far, "cross"), sigma, element_matrix, ionic, diagonal,
+    )
+    message, near = call(next_message_kernel, [(n_slab, 8, 128), (56, 128)], [], q, labels, near)
     wide_w, w, near, far = call(
         next_solve_kernel, [wide, field, *faces], [(2, 56, 128), (2, 96, 128)],
-        place, gather(message), scaled, wide_labels, *exchange(near, far, "slab"), scale, smem=(0,),
+        gather(message), scaled, wide_labels, *exchange(near, far, "slab"), scale,
     )
     t, message = call(
         next_image_kernel, [field, (n_slab // 2, 1, 128)], space,
-        place, wide_w, w, *exchange(near, far, "cross"), sigma, element_matrix, ionic, r, z, q, smem=(0,),
+        wide_w, w, *exchange(near, far, "cross"), sigma, element_matrix, ionic, r, z, q,
     )
     parts = lax.all_to_all(message, "slab", 0, 0, axis_index_groups=planes, tiled=True)
     parts = jnp.broadcast_to(jnp.sum(parts, 0)[None], (2 * n_cross, 1, 128))

time: 115 us -> 114 us (level)
  Pallas kernels: 9.02 us -> 6.44 us
  waiting for transfers between devices: 13.5 us -> 15.3 us
    ppermute x4, starting transfers between devices: 17.2 us -> 12.7 us  [exchange(): far = lax.ppermute(far, axis, far_pairs)]
    all_to_all x2, starting transfers between devices: 18.6 us -> 22.2 us  [gather(): return lax.all_to_all(copies, 'slab', 0, 0, tiled=True)]
    ppermute x2, starting transfers between devices: 6.08 us -> 9.08 us  [shifted(): return lax.ppermute(value, axis, pairs)]
    ppermute x1, starting transfers between devices: 6.6 us -> 3.62 us  [body(): corner = lax.ppermute(regions[1, 1:2], ('slab', 'cross'), pairs)]
    pallas_call x7 -> x9, Pallas kernels: 9.02 us -> 6.44 us  [call(): pl.pallas_call(kernel, out_shape=[jax.ShapeDtypeStruct(shape, F32) for sh...]
    all_to_all x2, waiting for transfers between devices: 7.79 us -> 8.97 us  [gather(): return lax.all_to_all(copies, 'slab', 0, 0, tiled=True)]
  transfers between devices with their start and end apart: 13 -> 13, of which waited for: 6 -> 7; matrix products, arithmetic and copies ran while one was open for 0% -> 0% of each run, Pallas kernels for 1% -> 1%
where the time goes in v6:
time: 114 us; the launch traced here: 113 us
  starting transfers between devices  62.1 us (54%)
  blocking collectives  27.7 us (24%)
  waiting for transfers between devices  15.3 us (13%)
  Pallas kernels  6.44 us (6%)
    all_to_all x2, starting transfers between devices, gather(): return lax.all_to_all(copies, 'slab', 0, 0, tiled=True)  22.2 us
    all_to_all x1, blocking collectives, body(): lax.all_to_all(parts, ('slab', 'cross'), 0, 0, axis_index_groups=columns,...  14.7 us
    ppermute x4, starting transfers between devices, exchange(): return (far, lax.ppermute(near, axis, [(c, c ^ 1) for c in range(count)]))  14.5 us
    all_to_all x1, blocking collectives, body(): lax.all_to_all(message, 'slab', 0, 0, axis_index_groups=planes, tiled=True)  13 us
    ppermute x4, starting transfers between devices, exchange(): far = lax.ppermute(far, axis, far_pairs)  12.7 us
    ppermute x2, starting transfers between devices, shifted(): return lax.ppermute(value, axis, pairs)  9.08 us
    all_to_all x2, waiting for transfers between devices, gather(): return lax.all_to_all(copies, 'slab', 0, 0, tiled=True)  8.97 us
    pallas_call x9, Pallas kernels, call(): pl.pallas_call(kernel, out_shape=[jax.ShapeDtypeStruct(shape, F32) for sh...  6.44 us
  transfers between devices with their start and end apart: 13, of which 7 were waited for; matrix products, arithmetic and copies ran while one was open for 0% of the time, Pallas kernels for 1%

profile of v6, /device:TPU:1, one launch (start us, length us, event | category | flops | bytes accessed | tf_op | source)
XLA Modules:
  0.0 113.2 jit_solution(8956979548740396584)
XLA Ops:
  0.6 0.7 copy_add_fusion
  1.3 4.0 %collective-permute-start.1 = (s32[2,128]{1,0:T(2,128)S(1)}, s32[2,128]{1,0:T(2,128)S(1)}, u32[]{:S(2)}, u32[]{:S(2)}) collective-permute-start(s32[2,128]{1,0:T(2,128)S(1)} %bitcast.5), channel_id=1, source_target_pairs={{0,8},{8,16},{16,24},{24,32},{32,40},{40,48},{48,56},{56,64},{64,7... | collective-permute-start | bytes 3080 | tf_op jit(solution)/shard_map/ppermute | solution.py:384
  5.4 5.1 %collective-permute-start.2 = (s32[2,128]{1,0:T(2,128)S(1)}, s32[2,128]{1,0:T(2,128)S(1)}, u32[]{:S(2)}, u32[]{:S(2)}) collective-permute-start(s32[2,128]{1,0:T(2,128)S(1)} %slice_bitcast_fusion), channel_id=1, source_target_pairs={{0,1},{1,2},{2,3},{3,4},{4,5},{5,6},{6,7},{8,9},{9,10},{10,11},{11... | collective-permute-start | bytes 3080 | tf_op jit(solution)/shard_map/ppermute | solution.py:384
  10.4 0.0 copy-start
  10.4 3.6 %collective-permute-start = (s32[1,128]{1,0:T(1,128)S(1)}, s32[1,128]{1,0:T(1,128)S(1)}, u32[]{:S(2)}, u32[]{:S(2)}) collective-permute-start(s32[1,128]{1,0:T(1,128)S(1)} %slice_bitcast_fusion.1), channel_id=1, source_target_pairs={{0,9},{1,10},{2,11},{3,12},{4,13},{5,14},{6,15},{8,17},{9,18},{10,... | collective-permute-start | bytes 1544 | tf_op jit(solution)/shard_map/ppermute | solution.py:397
  14.1 1.4 %shard_map.77 = (f32[18,8,128]{2,1,0:T(8,128)S(1)}, f32[18,8,128]{2,1,0:T(8,128)S(1)}, f32[18,8,128]{2,1,0:T(8,128)S(1)}, f32[8,128]{1,0:T(8,128)S(1)}, f32[4,128]{1,0:T(4,128)S(1)}, /*index=5*/f32[4,128]{1,0:T(4,128)S(1)}) custom-call(f32[6,6,384]{2,1,0:T(8,128)} %source_hbm.1, f32[6,6,384]{2,1,0:T(8,128)} %potential_hbm.1, s32[6,6,384]{2,1,0:T(8,128)} %map_hbm.1, ...), custom_call_target="tpu_custom_call" | custom-call | tf_op jit(solution)/shard_map/pallas_call | solution.py:40
  15.5 0.0 collective-permute-done.corner_ref
  15.5 0.0 collective-permute-done.1.below_ref
  15.5 0.0 collective-permute-done.2.beside_ref
  15.6 0.0 copy-done
  15.6 0.3 shard_map.78
  15.8 0.9 shard_map.79
  16.7 15.3 %all-to-all-start = ((f32[64,8,128]{2,1,0:T(8,128)}), f32[64,8,128]{2,1,0:T(8,128)S(1)}, u32[]{:S(2)}, u32[]{:S(2)}) async-start(f32[64,8,128]{2,1,0:T(8,128)} %get-tuple-element.41), calls=%async_computation | async-start | bytes 524288 | tf_op jit(solution)/shard_map/all_to_all | solution.py:387
  32.0 0.7 collective-permute-start.3
  32.7 5.3 %collective-permute-start.4 = (f32[112,128]{1,0:T(8,128)S(1)}, f32[112,128]{1,0:T(8,128)S(1)}, u32[]{:S(2)}, u32[]{:S(2)}) collective-permute-start(f32[112,128]{1,0:T(8,128)S(1)} %get-tuple-element.44), channel_id=1, source_target_pairs={{0,8},{8,0},{16,24},{24,16},{32,40},{40,32},{48,56},{56,48},{64,72... | collective-permute-start | bytes 172040 | tf_op jit(solution)/shard_map/ppermute | solution.py:420
  38.1 0.0 collective-permute-done.3.left_ref
  38.1 2.4 %collective-permute-done.4.right_ref = f32[112,128]{1,0:T(8,128)S(1)} collective-permute-done((f32[112,128]{1,0:T(8,128)S(1)}, f32[112,128]{1,0:T(8,128)S(1)}, u32[]{:S(2)}, u32[]{:S(2)}) %collective-permute-start.4) | collective-permute-done | bytes 57376 | tf_op jit(solution)/shard_map/ppermute | solution.py:420
  40.5 5.2 %all-to-all-done.gathered_ref = f32[64,8,128]{2,1,0:T(8,128)S(1)} async-done(((f32[64,8,128]{2,1,0:T(8,128)}), f32[64,8,128]{2,1,0:T(8,128)S(1)}, u32[]{:S(2)}, u32[]{:S(2)}) %all-to-all-start) | async-done | bytes 262176 | tf_op jit(solution)/shard_map/all_to_all | solution.py:387
  45.7 0.4 shard_map.80
  46.1 3.6 %collective-permute-start.5 = (f32[96,128]{1,0:T(8,128)S(1)}, f32[96,128]{1,0:T(8,128)S(1)}, u32[]{:S(2)}, u32[]{:S(2)}) collective-permute-start(f32[96,128]{1,0:T(8,128)S(1)} %get-tuple-element.47), channel_id=1, source_target_pairs={{1,2},{3,4},{5,6},{2,1},{4,3},{6,5},{9,10},{11,12},{13,14},{10,9},... | collective-permute-start | bytes 147464 | tf_op jit(solution)/shard_map/ppermute | solution.py:419
  49.8 1.9 %collective-permute-start.6 = (f32[96,128]{1,0:T(8,128)S(1)}, f32[96,128]{1,0:T(8,128)S(1)}, u32[]{:S(2)}, u32[]{:S(2)}) collective-permute-start(f32[96,128]{1,0:T(8,128)S(1)} %get-tuple-element.48), channel_id=1, source_target_pairs={{0,1},{1,0},{2,3},{3,2},{4,5},{5,4},{6,7},{7,6},{8,9},{9,8},{10,11... | collective-permute-start | bytes 147464 | tf_op jit(solution)/shard_map/ppermute | solution.py:420
  51.7 0.7 collective-permute-done.5.far_ref
  52.4 0.5 collective-permute-done.6.near_ref
  52.9 0.5 shard_map.81
  53.4 0.9 shard_map.82
  54.3 6.8 %all-to-all-start.1 = ((f32[64,8,128]{2,1,0:T(8,128)}), f32[64,8,128]{2,1,0:T(8,128)S(1)}, u32[]{:S(2)}, u32[]{:S(2)}) async-start(f32[64,8,128]{2,1,0:T(8,128)} %get-tuple-element.52), calls=%async_computation.1 | async-start | bytes 524288 | tf_op jit(solution)/shard_map/all_to_all | solution.py:387
  61.1 0.7 collective-permute-start.7
  61.8 5.3 %collective-permute-start.8 = (f32[56,128]{1,0:T(8,128)S(1)}, f32[56,128]{1,0:T(8,128)S(1)}, u32[]{:S(2)}, u32[]{:S(2)}) collective-permute-start(f32[56,128]{1,0:T(8,128)S(1)} %get-tuple-element.56), channel_id=1, source_target_pairs={{0,8},{8,0},{16,24},{24,16},{32,40},{40,32},{48,56},{56,48},{64,72... | collective-permute-start | bytes 86024 | tf_op jit(solution)/shard_map/ppermute | solution.py:420
  67.1 0.0 collective-permute-done.7.left_ref
  67.1 1.5 %collective-permute-done.8.right_ref = f32[56,128]{1,0:T(8,128)S(1)} collective-permute-done((f32[56,128]{1,0:T(8,128)S(1)}, f32[56,128]{1,0:T(8,128)S(1)}, u32[]{:S(2)}, u32[]{:S(2)}) %collective-permute-start.8) | collective-permute-done | bytes 28704 | tf_op jit(solution)/shard_map/ppermute | solution.py:420
  68.7 3.8 %all-to-all-done.1.gathered_ref = f32[64,8,128]{2,1,0:T(8,128)S(1)} async-done(((f32[64,8,128]{2,1,0:T(8,128)}), f32[64,8,128]{2,1,0:T(8,128)S(1)}, u32[]{:S(2)}, u32[]{:S(2)}) %all-to-all-start.1) | async-done | bytes 262176 | tf_op jit(solution)/shard_map/all_to_all | solution.py:387
  72.4 0.4 shard_map.83
  72.8 7.7 %collective-permute-start.9 = (f32[96,128]{1,0:T(8,128)S(1)}, f32[96,128]{1,0:T(8,128)S(1)}, u32[]{:S(2)}, u32[]{:S(2)}) collective-permute-start(f32[96,128]{1,0:T(8,128)S(1)} %get-tuple-element.60), channel_id=1, source_target_pairs={{1,2},{3,4},{5,6},{2,1},{4,3},{6,5},{9,10},{11,12},{13,14},{10,9},... | collective-permute-start | bytes 147464 | tf_op jit(solution)/shard_map/ppermute | solution.py:419
  80.6 1.9 %collective-permute-start.10 = (f32[96,128]{1,0:T(8,128)S(1)}, f32[96,128]{1,0:T(8,128)S(1)}, u32[]{:S(2)}, u32[]{:S(2)}) collective-permute-start(f32[96,128]{1,0:T(8,128)S(1)} %get-tuple-element.61), channel_id=1, source_target_pairs={{0,1},{1,0},{2,3},{3,2},{4,5},{5,4},{6,7},{7,6},{8,9},{9,8},{10,11... | collective-permute-start | bytes 147464 | tf_op jit(solution)/shard_map/ppermute | solution.py:420
  82.5 0.0 collective-permute-done.9.far_ref
  82.5 1.2 %collective-permute-done.10.near_ref = f32[96,128]{1,0:T(8,128)S(1)} collective-permute-done((f32[96,128]{1,0:T(8,128)S(1)}, f32[96,128]{1,0:T(8,128)S(1)}, u32[]{:S(2)}, u32[]{:S(2)}) %collective-permute-start.10) | collective-permute-done | bytes 49184 | tf_op jit(solution)/shard_map/ppermute | solution.py:420
  83.7 0.6 shard_map.84
  84.3 13.0 %all_to_all.20 = f32[32,1,128]{2,1,0:T(1,128)S(1)} all-to-all(f32[32,1,128]{2,1,0:T(1,128)S(1)} %get-tuple-element.62), channel_id=1, replica_groups={{0,16,32,48,64,80,96,112,128,144,160,176,192,208,224,240,256,272,288,30..., dimensions={0} | all-to-all | bytes 32768 | tf_op jit(solution)/shard_map/all_to_all | solution.py:441
  97.3 0.1 reduce_sum.9
  97.4 14.7 %all_to_all.21.dots_ref = f32[16,1,128]{2,1,0:T(1,128)S(1)} all-to-all(f32[16,1,128]{2,1,0:T(1,128)S(1)} %broadcast_in_dim.2), channel_id=1, replica_groups={{0,1,2,3,4,5,6,7,8,9,10,11,12,13,14,15},{16,17,18,19,20,21,22,23,24,25,..., dimensions={0} | all-to-all | bytes 16384 | tf_op jit(solution)/shard_map/all_to_all | solution.py:443
  112.1 1.1 shard_map.85
  (4 shorter events, 0.0 us)
Async XLA Ops:
  1.3 14.2 %collective-permute-start.1 = (s32[2,128]{1,0:T(2,128)S(1)}, s32[2,128]{1,0:T(2,128)S(1)}, u32[]{:S(2)}, u32[]{:S(2)}) collective-permute-start(s32[2,128]{1,0:T(2,128)S(1)} %bitcast.5), channel_id=1, source_target_pairs={{0,8},{8,16},{16,24},{24,32},{32,40},{40,48},{48,56},{56,64},{64,7... | collective-permute-start | bytes 3080 | tf_op jit(solution)/shard_map/ppermute | solution.py:384
  5.4 10.2 %collective-permute-start.2 = (s32[2,128]{1,0:T(2,128)S(1)}, s32[2,128]{1,0:T(2,128)S(1)}, u32[]{:S(2)}, u32[]{:S(2)}) collective-permute-start(s32[2,128]{1,0:T(2,128)S(1)} %slice_bitcast_fusion), channel_id=1, source_target_pairs={{0,1},{1,2},{2,3},{3,4},{4,5},{5,6},{6,7},{8,9},{9,10},{10,11},{11... | collective-permute-start | bytes 3080 | tf_op jit(solution)/shard_map/ppermute | solution.py:384
  10.4 5.1 %copy-start = (f32[64,64]{1,0:T(8,128)S(1)}, f32[64,64]{1,0:T(8,128)}, u32[]{:S(2)}) copy-start(f32[64,64]{1,0:T(8,128)} %matrix_ref.5) | copy-start | bytes 49156
  10.4 5.1 %collective-permute-start = (s32[1,128]{1,0:T(1,128)S(1)}, s32[1,128]{1,0:T(1,128)S(1)}, u32[]{:S(2)}, u32[]{:S(2)}) collective-permute-start(s32[1,128]{1,0:T(1,128)S(1)} %slice_bitcast_fusion.1), channel_id=1, source_target_pairs={{0,9},{1,10},{2,11},{3,12},{4,13},{5,14},{6,15},{8,17},{9,18},{10,... | collective-permute-start | bytes 1544 | tf_op jit(solution)/shard_map/ppermute | solution.py:397
  16.7 29.0 %all-to-all-start = ((f32[64,8,128]{2,1,0:T(8,128)}), f32[64,8,128]{2,1,0:T(8,128)S(1)}, u32[]{:S(2)}, u32[]{:S(2)}) async-start(f32[64,8,128]{2,1,0:T(8,128)} %get-tuple-element.41), calls=%async_computation | async-start | bytes 524288 | tf_op jit(solution)/shard_map/all_to_all | solution.py:387
  32.0 6.0 %collective-permute-start.3 = (f32[112,128]{1,0:T(8,128)S(1)}, f32[112,128]{1,0:T(8,128)S(1)}, u32[]{:S(2)}, u32[]{:S(2)}) collective-permute-start(f32[112,128]{1,0:T(8,128)S(1)} %get-tuple-element.43), channel_id=1, source_target_pairs={{8,16},{24,32},{40,48},{56,64},{72,80},{88,96},{104,112},{120,128}... | collective-permute-start | bytes 172040 | tf_op jit(solution)/shard_map/ppermute | solution.py:419
  32.7 7.8 %collective-permute-start.4 = (f32[112,128]{1,0:T(8,128)S(1)}, f32[112,128]{1,0:T(8,128)S(1)}, u32[]{:S(2)}, u32[]{:S(2)}) collective-permute-start(f32[112,128]{1,0:T(8,128)S(1)} %get-tuple-element.44), channel_id=1, source_target_pairs={{0,8},{8,0},{16,24},{24,16},{32,40},{40,32},{48,56},{56,48},{64,72... | collective-permute-start | bytes 172040 | tf_op jit(solution)/shard_map/ppermute | solution.py:420
  46.1 6.3 %collective-permute-start.5 = (f32[96,128]{1,0:T(8,128)S(1)}, f32[96,128]{1,0:T(8,128)S(1)}, u32[]{:S(2)}, u32[]{:S(2)}) collective-permute-start(f32[96,128]{1,0:T(8,128)S(1)} %get-tuple-element.47), channel_id=1, source_target_pairs={{1,2},{3,4},{5,6},{2,1},{4,3},{6,5},{9,10},{11,12},{13,14},{10,9},... | collective-permute-start | bytes 147464 | tf_op jit(solution)/shard_map/ppermute | solution.py:419
  49.8 3.1 %collective-permute-start.6 = (f32[96,128]{1,0:T(8,128)S(1)}, f32[96,128]{1,0:T(8,128)S(1)}, u32[]{:S(2)}, u32[]{:S(2)}) collective-permute-start(f32[96,128]{1,0:T(8,128)S(1)} %get-tuple-element.48), channel_id=1, source_target_pairs={{0,1},{1,0},{2,3},{3,2},{4,5},{5,4},{6,7},{7,6},{8,9},{9,8},{10,11... | collective-permute-start | bytes 147464 | tf_op jit(solution)/shard_map/ppermute | solution.py:420
  54.3 18.2 %all-to-all-start.1 = ((f32[64,8,128]{2,1,0:T(8,128)}), f32[64,8,128]{2,1,0:T(8,128)S(1)}, u32[]{:S(2)}, u32[]{:S(2)}) async-start(f32[64,8,128]{2,1,0:T(8,128)} %get-tuple-element.52), calls=%async_computation.1 | async-start | bytes 524288 | tf_op jit(solution)/shard_map/all_to_all | solution.py:387
  61.1 6.0 %collective-permute-start.7 = (f32[56,128]{1,0:T(8,128)S(1)}, f32[56,128]{1,0:T(8,128)S(1)}, u32[]{:S(2)}, u32[]{:S(2)}) collective-permute-start(f32[56,128]{1,0:T(8,128)S(1)} %get-tuple-element.55), channel_id=1, source_target_pairs={{8,16},{24,32},{40,48},{56,64},{72,80},{88,96},{104,112},{120,128}... | collective-permute-start | bytes 86024 | tf_op jit(solution)/shard_map/ppermute | solution.py:419
  61.8 6.9 %collective-permute-start.8 = (f32[56,128]{1,0:T(8,128)S(1)}, f32[56,128]{1,0:T(8,128)S(1)}, u32[]{:S(2)}, u32[]{:S(2)}) collective-permute-start(f32[56,128]{1,0:T(8,128)S(1)} %get-tuple-element.56), channel_id=1, source_target_pairs={{0,8},{8,0},{16,24},{24,16},{32,40},{40,32},{48,56},{56,48},{64,72... | collective-permute-start | bytes 86024 | tf_op jit(solution)/shard_map/ppermute | solution.py:420
  72.8 9.7 %collective-permute-start.9 = (f32[96,128]{1,0:T(8,128)S(1)}, f32[96,128]{1,0:T(8,128)S(1)}, u32[]{:S(2)}, u32[]{:S(2)}) collective-permute-start(f32[96,128]{1,0:T(8,128)S(1)} %get-tuple-element.60), channel_id=1, source_target_pairs={{1,2},{3,4},{5,6},{2,1},{4,3},{6,5},{9,10},{11,12},{13,14},{10,9},... | collective-permute-start | bytes 147464 | tf_op jit(solution)/shard_map/ppermute | solution.py:419
  80.6 3.1 %collective-permute-start.10 = (f32[96,128]{1,0:T(8,128)S(1)}, f32[96,128]{1,0:T(8,128)S(1)}, u32[]{:S(2)}, u32[]{:S(2)}) collective-permute-start(f32[96,128]{1,0:T(8,128)S(1)} %get-tuple-element.61), channel_id=1, source_target_pairs={{0,1},{1,0},{2,3},{3,2},{4,5},{5,4},{6,7},{7,6},{8,9},{9,8},{10,11... | collective-permute-start | bytes 147464 | tf_op jit(solution)/shard_map/ppermute | solution.py:420

commit v7 on v6

--- a/solution.py
+++ b/solution.py
@@ -67,11 +67,11 @@
     return field
 
 
-def assemble(product_of, total_ref):
+def assemble(product_of, limit, total_ref):
     total_ref[...] = jnp.zeros_like(total_ref)
     start = lanes((16, 128)) == 0
-    for i in SPAN:
-        low_a, high_a = {-1: (3, 4), 0: (0, 4), 1: (0, 3)}[i]
+    for i in range(-1, (limit + 2) // 3):
+        low_a, high_a = max(0, -3 * i), min(4, limit - 3 * i)
         for j in SPAN:
             product = product_of((i + 1) * 3 + j + 1)
             last = pltpu.roll(product[48:64], 1, 1)
@@ -151,18 +151,8 @@
     both_ref[1 - odd] = far_ref[...]
 
 
-def send_slab(odd, fields, near_ref, far_ref, both_ref):
-    both_ref[...] = jnp.zeros_like(both_ref)
-    for index, field_ref in enumerate(fields):
-        for n in range(18):
-            row = 56 * index + 3 * n
-            both_ref[0, row : row + 3, :] = field_ref[n, 3:6, :]
-            both_ref[1, 56 * index + n : 56 * index + n + 1, :] = field_ref[n, 0:1, :]
-    send(odd, both_ref, near_ref, far_ref)
-
-
-def diagonal_kernel(corner_ref, below_ref, beside_ref, own_ref, table_ref, matrix_ref, r_ref, ionic_ref, label_ref,
-                    sigma_ref, diagonal_ref, scaled_ref, near_ref, far_ref,
+def diagonal_kernel(corner_ref, below_ref, beside_ref, own_ref, table_ref, matrix_ref, r_ref, ionic_ref, label_ref, coarse_ref,
+                    sigma_ref, diagonal_ref, scaled_ref, message_ref, near_ref, far_ref,
                     total_ref, both_ref):
     sigma_ref[0:1, :] = conductance(corner_ref[...], table_ref)
     sigma_ref[1:3, :] = conductance(below_ref[...], table_ref)
@@ -172,26 +162,24 @@
     square = (64, 64)
     eye = lax.broadcasted_iota(jnp.int32, square, 0) == lax.broadcasted_iota(jnp.int32, square, 1)
     corner = jnp.sum(jnp.where(eye, matrix_ref[...], 0.0), axis=1, keepdims=True)
-    assemble(lambda e: corner * sigma_ref[e : e + 1, :], total_ref)
+    assemble(lambda e: corner * sigma_ref[e : e + 1, :], 6, total_ref)
     labels = label_ref[...]
     diagonal = jnp.where(labels == 0.0, 1.0, total_ref[...] + ionic_ref[...])
     diagonal_ref[...] = diagonal
+    even = lanes((8, 128)) % 2 == 0
+    message = jnp.where(even, coarse_ref[...], SHARE * restrict(diagonal, labels))
+    message_ref[...] = jnp.broadcast_to(message[None], message_ref.shape)
     scaled_ref[...] = r_ref[...] / diagonal
-    send_slab(parity("slab"), (scaled_ref, label_ref), near_ref, far_ref, both_ref)
-
-
-def first_message_kernel(diagonal_ref, label_ref, coarse_ref, held_ref, message_ref, near_ref):
-    labels = label_ref[...]
-    coarse_diag = SHARE * restrict(diagonal_ref[...], labels)
-    even = lanes((8, 128)) % 2 == 0
-    message = jnp.where(even, coarse_ref[...], coarse_diag)
-    message_ref[...] = jnp.broadcast_to(message[None], message_ref.shape)
-    near_ref[...] = held_ref[...]
-
-
-def next_message_kernel(q_ref, label_ref, held_ref, message_ref, near_ref):
-    message_ref[...] = jnp.broadcast_to(restrict(q_ref[...], label_ref[...])[None], message_ref.shape)
-    near_ref[...] = held_ref[...]
+    both_ref[...] = jnp.zeros_like(both_ref)
+    for n in range(18):
+        both_ref[0, 3 * n : 3 * n + 3, :] = scaled_ref[n, 3:6, :]
+        both_ref[0, 56 + 3 * n : 59 + 3 * n, :] = label_ref[n, 3:6, :]
+        both_ref[1, 4 * n : 4 * n + 4, :] = scaled_ref[n, 0:4, :]
+        both_ref[1, 72 + 4 * n : 76 + 4 * n, :] = label_ref[n, 0:4, :]
+        both_ref[1, 144 + n : 145 + n, :] = ionic_ref[n, 0:1, :]
+        both_ref[1, 162 + n : 163 + n, :] = diagonal_ref[n, 0:1, :]
+    both_ref[1, 180:183, :] = sigma_ref[3:6, :]
+    send(parity("slab"), both_ref, near_ref, far_ref)
 
 
 def along(values):
@@ -235,29 +223,29 @@
     return jnp.where(even, pltpu.roll(tiles, 127, tiles.ndim - 1), tiles)
 
 
-def widen(field_ref, both_ref, start, wide_ref):
+def widen(field_ref, both_ref, up_start, down_start, wide_ref):
     wide_ref[...] = jnp.zeros_like(wide_ref)
     for n in range(18):
-        wide_ref[n, 0:3, :] = both_ref[1, start + 3 * n : start + 3 * n + 3, :]
+        wide_ref[n, 0:3, :] = both_ref[1, up_start + 3 * n : up_start + 3 * n + 3, :]
         wide_ref[n, 3:9, :] = field_ref[n, 0:6, :]
-        wide_ref[n, 9:10, :] = both_ref[0, start + n : start + n + 1, :]
-
-
-def send_cross(odd, wide_ref, own_ref, near_ref, far_ref, both_ref):
+        wide_ref[n, 9:13, :] = both_ref[0, down_start + 4 * n : down_start + 4 * n + 4, :]
+
+
+def send_cross(odd, width, wide_ref, own_ref, near_ref, far_ref, both_ref):
     own_ref[...] = jnp.zeros_like(own_ref)
     for n in range(18):
         own_ref[n, 0:6, :] = wide_ref[n, 3:9, :]
     both_ref[...] = jnp.zeros_like(both_ref)
     for c in range(3):
         for y in range(3):
-            row = (3 * c + y) * 10
-            both_ref[0, row : row + 10, :] = wide_ref[6 * c + 3 + y, 0:10, :]
-        both_ref[1, 10 * c : 10 * c + 10, :] = wide_ref[6 * c, 0:10, :]
+            row = (3 * c + y) * width
+            both_ref[0, row : row + width, :] = wide_ref[6 * c + 3 + y, 0:width, :]
+        both_ref[1, width * c : width * c + width, :] = wide_ref[6 * c, 0:width, :]
     send(odd, both_ref, near_ref, far_ref)
 
 
 def first_solve_kernel(gathered_ref, scaled_ref, label_ref, left_ref, right_ref,
-                       wide_ref, z_ref, near_ref, far_ref, scale_ref, wide_label_ref, slab_ref, cross_ref):
+                       wide_ref, z_ref, near_ref, far_ref, scale_ref, wide_label_ref, edge_ref, slab_ref, cross_ref):
     receive(parity("slab"), right_ref, left_ref, slab_ref)
     rows, valid = around(gathered_ref.shape[0])
     tiles = jnp.concatenate([gathered_ref[pl.ds(row, 1)] for row in rows], 0)
@@ -268,41 +256,45 @@
     scale_ref[2 * NEAR + 1] = share
     level = smooth(DAMPING * even_part(tiles) * inverse, valid)
     coarse = level * inverse[REACH : REACH + 3] + (even_part(sums) * share)[None]
-    widen(label_ref, slab_ref, 56, wide_label_ref)
-    widen(scaled_ref, slab_ref, 0, wide_ref)
+    edge_ref[...] = slab_ref[0, 144:184, :]
+    widen(label_ref, slab_ref, 56, 72, wide_label_ref)
+    widen(scaled_ref, slab_ref, 0, 0, wide_ref)
     wide_ref[...] += prolong(coarse, wide_label_ref[...])
-    send_cross(parity("cross"), wide_ref, z_ref, near_ref, far_ref, cross_ref)
-
-
-def next_solve_kernel(gathered_ref, scaled_ref, wide_label_ref, left_ref, right_ref, scale_ref,
-                      wide_ref, w_ref, near_ref, far_ref, slab_ref, cross_ref):
-    receive(parity("slab"), right_ref, left_ref, slab_ref)
+    send_cross(parity("cross"), 13, wide_ref, z_ref, near_ref, far_ref, cross_ref)
+
+
+def next_solve_kernel(gathered_ref, scaled_ref, wide_label_ref, low_ref, scale_ref,
+                      wide_ref, w_ref, near_ref, far_ref, cross_ref):
     rows, valid = around(gathered_ref.shape[0])
     tiles = jnp.concatenate([gathered_ref[pl.ds(row, 1)] for row in rows], 0)
     sums = jnp.sum(gathered_ref[...], axis=0)
     inverse = scale_ref[0 : 2 * NEAR + 1]
     level = smooth(DAMPING * tiles * inverse, valid)
     coarse = level * inverse[REACH : REACH + 3] + (sums * scale_ref[2 * NEAR + 1])[None]
-    widen(scaled_ref, slab_ref, 0, wide_ref)
+    wide_ref[...] = jnp.zeros_like(wide_ref)
+    for n in range(18):
+        wide_ref[n, 0:3, :] = low_ref[3 * n : 3 * n + 3, :]
+        wide_ref[n, 3:10, :] = scaled_ref[n, 0:7, :]
     wide_ref[...] += prolong(coarse, wide_label_ref[...])
-    send_cross(parity("cross"), wide_ref, w_ref, near_ref, far_ref, cross_ref)
-
-
-def operate(wide_ref, field_ref, near_ref, far_ref, sigma_ref, matrix_ref, ionic_ref,
+    send_cross(parity("cross"), 10, wide_ref, w_ref, near_ref, far_ref, cross_ref)
+
+
+def operate(limit, wide_ref, near_ref, far_ref, sigma_ref, matrix_ref, ionic_ref,
             cross_ref, grid_ref, local_ref, product_ref, total_ref):
-    for n in range(18):
-        grid_ref[n // 6 * 10 + 3 + n % 6, 0:10, :] = wide_ref[n, 0:10, :]
-
+    columns = range(-1, (limit + 2) // 3)
+    width = 3 * len(columns) + 1
+    for n in range(18):
+        grid_ref[n // 6 * 10 + 3 + n % 6, 0:width, :] = wide_ref[n, 0:width, :]
     receive(parity("cross"), near_ref, far_ref, cross_ref)
     for c in range(3):
         for y in range(3):
-            row = (3 * c + y) * 10
-            grid_ref[10 * c + y, 0:10, :] = cross_ref[1, row : row + 10, :]
-        grid_ref[10 * c + 9, 0:10, :] = cross_ref[0, 10 * c : 10 * c + 10, :]
-    end = lanes((10, 128)) == 127
+            row = (3 * c + y) * width
+            grid_ref[10 * c + y, 0:width, :] = cross_ref[1, row : row + width, :]
+        grid_ref[10 * c + 9, 0:width, :] = cross_ref[0, width * c : width * c + width, :]
+    end = lanes((width, 128)) == 127
     for y in range(10):
-        grid_ref[30 + y, 0:10, :] = jnp.where(end, 0.0, pltpu.roll(grid_ref[y, 0:10, :], 127, 1))
-    for i in SPAN:
+        grid_ref[30 + y, 0:width, :] = jnp.where(end, 0.0, pltpu.roll(grid_ref[y, 0:width, :], 127, 1))
+    for i in columns:
         for j in SPAN:
             left = ((i + 1) * 3 + j + 1) * 128
             for c in range(4):
@@ -318,21 +310,36 @@
     low = (local - high.astype(F32)).astype(BF16)
     dot = functools.partial(jnp.dot, preferred_element_type=F32)
     product_ref[...] = dot(matrix_high, high) + (dot(matrix_high, low) + dot(matrix_low, high))
-    assemble(lambda e: product_ref[:, 128 * e : 128 * e + 128] * sigma_ref[e : e + 1, :], total_ref)
-    return total_ref[...] + ionic_ref[...] * field_ref[...]
-
-
-def first_image_kernel(wide_ref, z_ref, far_ref, near_ref, sigma_ref, matrix_ref, ionic_ref, diagonal_ref,
-                       q_ref, scaled_ref, left_ref, right_ref, both_ref, *scratch):
-    image = operate(wide_ref, z_ref, near_ref, far_ref, sigma_ref, matrix_ref, ionic_ref, *scratch)
+    assemble(lambda e: product_ref[:, 128 * e : 128 * e + 128] * sigma_ref[e : e + 1, :], limit, total_ref)
+    for n in range(18):
+        total_ref[n, 0:limit, :] += ionic_ref[n, 0:limit, :] * wide_ref[n, 3 : 3 + limit, :]
+
+
+def first_image_kernel(wide_ref, far_ref, near_ref, sigma_ref, matrix_ref, ionic_ref, diagonal_ref, label_ref, edge_ref,
+                       q_ref, scaled_ref, message_ref, up_ref,
+                       all_sigma_ref, all_ionic_ref, all_diagonal_ref, *scratch):
+    all_sigma_ref[0:9, :] = sigma_ref[...]
+    all_sigma_ref[9:12, :] = edge_ref[36:39, :]
+    all_ionic_ref[...] = ionic_ref[...]
+    all_diagonal_ref[...] = diagonal_ref[...]
+    for n in range(18):
+        all_ionic_ref[n, 6:7, :] = edge_ref[n : n + 1, :]
+        beyond = edge_ref[18 + n : 19 + n, :]
+        all_diagonal_ref[n, 6:7, :] = jnp.where(beyond == 0.0, jnp.inf, beyond)
+    operate(7, wide_ref, near_ref, far_ref, all_sigma_ref, matrix_ref, all_ionic_ref, *scratch)
+    image = scratch[-1][...]
     q_ref[...] = image
-    scaled_ref[...] = image / diagonal_ref[...]
-    send_slab(parity("slab"), (scaled_ref,), left_ref, right_ref, both_ref)
-
-
-def next_image_kernel(wide_ref, w_ref, far_ref, near_ref, sigma_ref, matrix_ref, ionic_ref,
-                      r_ref, z_ref, q_ref, t_ref, message_ref, *scratch):
-    image = operate(wide_ref, w_ref, near_ref, far_ref, sigma_ref, matrix_ref, ionic_ref, *scratch)
+    message_ref[...] = jnp.broadcast_to(restrict(image, label_ref[...])[None], message_ref.shape)
+    scaled_ref[...] = image / all_diagonal_ref[...]
+    up_ref[...] = jnp.zeros_like(up_ref)
+    for n in range(18):
+        up_ref[3 * n : 3 * n + 3, :] = scaled_ref[n, 3:6, :]
+
+
+def next_image_kernel(wide_ref, far_ref, near_ref, sigma_ref, matrix_ref, ionic_ref,
+                      w_ref, r_ref, z_ref, q_ref, t_ref, message_ref, *scratch):
+    operate(6, wide_ref, near_ref, far_ref, sigma_ref, matrix_ref, ionic_ref, *scratch)
+    image = scratch[-1][...]
     t_ref[...] = image
     r, z, q, w = r_ref[...], z_ref[...], q_ref[...], w_ref[...]
     row = jnp.zeros((1, 128), F32)
@@ -387,7 +394,10 @@
         return lax.all_to_all(copies, "slab", 0, 0, tiled=True)
 
     field, wide = (18, 8, 128), (18, 16, 128)
-    space = [(2, 96, 128), (40, 16, 128), (64, 1152), (64, 1152), field]
+
+    def space(columns, rows):
+        return [(2, rows, 128), (40, 16, 128), (64, 384 * columns), (64, 384 * columns), field]
+
     regions = region_labels + 1
     pairs = [
         (here * n_cross + beside, (here + 1) * n_cross + beside + 1)
@@ -403,13 +413,10 @@
          pltpu.VMEM((2, 2, 128), jnp.int32), pltpu.SMEM((4,), F32), pltpu.SemaphoreType.DMA((5,))],
         adjoint_source, potential, restriction_map, region_labels, conductivity, away=(0, 1, 2, 3, 4),
     )
-    sigma, diagonal, scaled, near, far = call(
-        diagonal_kernel, [(9, 128), field, field, (112, 128), (112, 128)],
-        [field, (2, 112, 128)],
-        corner, below, beside, own, table, element_matrix, r, ionic, labels,
-    )
-    message, near = call(
-        first_message_kernel, [(n_slab, 8, 128), (112, 128)], [], diagonal, labels, coarse, near
+    sigma, diagonal, scaled, message, near, far = call(
+        diagonal_kernel, [(9, 128), field, field, (n_slab, 8, 128), (184, 128), (184, 128)],
+        [field, (2, 184, 128)],
+        corner, below, beside, own, table, element_matrix, r, ionic, labels, coarse,
     )
 
     def exchange(near, far, axis):
@@ -419,24 +426,23 @@
         far = lax.ppermute(far, axis, far_pairs)
         return far, lax.ppermute(near, axis, [(c, c ^ 1) for c in range(count)])
 
-    faces = [(96, 128), (96, 128)]
-    wide_z, z, near, far, scale, wide_labels = call(
-        first_solve_kernel, [wide, field, *faces, (10, 8, 128), wide], [(2, 112, 128), (2, 96, 128)],
+    wide_z, z, near, far, scale, wide_labels, edge = call(
+        first_solve_kernel, [wide, field, (120, 128), (120, 128), (10, 8, 128), wide, (40, 128)],
+        [(2, 184, 128), (2, 120, 128)],
         gather(message), scaled, labels, *exchange(near, far, "slab"),
     )
-    q, scaled, near, far = call(
-        first_image_kernel, [field, field, (56, 128), (56, 128)],
-        [(2, 56, 128), *space],
-        wide_z, z, *exchange(near, far, "cross"), sigma, element_matrix, ionic, diagonal,
-    )
-    message, near = call(next_message_kernel, [(n_slab, 8, 128), (56, 128)], [], q, labels, near)
+    q, scaled, message, up = call(
+        first_image_kernel, [field, field, (n_slab, 8, 128), (56, 128)],
+        [(12, 128), field, field, *space(4, 120)],
+        wide_z, *exchange(near, far, "cross"), sigma, element_matrix, ionic, diagonal, labels, edge,
+    )
     wide_w, w, near, far = call(
-        next_solve_kernel, [wide, field, *faces], [(2, 56, 128), (2, 96, 128)],
-        gather(message), scaled, wide_labels, *exchange(near, far, "slab"), scale,
+        next_solve_kernel, [wide, field, (96, 128), (96, 128)], [(2, 96, 128)],
+        gather(message), scaled, wide_labels, shifted(up, "slab", 1), scale,
     )
     t, message = call(
-        next_image_kernel, [field, (n_slab // 2, 1, 128)], space,
-        wide_w, w, *exchange(near, far, "cross"), sigma, element_matrix, ionic, r, z, q,
+        next_image_kernel, [field, (n_slab // 2, 1, 128)], space(3, 96),
+        wide_w, *exchange(near, far, "cross"), sigma, element_matrix, ionic, w, r, z, q,
     )
     parts = lax.all_to_all(message, "slab", 0, 0, axis_index_groups=planes, tiled=True)
     parts = jnp.broadcast_to(jnp.sum(parts, 0)[None], (2 * n_cross, 1, 128))

time: 114 us -> 113 us (level)
  waiting for transfers between devices: 15.3 us -> 19.2 us
  starting transfers between devices: 62.1 us -> 58.6 us
    ppermute x4 -> x3, starting transfers between devices: 14.5 us -> 9.18 us  [exchange(): return (far, lax.ppermute(near, axis, [(c, c ^ 1) for c in range(count)]))]
    all_to_all x2, waiting for transfers between devices: 8.97 us -> 12.1 us  [gather(): return lax.all_to_all(copies, 'slab', 0, 0, tiled=True)]
    ppermute x2 -> x3, starting transfers between devices: 9.08 us -> 12 us  [shifted(): return lax.ppermute(value, axis, pairs)]
    all_to_all x1, blocking collectives: 13 us -> 11.8 us  [body(): lax.all_to_all(message, 'slab', 0, 0, axis_index_groups=planes, tiled=True)]
    ppermute x4 -> x3, starting transfers between devices: 12.7 us -> 11.7 us  [exchange(): far = lax.ppermute(far, axis, far_pairs)]
    ppermute x4 -> x3, waiting for transfers between devices: 5.59 us -> 5.33 us  [exchange(): return (far, lax.ppermute(near, axis, [(c, c ^ 1) for c in range(count)]))]
    pallas_call x9 -> x7, Pallas kernels: 6.44 us -> 6.48 us  [call(): pl.pallas_call(kernel, out_shape=[jax.ShapeDtypeStruct(shape, F32) for sh...]
  transfers between devices with their start and end apart: 13 -> 12, of which waited for: 7 -> 7; matrix products, arithmetic and copies ran while one was open for 0% -> 0% of each run, Pallas kernels for 1% -> 1%
where the time goes in v7:
time: 113 us
  starting transfers between devices  58.6 us (52%)
  blocking collectives  26.8 us (24%)
  waiting for transfers between devices  19.2 us (17%)
  Pallas kernels  6.48 us (6%)
    all_to_all x2, starting transfers between devices, gather(): return lax.all_to_all(copies, 'slab', 0, 0, tiled=True)  22.1 us
    all_to_all x1, blocking collectives, body(): lax.all_to_all(parts, ('slab', 'cross'), 0, 0, axis_index_groups=columns,...  15 us
    all_to_all x2, waiting for transfers between devices, gather(): return lax.all_to_all(copies, 'slab', 0, 0, tiled=True)  12.1 us
    ppermute x3, starting transfers between devices, shifted(): return lax.ppermute(value, axis, pairs)  12 us
    all_to_all x1, blocking collectives, body(): lax.all_to_all(message, 'slab', 0, 0, axis_index_groups=planes, tiled=True)  11.8 us
    ppermute x3, starting transfers between devices, exchange(): far = lax.ppermute(far, axis, far_pairs)  11.7 us
    ppermute x3, starting transfers between devices, exchange(): return (far, lax.ppermute(near, axis, [(c, c ^ 1) for c in range(count)]))  9.18 us
    pallas_call x7, Pallas kernels, call(): pl.pallas_call(kernel, out_shape=[jax.ShapeDtypeStruct(shape, F32) for sh...  6.48 us
  transfers between devices with their start and end apart: 12, of which 7 were waited for; matrix products, arithmetic and copies ran while one was open for 0% of the time, Pallas kernels for 1%

profile of v7, /device:TPU:1, one launch (start us, length us, event | category | flops | bytes accessed | tf_op | source)
XLA Modules:
  0.0 112.7 jit_solution(8542279800855068136)
XLA Ops:
  0.6 0.7 copy_add_fusion
  1.3 4.0 %collective-permute-start.1 = (s32[2,128]{1,0:T(2,128)S(1)}, s32[2,128]{1,0:T(2,128)S(1)}, u32[]{:S(2)}, u32[]{:S(2)}) collective-permute-start(s32[2,128]{1,0:T(2,128)S(1)} %bitcast.5), channel_id=1, source_target_pairs={{0,8},{8,16},{16,24},{24,32},{32,40},{40,48},{48,56},{56,64},{64,7... | collective-permute-start | bytes 3080 | tf_op jit(solution)/shard_map/ppermute | solution.py:391
  5.4 5.1 %collective-permute-start.2 = (s32[2,128]{1,0:T(2,128)S(1)}, s32[2,128]{1,0:T(2,128)S(1)}, u32[]{:S(2)}, u32[]{:S(2)}) collective-permute-start(s32[2,128]{1,0:T(2,128)S(1)} %slice_bitcast_fusion), channel_id=1, source_target_pairs={{0,1},{1,2},{2,3},{3,4},{4,5},{5,6},{6,7},{8,9},{9,10},{10,11},{11... | collective-permute-start | bytes 3080 | tf_op jit(solution)/shard_map/ppermute | solution.py:391
  10.4 3.6 %collective-permute-start = (s32[1,128]{1,0:T(1,128)S(1)}, s32[1,128]{1,0:T(1,128)S(1)}, u32[]{:S(2)}, u32[]{:S(2)}) collective-permute-start(s32[1,128]{1,0:T(1,128)S(1)} %slice_bitcast_fusion.1), channel_id=1, source_target_pairs={{0,9},{1,10},{2,11},{3,12},{4,13},{5,14},{6,15},{8,17},{9,18},{10,... | collective-permute-start | bytes 1544 | tf_op jit(solution)/shard_map/ppermute | solution.py:407
  14.1 0.0 copy-start
  14.1 1.4 %shard_map.77 = (f32[18,8,128]{2,1,0:T(8,128)S(1)}, f32[18,8,128]{2,1,0:T(8,128)S(1)}, f32[18,8,128]{2,1,0:T(8,128)S(1)}, f32[8,128]{1,0:T(8,128)S(1)}, f32[4,128]{1,0:T(4,128)S(1)}, /*index=5*/f32[4,128]{1,0:T(4,128)S(1)}) custom-call(f32[6,6,384]{2,1,0:T(8,128)} %source_hbm.1, f32[6,6,384]{2,1,0:T(8,128)} %potential_hbm.1, s32[6,6,384]{2,1,0:T(8,128)} %map_hbm.1, ...), custom_call_target="tpu_custom_call" | custom-call | tf_op jit(solution)/shard_map/pallas_call | solution.py:40
  15.5 0.0 collective-permute-done.corner_ref
  15.5 0.0 collective-permute-done.1.below_ref
  15.5 0.0 collective-permute-done.2.beside_ref
  15.6 0.0 copy-done
  15.6 1.1 shard_map.78
  16.7 15.3 %all-to-all-start = ((f32[64,8,128]{2,1,0:T(8,128)}), f32[64,8,128]{2,1,0:T(8,128)S(1)}, u32[]{:S(2)}, u32[]{:S(2)}) async-start(f32[64,8,128]{2,1,0:T(8,128)} %get-tuple-element.37), calls=%async_computation | async-start | bytes 524288 | tf_op jit(solution)/shard_map/all_to_all | solution.py:394
  32.0 0.7 collective-permute-start.3
  32.7 5.3 %collective-permute-start.4 = (f32[184,128]{1,0:T(8,128)S(1)}, f32[184,128]{1,0:T(8,128)S(1)}, u32[]{:S(2)}, u32[]{:S(2)}) collective-permute-start(f32[184,128]{1,0:T(8,128)S(1)} %get-tuple-element.40), channel_id=1, source_target_pairs={{0,8},{8,0},{16,24},{24,16},{32,40},{40,32},{48,56},{56,48},{64,72... | collective-permute-start | bytes 282632 | tf_op jit(solution)/shard_map/ppermute | solution.py:427
  38.0 0.0 collective-permute-done.3.left_ref
  38.0 3.8 %collective-permute-done.4.right_ref = f32[184,128]{1,0:T(8,128)S(1)} collective-permute-done((f32[184,128]{1,0:T(8,128)S(1)}, f32[184,128]{1,0:T(8,128)S(1)}, u32[]{:S(2)}, u32[]{:S(2)}) %collective-permute-start.4) | collective-permute-done | bytes 94240 | tf_op jit(solution)/shard_map/ppermute | solution.py:427
  41.8 4.6 %all-to-all-done.gathered_ref = f32[64,8,128]{2,1,0:T(8,128)S(1)} async-done(((f32[64,8,128]{2,1,0:T(8,128)}), f32[64,8,128]{2,1,0:T(8,128)S(1)}, u32[]{:S(2)}, u32[]{:S(2)}) %all-to-all-start) | async-done | bytes 262176 | tf_op jit(solution)/shard_map/all_to_all | solution.py:394
  46.5 0.5 shard_map.79
  46.9 3.6 %collective-permute-start.5 = (f32[120,128]{1,0:T(8,128)S(1)}, f32[120,128]{1,0:T(8,128)S(1)}, u32[]{:S(2)}, u32[]{:S(2)}) collective-permute-start(f32[120,128]{1,0:T(8,128)S(1)} %get-tuple-element.42), channel_id=1, source_target_pairs={{1,2},{3,4},{5,6},{2,1},{4,3},{6,5},{9,10},{11,12},{13,14},{10,9},... | collective-permute-start | bytes 184328 | tf_op jit(solution)/shard_map/ppermute | solution.py:426
  50.6 1.9 %collective-permute-start.6 = (f32[120,128]{1,0:T(8,128)S(1)}, f32[120,128]{1,0:T(8,128)S(1)}, u32[]{:S(2)}, u32[]{:S(2)}) collective-permute-start(f32[120,128]{1,0:T(8,128)S(1)} %get-tuple-element.43), channel_id=1, source_target_pairs={{0,1},{1,0},{2,3},{3,2},{4,5},{5,4},{6,7},{7,6},{8,9},{9,8},{10,11... | collective-permute-start | bytes 184328 | tf_op jit(solution)/shard_map/ppermute | solution.py:427
  52.5 0.9 collective-permute-done.5.far_ref
  53.4 0.4 collective-permute-done.6.near_ref
  53.7 1.4 %shard_map.80 = (f32[18,8,128]{2,1,0:T(8,128)S(1)}, f32[18,8,128]{2,1,0:T(8,128)S(1)}, f32[64,8,128]{2,1,0:T(8,128)}, f32[56,128]{1,0:T(8,128)S(1)}) custom-call(f32[18,16,128]{2,1,0:T(8,128)S(1)} %get-tuple-element.41.wide_ref, f32[120,128]{1,0:T(8,128)S(1)} %collective-permute-done.5.far_ref, f32[120,128]{1,0:T(8,128)S(1)} %collective-permute-done.6.near_ref, ...), custom_call_target="tpu_custom_call" | custom-call | tf_op jit(solution)/shard_map/pallas_call | solution.py:40
  55.1 6.8 %all-to-all-start.1 = ((f32[64,8,128]{2,1,0:T(8,128)}), f32[64,8,128]{2,1,0:T(8,128)S(1)}, u32[]{:S(2)}, u32[]{:S(2)}) async-start(f32[64,8,128]{2,1,0:T(8,128)} %get-tuple-element.47), calls=%async_computation.1 | async-start | bytes 524288 | tf_op jit(solution)/shard_map/all_to_all | solution.py:394
  61.9 2.9 %collective-permute-start.7 = (f32[56,128]{1,0:T(8,128)S(1)}, f32[56,128]{1,0:T(8,128)S(1)}, u32[]{:S(2)}, u32[]{:S(2)}) collective-permute-start(f32[56,128]{1,0:T(8,128)S(1)} %get-tuple-element.50), channel_id=1, source_target_pairs={{0,8},{8,16},{16,24},{24,32},{32,40},{40,48},{48,56},{56,64},{64,7... | collective-permute-start | bytes 86024 | tf_op jit(solution)/shard_map/ppermute | solution.py:391
  64.8 1.0 collective-permute-done.7.low_ref
  65.8 7.4 %all-to-all-done.1.gathered_ref = f32[64,8,128]{2,1,0:T(8,128)S(1)} async-done(((f32[64,8,128]{2,1,0:T(8,128)}), f32[64,8,128]{2,1,0:T(8,128)S(1)}, u32[]{:S(2)}, u32[]{:S(2)}) %all-to-all-start.1) | async-done | bytes 262176 | tf_op jit(solution)/shard_map/all_to_all | solution.py:394
  73.2 0.4 shard_map.81
  73.6 7.4 %collective-permute-start.8 = (f32[96,128]{1,0:T(8,128)S(1)}, f32[96,128]{1,0:T(8,128)S(1)}, u32[]{:S(2)}, u32[]{:S(2)}) collective-permute-start(f32[96,128]{1,0:T(8,128)S(1)} %get-tuple-element.53), channel_id=1, source_target_pairs={{1,2},{3,4},{5,6},{2,1},{4,3},{6,5},{9,10},{11,12},{13,14},{10,9},... | collective-permute-start | bytes 147464 | tf_op jit(solution)/shard_map/ppermute | solution.py:426
  81.0 1.9 %collective-permute-start.9 = (f32[96,128]{1,0:T(8,128)S(1)}, f32[96,128]{1,0:T(8,128)S(1)}, u32[]{:S(2)}, u32[]{:S(2)}) collective-permute-start(f32[96,128]{1,0:T(8,128)S(1)} %get-tuple-element.54), channel_id=1, source_target_pairs={{0,1},{1,0},{2,3},{3,2},{4,5},{5,4},{6,7},{7,6},{8,9},{9,8},{10,11... | collective-permute-start | bytes 147464 | tf_op jit(solution)/shard_map/ppermute | solution.py:427
  82.9 0.0 collective-permute-done.8.far_ref
  82.9 1.2 %collective-permute-done.9.near_ref = f32[96,128]{1,0:T(8,128)S(1)} collective-permute-done((f32[96,128]{1,0:T(8,128)S(1)}, f32[96,128]{1,0:T(8,128)S(1)}, u32[]{:S(2)}, u32[]{:S(2)}) %collective-permute-start.9) | collective-permute-done | bytes 49184 | tf_op jit(solution)/shard_map/ppermute | solution.py:427
  84.1 0.6 shard_map.82
  84.7 11.8 %all_to_all.20 = f32[32,1,128]{2,1,0:T(1,128)S(1)} all-to-all(f32[32,1,128]{2,1,0:T(1,128)S(1)} %get-tuple-element.58), channel_id=1, replica_groups={{0,16,32,48,64,80,96,112,128,144,160,176,192,208,224,240,256,272,288,30..., dimensions={0} | all-to-all | bytes 32768 | tf_op jit(solution)/shard_map/all_to_all | solution.py:447
  96.5 0.1 reduce_sum.9
  96.6 15.0 %all_to_all.21.dots_ref = f32[16,1,128]{2,1,0:T(1,128)S(1)} all-to-all(f32[16,1,128]{2,1,0:T(1,128)S(1)} %broadcast_in_dim.2), channel_id=1, replica_groups={{0,1,2,3,4,5,6,7,8,9,10,11,12,13,14,15},{16,17,18,19,20,21,22,23,24,25,..., dimensions={0} | all-to-all | bytes 16384 | tf_op jit(solution)/shard_map/all_to_all | solution.py:449
  111.6 1.1 shard_map.83
  (4 shorter events, 0.0 us)
Async XLA Ops:
  1.3 14.2 %collective-permute-start.1 = (s32[2,128]{1,0:T(2,128)S(1)}, s32[2,128]{1,0:T(2,128)S(1)}, u32[]{:S(2)}, u32[]{:S(2)}) collective-permute-start(s32[2,128]{1,0:T(2,128)S(1)} %bitcast.5), channel_id=1, source_target_pairs={{0,8},{8,16},{16,24},{24,32},{32,40},{40,48},{48,56},{56,64},{64,7... | collective-permute-start | bytes 3080 | tf_op jit(solution)/shard_map/ppermute | solution.py:391
  5.4 10.2 %collective-permute-start.2 = (s32[2,128]{1,0:T(2,128)S(1)}, s32[2,128]{1,0:T(2,128)S(1)}, u32[]{:S(2)}, u32[]{:S(2)}) collective-permute-start(s32[2,128]{1,0:T(2,128)S(1)} %slice_bitcast_fusion), channel_id=1, source_target_pairs={{0,1},{1,2},{2,3},{3,4},{4,5},{5,6},{6,7},{8,9},{9,10},{10,11},{11... | collective-permute-start | bytes 3080 | tf_op jit(solution)/shard_map/ppermute | solution.py:391
  10.4 5.1 %collective-permute-start = (s32[1,128]{1,0:T(1,128)S(1)}, s32[1,128]{1,0:T(1,128)S(1)}, u32[]{:S(2)}, u32[]{:S(2)}) collective-permute-start(s32[1,128]{1,0:T(1,128)S(1)} %slice_bitcast_fusion.1), channel_id=1, source_target_pairs={{0,9},{1,10},{2,11},{3,12},{4,13},{5,14},{6,15},{8,17},{9,18},{10,... | collective-permute-start | bytes 1544 | tf_op jit(solution)/shard_map/ppermute | solution.py:407
  14.1 1.5 %copy-start = (f32[64,64]{1,0:T(8,128)S(1)}, f32[64,64]{1,0:T(8,128)}, u32[]{:S(2)}) copy-start(f32[64,64]{1,0:T(8,128)} %matrix_ref.5) | copy-start | bytes 49156
  16.7 29.8 %all-to-all-start = ((f32[64,8,128]{2,1,0:T(8,128)}), f32[64,8,128]{2,1,0:T(8,128)S(1)}, u32[]{:S(2)}, u32[]{:S(2)}) async-start(f32[64,8,128]{2,1,0:T(8,128)} %get-tuple-element.37), calls=%async_computation | async-start | bytes 524288 | tf_op jit(solution)/shard_map/all_to_all | solution.py:394
  32.0 6.0 %collective-permute-start.3 = (f32[184,128]{1,0:T(8,128)S(1)}, f32[184,128]{1,0:T(8,128)S(1)}, u32[]{:S(2)}, u32[]{:S(2)}) collective-permute-start(f32[184,128]{1,0:T(8,128)S(1)} %get-tuple-element.39), channel_id=1, source_target_pairs={{8,16},{24,32},{40,48},{56,64},{72,80},{88,96},{104,112},{120,128}... | collective-permute-start | bytes 282632 | tf_op jit(solution)/shard_map/ppermute | solution.py:426
  32.7 9.1 %collective-permute-start.4 = (f32[184,128]{1,0:T(8,128)S(1)}, f32[184,128]{1,0:T(8,128)S(1)}, u32[]{:S(2)}, u32[]{:S(2)}) collective-permute-start(f32[184,128]{1,0:T(8,128)S(1)} %get-tuple-element.40), channel_id=1, source_target_pairs={{0,8},{8,0},{16,24},{24,16},{32,40},{40,32},{48,56},{56,48},{64,72... | collective-permute-start | bytes 282632 | tf_op jit(solution)/shard_map/ppermute | solution.py:427
  46.9 6.4 %collective-permute-start.5 = (f32[120,128]{1,0:T(8,128)S(1)}, f32[120,128]{1,0:T(8,128)S(1)}, u32[]{:S(2)}, u32[]{:S(2)}) collective-permute-start(f32[120,128]{1,0:T(8,128)S(1)} %get-tuple-element.42), channel_id=1, source_target_pairs={{1,2},{3,4},{5,6},{2,1},{4,3},{6,5},{9,10},{11,12},{13,14},{10,9},... | collective-permute-start | bytes 184328 | tf_op jit(solution)/shard_map/ppermute | solution.py:426
  50.6 3.1 %collective-permute-start.6 = (f32[120,128]{1,0:T(8,128)S(1)}, f32[120,128]{1,0:T(8,128)S(1)}, u32[]{:S(2)}, u32[]{:S(2)}) collective-permute-start(f32[120,128]{1,0:T(8,128)S(1)} %get-tuple-element.43), channel_id=1, source_target_pairs={{0,1},{1,0},{2,3},{3,2},{4,5},{5,4},{6,7},{7,6},{8,9},{9,8},{10,11... | collective-permute-start | bytes 184328 | tf_op jit(solution)/shard_map/ppermute | solution.py:427
  55.1 18.1 %all-to-all-start.1 = ((f32[64,8,128]{2,1,0:T(8,128)}), f32[64,8,128]{2,1,0:T(8,128)S(1)}, u32[]{:S(2)}, u32[]{:S(2)}) async-start(f32[64,8,128]{2,1,0:T(8,128)} %get-tuple-element.47), calls=%async_computation.1 | async-start | bytes 524288 | tf_op jit(solution)/shard_map/all_to_all | solution.py:394
  61.9 3.9 %collective-permute-start.7 = (f32[56,128]{1,0:T(8,128)S(1)}, f32[56,128]{1,0:T(8,128)S(1)}, u32[]{:S(2)}, u32[]{:S(2)}) collective-permute-start(f32[56,128]{1,0:T(8,128)S(1)} %get-tuple-element.50), channel_id=1, source_target_pairs={{0,8},{8,16},{16,24},{24,32},{32,40},{40,48},{48,56},{56,64},{64,7... | collective-permute-start | bytes 86024 | tf_op jit(solution)/shard_map/ppermute | solution.py:391
  73.6 9.3 %collective-permute-start.8 = (f32[96,128]{1,0:T(8,128)S(1)}, f32[96,128]{1,0:T(8,128)S(1)}, u32[]{:S(2)}, u32[]{:S(2)}) collective-permute-start(f32[96,128]{1,0:T(8,128)S(1)} %get-tuple-element.53), channel_id=1, source_target_pairs={{1,2},{3,4},{5,6},{2,1},{4,3},{6,5},{9,10},{11,12},{13,14},{10,9},... | collective-permute-start | bytes 147464 | tf_op jit(solution)/shard_map/ppermute | solution.py:426
  81.0 3.1 %collective-permute-start.9 = (f32[96,128]{1,0:T(8,128)S(1)}, f32[96,128]{1,0:T(8,128)S(1)}, u32[]{:S(2)}, u32[]{:S(2)}) collective-permute-start(f32[96,128]{1,0:T(8,128)S(1)} %get-tuple-element.54), channel_id=1, source_target_pairs={{0,1},{1,0},{2,3},{3,2},{4,5},{5,4},{6,7},{7,6},{8,9},{9,8},{10,11... | collective-permute-start | bytes 147464 | tf_op jit(solution)/shard_map/ppermute | solution.py:427

commit v8 on v7

--- a/solution.py
+++ b/solution.py
@@ -151,7 +151,7 @@
     both_ref[1 - odd] = far_ref[...]
 
 
-def diagonal_kernel(corner_ref, below_ref, beside_ref, own_ref, table_ref, matrix_ref, r_ref, ionic_ref, label_ref, coarse_ref,
+def diagonal_kernel(own_ref, corner_ref, below_ref, beside_ref, table_ref, matrix_ref, r_ref, ionic_ref, label_ref, coarse_ref,
                     sigma_ref, diagonal_ref, scaled_ref, message_ref, near_ref, far_ref,
                     total_ref, both_ref):
     sigma_ref[0:1, :] = conductance(corner_ref[...], table_ref)
@@ -182,6 +182,14 @@
     send(parity("slab"), both_ref, near_ref, far_ref)
 
 
+def halved(coarse):
+    return jnp.where(lanes((4, 128)) % 2 == 0, coarse[0:4], coarse[4:8])
+
+
+def restored(tiles):
+    return jnp.concatenate([even_part(tiles), odd_part(tiles)], tiles.ndim - 2)
+
+
 def along(values):
     lane = lanes(values.shape)
     row = lax.broadcasted_iota(jnp.int32, values.shape, 1)
@@ -267,7 +275,8 @@
                       wide_ref, w_ref, near_ref, far_ref, cross_ref):
     rows, valid = around(gathered_ref.shape[0])
     tiles = jnp.concatenate([gathered_ref[pl.ds(row, 1)] for row in rows], 0)
-    sums = jnp.sum(gathered_ref[...], axis=0)
+    tiles = restored(tiles)
+    sums = restored(jnp.sum(gathered_ref[...], axis=0))
     inverse = scale_ref[0 : 2 * NEAR + 1]
     level = smooth(DAMPING * tiles * inverse, valid)
     coarse = level * inverse[REACH : REACH + 3] + (sums * scale_ref[2 * NEAR + 1])[None]
@@ -329,7 +338,7 @@
     operate(7, wide_ref, near_ref, far_ref, all_sigma_ref, matrix_ref, all_ionic_ref, *scratch)
     image = scratch[-1][...]
     q_ref[...] = image
-    message_ref[...] = jnp.broadcast_to(restrict(image, label_ref[...])[None], message_ref.shape)
+    message_ref[...] = jnp.broadcast_to(halved(restrict(image, label_ref[...]))[None], message_ref.shape)
     scaled_ref[...] = image / all_diagonal_ref[...]
     up_ref[...] = jnp.zeros_like(up_ref)
     for n in range(18):
@@ -416,7 +425,7 @@
     sigma, diagonal, scaled, message, near, far = call(
         diagonal_kernel, [(9, 128), field, field, (n_slab, 8, 128), (184, 128), (184, 128)],
         [field, (2, 184, 128)],
-        corner, below, beside, own, table, element_matrix, r, ionic, labels, coarse,
+        own, corner, below, beside, table, element_matrix, r, ionic, labels, coarse,
     )
 
     def exchange(near, far, axis):
@@ -432,7 +441,7 @@
         gather(message), scaled, labels, *exchange(near, far, "slab"),
     )
     q, scaled, message, up = call(
-        first_image_kernel, [field, field, (n_slab, 8, 128), (56, 128)],
+        first_image_kernel, [field, field, (n_slab, 4, 128), (56, 128)],
         [(12, 128), field, field, *space(4, 120)],
         wide_z, *exchange(near, far, "cross"), sigma, element_matrix, ionic, diagonal, labels, edge,
     )

time: 113 us -> 113 us (level)
  blocking collectives: 26.8 us -> 30.3 us
  waiting for transfers between devices: 19.2 us -> 17.3 us
  starting transfers between devices: 58.6 us -> 57.1 us
    all_to_all x1, blocking collectives: 11.8 us -> 15.2 us  [body(): lax.all_to_all(message, 'slab', 0, 0, axis_index_groups=planes, tiled=True)]
    all_to_all x2, waiting for transfers between devices: 12.1 us -> 10.2 us  [gather(): return lax.all_to_all(copies, 'slab', 0, 0, tiled=True)]
    ppermute x3, starting transfers between devices: 11.7 us -> 10.1 us  [exchange(): far = lax.ppermute(far, axis, far_pairs)]
where the time goes in v8:
time: 113 us
  starting transfers between devices  57.1 us (51%)
  blocking collectives  30.3 us (27%)
  waiting for transfers between devices  17.3 us (15%)
  Pallas kernels  6.53 us (6%)
    all_to_all x2, starting transfers between devices, gather(): return lax.all_to_all(copies, 'slab', 0, 0, tiled=True)  22.1 us
    all_to_all x1, blocking collectives, body(): lax.all_to_all(message, 'slab', 0, 0, axis_index_groups=planes, tiled=True)  15.2 us
    all_to_all x1, blocking collectives, body(): lax.all_to_all(parts, ('slab', 'cross'), 0, 0, axis_index_groups=columns,...  15.1 us
    ppermute x3, starting transfers between devices, shifted(): return lax.ppermute(value, axis, pairs)  12 us
    all_to_all x2, waiting for transfers between devices, gather(): return lax.all_to_all(copies, 'slab', 0, 0, tiled=True)  10.2 us
    ppermute x3, starting transfers between devices, exchange(): far = lax.ppermute(far, axis, far_pairs)  10.1 us
    ppermute x3, starting transfers between devices, exchange(): return (far, lax.ppermute(near, axis, [(c, c ^ 1) for c in range(count)]))  9.18 us
    pallas_call x7, Pallas kernels, call(): pl.pallas_call(kernel, out_shape=[jax.ShapeDtypeStruct(shape, F32) for sh...  6.53 us
  transfers between devices with their start and end apart: 12, of which 7 were waited for; matrix products, arithmetic and copies ran while one was open for 0% of the time, Pallas kernels for 1%

profile of v8, /device:TPU:1, one launch (start us, length us, event | category | flops | bytes accessed | tf_op | source)
XLA Modules:
  0.0 112.8 jit_solution(5850536579315059409)
XLA Ops:
  0.6 0.7 copy_add_fusion
  1.3 4.0 %collective-permute-start.1 = (s32[2,128]{1,0:T(2,128)S(1)}, s32[2,128]{1,0:T(2,128)S(1)}, u32[]{:S(2)}, u32[]{:S(2)}) collective-permute-start(s32[2,128]{1,0:T(2,128)S(1)} %bitcast.5), channel_id=1, source_target_pairs={{0,8},{8,16},{16,24},{24,32},{32,40},{40,48},{48,56},{56,64},{64,7... | collective-permute-start | bytes 3080 | tf_op jit(solution)/shard_map/ppermute | solution.py:400
  5.4 5.1 %collective-permute-start.2 = (s32[2,128]{1,0:T(2,128)S(1)}, s32[2,128]{1,0:T(2,128)S(1)}, u32[]{:S(2)}, u32[]{:S(2)}) collective-permute-start(s32[2,128]{1,0:T(2,128)S(1)} %slice_bitcast_fusion), channel_id=1, source_target_pairs={{0,1},{1,2},{2,3},{3,4},{4,5},{5,6},{6,7},{8,9},{9,10},{10,11},{11... | collective-permute-start | bytes 3080 | tf_op jit(solution)/shard_map/ppermute | solution.py:400
  10.4 3.6 %collective-permute-start = (s32[1,128]{1,0:T(1,128)S(1)}, s32[1,128]{1,0:T(1,128)S(1)}, u32[]{:S(2)}, u32[]{:S(2)}) collective-permute-start(s32[1,128]{1,0:T(1,128)S(1)} %slice_bitcast_fusion.1), channel_id=1, source_target_pairs={{0,9},{1,10},{2,11},{3,12},{4,13},{5,14},{6,15},{8,17},{9,18},{10,... | collective-permute-start | bytes 1544 | tf_op jit(solution)/shard_map/ppermute | solution.py:416
  14.1 0.0 copy-start
  14.1 1.4 %shard_map.77 = (f32[18,8,128]{2,1,0:T(8,128)S(1)}, f32[18,8,128]{2,1,0:T(8,128)S(1)}, f32[18,8,128]{2,1,0:T(8,128)S(1)}, f32[8,128]{1,0:T(8,128)S(1)}, f32[4,128]{1,0:T(4,128)S(1)}, /*index=5*/f32[4,128]{1,0:T(4,128)S(1)}) custom-call(f32[6,6,384]{2,1,0:T(8,128)} %source_hbm.1, f32[6,6,384]{2,1,0:T(8,128)} %potential_hbm.1, s32[6,6,384]{2,1,0:T(8,128)} %map_hbm.1, ...), custom_call_target="tpu_custom_call" | custom-call | tf_op jit(solution)/shard_map/pallas_call | solution.py:40
  15.5 0.0 collective-permute-done.corner_ref
  15.5 0.0 collective-permute-done.1.below_ref
  15.5 0.0 collective-permute-done.2.beside_ref
  15.6 0.0 copy-done
  15.6 1.1 shard_map.78
  16.7 15.3 %all-to-all-start = ((f32[64,8,128]{2,1,0:T(8,128)}), f32[64,8,128]{2,1,0:T(8,128)S(1)}, u32[]{:S(2)}, u32[]{:S(2)}) async-start(f32[64,8,128]{2,1,0:T(8,128)} %get-tuple-element.37), calls=%async_computation | async-start | bytes 524288 | tf_op jit(solution)/shard_map/all_to_all | solution.py:403
  32.0 0.7 collective-permute-start.3
  32.7 5.3 %collective-permute-start.4 = (f32[184,128]{1,0:T(8,128)S(1)}, f32[184,128]{1,0:T(8,128)S(1)}, u32[]{:S(2)}, u32[]{:S(2)}) collective-permute-start(f32[184,128]{1,0:T(8,128)S(1)} %get-tuple-element.40), channel_id=1, source_target_pairs={{0,8},{8,0},{16,24},{24,16},{32,40},{40,32},{48,56},{56,48},{64,72... | collective-permute-start | bytes 282632 | tf_op jit(solution)/shard_map/ppermute | solution.py:436
  38.0 0.0 collective-permute-done.3.left_ref
  38.0 3.8 %collective-permute-done.4.right_ref = f32[184,128]{1,0:T(8,128)S(1)} collective-permute-done((f32[184,128]{1,0:T(8,128)S(1)}, f32[184,128]{1,0:T(8,128)S(1)}, u32[]{:S(2)}, u32[]{:S(2)}) %collective-permute-start.4) | collective-permute-done | bytes 94240 | tf_op jit(solution)/shard_map/ppermute | solution.py:436
  41.8 4.6 %all-to-all-done.gathered_ref = f32[64,8,128]{2,1,0:T(8,128)S(1)} async-done(((f32[64,8,128]{2,1,0:T(8,128)}), f32[64,8,128]{2,1,0:T(8,128)S(1)}, u32[]{:S(2)}, u32[]{:S(2)}) %all-to-all-start) | async-done | bytes 262176 | tf_op jit(solution)/shard_map/all_to_all | solution.py:403
  46.5 0.5 shard_map.79
  46.9 3.6 %collective-permute-start.5 = (f32[120,128]{1,0:T(8,128)S(1)}, f32[120,128]{1,0:T(8,128)S(1)}, u32[]{:S(2)}, u32[]{:S(2)}) collective-permute-start(f32[120,128]{1,0:T(8,128)S(1)} %get-tuple-element.42), channel_id=1, source_target_pairs={{1,2},{3,4},{5,6},{2,1},{4,3},{6,5},{9,10},{11,12},{13,14},{10,9},... | collective-permute-start | bytes 184328 | tf_op jit(solution)/shard_map/ppermute | solution.py:435
  50.6 1.9 %collective-permute-start.6 = (f32[120,128]{1,0:T(8,128)S(1)}, f32[120,128]{1,0:T(8,128)S(1)}, u32[]{:S(2)}, u32[]{:S(2)}) collective-permute-start(f32[120,128]{1,0:T(8,128)S(1)} %get-tuple-element.43), channel_id=1, source_target_pairs={{0,1},{1,0},{2,3},{3,2},{4,5},{5,4},{6,7},{7,6},{8,9},{9,8},{10,11... | collective-permute-start | bytes 184328 | tf_op jit(solution)/shard_map/ppermute | solution.py:436
  52.5 0.9 collective-permute-done.5.far_ref
  53.4 0.4 collective-permute-done.6.near_ref
  53.7 1.3 %shard_map.80 = (f32[18,8,128]{2,1,0:T(8,128)S(1)}, f32[18,8,128]{2,1,0:T(8,128)S(1)}, f32[64,4,128]{2,1,0:T(4,128)}, f32[56,128]{1,0:T(8,128)S(1)}) custom-call(f32[18,16,128]{2,1,0:T(8,128)S(1)} %get-tuple-element.41.wide_ref, f32[120,128]{1,0:T(8,128)S(1)} %collective-permute-done.5.far_ref, f32[120,128]{1,0:T(8,128)S(1)} %collective-permute-done.6.near_ref, ...), custom_call_target="tpu_custom_call" | custom-call | tf_op jit(solution)/shard_map/pallas_call | solution.py:40
  55.1 6.8 %all-to-all-start.1 = ((f32[64,4,128]{2,1,0:T(4,128)}), f32[64,4,128]{2,1,0:T(4,128)S(1)}, u32[]{:S(2)}, u32[]{:S(2)}) async-start(f32[64,4,128]{2,1,0:T(4,128)} %get-tuple-element.47), calls=%async_computation.1 | async-start | bytes 262144 | tf_op jit(solution)/shard_map/all_to_all | solution.py:403
  61.9 2.9 %collective-permute-start.7 = (f32[56,128]{1,0:T(8,128)S(1)}, f32[56,128]{1,0:T(8,128)S(1)}, u32[]{:S(2)}, u32[]{:S(2)}) collective-permute-start(f32[56,128]{1,0:T(8,128)S(1)} %get-tuple-element.50), channel_id=1, source_target_pairs={{0,8},{8,16},{16,24},{24,32},{32,40},{40,48},{48,56},{56,64},{64,7... | collective-permute-start | bytes 86024 | tf_op jit(solution)/shard_map/ppermute | solution.py:400
  64.8 1.0 collective-permute-done.7.low_ref
  65.8 5.5 %all-to-all-done.1.gathered_ref = f32[64,4,128]{2,1,0:T(4,128)S(1)} async-done(((f32[64,4,128]{2,1,0:T(4,128)}), f32[64,4,128]{2,1,0:T(4,128)S(1)}, u32[]{:S(2)}, u32[]{:S(2)}) %all-to-all-start.1) | async-done | bytes 131104 | tf_op jit(solution)/shard_map/all_to_all | solution.py:403
  71.3 0.4 shard_map.81
  71.8 5.8 %collective-permute-start.8 = (f32[96,128]{1,0:T(8,128)S(1)}, f32[96,128]{1,0:T(8,128)S(1)}, u32[]{:S(2)}, u32[]{:S(2)}) collective-permute-start(f32[96,128]{1,0:T(8,128)S(1)} %get-tuple-element.53), channel_id=1, source_target_pairs={{1,2},{3,4},{5,6},{2,1},{4,3},{6,5},{9,10},{11,12},{13,14},{10,9},... | collective-permute-start | bytes 147464 | tf_op jit(solution)/shard_map/ppermute | solution.py:435
  77.6 1.9 %collective-permute-start.9 = (f32[96,128]{1,0:T(8,128)S(1)}, f32[96,128]{1,0:T(8,128)S(1)}, u32[]{:S(2)}, u32[]{:S(2)}) collective-permute-start(f32[96,128]{1,0:T(8,128)S(1)} %get-tuple-element.54), channel_id=1, source_target_pairs={{0,1},{1,0},{2,3},{3,2},{4,5},{5,4},{6,7},{7,6},{8,9},{9,8},{10,11... | collective-permute-start | bytes 147464 | tf_op jit(solution)/shard_map/ppermute | solution.py:436
  79.5 0.0 collective-permute-done.8.far_ref
  79.5 1.2 %collective-permute-done.9.near_ref = f32[96,128]{1,0:T(8,128)S(1)} collective-permute-done((f32[96,128]{1,0:T(8,128)S(1)}, f32[96,128]{1,0:T(8,128)S(1)}, u32[]{:S(2)}, u32[]{:S(2)}) %collective-permute-start.9) | collective-permute-done | bytes 49184 | tf_op jit(solution)/shard_map/ppermute | solution.py:436
  80.7 0.6 shard_map.82
  81.3 15.2 %all_to_all.20 = f32[32,1,128]{2,1,0:T(1,128)S(1)} all-to-all(f32[32,1,128]{2,1,0:T(1,128)S(1)} %get-tuple-element.58), channel_id=1, replica_groups={{0,16,32,48,64,80,96,112,128,144,160,176,192,208,224,240,256,272,288,30..., dimensions={0} | all-to-all | bytes 32768 | tf_op jit(solution)/shard_map/all_to_all | solution.py:456
  96.5 0.1 reduce_sum.9
  96.6 15.1 %all_to_all.21.dots_ref = f32[16,1,128]{2,1,0:T(1,128)S(1)} all-to-all(f32[16,1,128]{2,1,0:T(1,128)S(1)} %broadcast_in_dim.2), channel_id=1, replica_groups={{0,1,2,3,4,5,6,7,8,9,10,11,12,13,14,15},{16,17,18,19,20,21,22,23,24,25,..., dimensions={0} | all-to-all | bytes 16384 | tf_op jit(solution)/shard_map/all_to_all | solution.py:458
  111.7 1.1 shard_map.83
  (4 shorter events, 0.0 us)
Async XLA Ops:
  1.3 14.2 %collective-permute-start.1 = (s32[2,128]{1,0:T(2,128)S(1)}, s32[2,128]{1,0:T(2,128)S(1)}, u32[]{:S(2)}, u32[]{:S(2)}) collective-permute-start(s32[2,128]{1,0:T(2,128)S(1)} %bitcast.5), channel_id=1, source_target_pairs={{0,8},{8,16},{16,24},{24,32},{32,40},{40,48},{48,56},{56,64},{64,7... | collective-permute-start | bytes 3080 | tf_op jit(solution)/shard_map/ppermute | solution.py:400
  5.4 10.2 %collective-permute-start.2 = (s32[2,128]{1,0:T(2,128)S(1)}, s32[2,128]{1,0:T(2,128)S(1)}, u32[]{:S(2)}, u32[]{:S(2)}) collective-permute-start(s32[2,128]{1,0:T(2,128)S(1)} %slice_bitcast_fusion), channel_id=1, source_target_pairs={{0,1},{1,2},{2,3},{3,4},{4,5},{5,6},{6,7},{8,9},{9,10},{10,11},{11... | collective-permute-start | bytes 3080 | tf_op jit(solution)/shard_map/ppermute | solution.py:400
  10.4 5.1 %collective-permute-start = (s32[1,128]{1,0:T(1,128)S(1)}, s32[1,128]{1,0:T(1,128)S(1)}, u32[]{:S(2)}, u32[]{:S(2)}) collective-permute-start(s32[1,128]{1,0:T(1,128)S(1)} %slice_bitcast_fusion.1), channel_id=1, source_target_pairs={{0,9},{1,10},{2,11},{3,12},{4,13},{5,14},{6,15},{8,17},{9,18},{10,... | collective-permute-start | bytes 1544 | tf_op jit(solution)/shard_map/ppermute | solution.py:416
  14.1 1.5 %copy-start = (f32[64,64]{1,0:T(8,128)S(1)}, f32[64,64]{1,0:T(8,128)}, u32[]{:S(2)}) copy-start(f32[64,64]{1,0:T(8,128)} %matrix_ref.5) | copy-start | bytes 49156
  16.7 29.8 %all-to-all-start = ((f32[64,8,128]{2,1,0:T(8,128)}), f32[64,8,128]{2,1,0:T(8,128)S(1)}, u32[]{:S(2)}, u32[]{:S(2)}) async-start(f32[64,8,128]{2,1,0:T(8,128)} %get-tuple-element.37), calls=%async_computation | async-start | bytes 524288 | tf_op jit(solution)/shard_map/all_to_all | solution.py:403
  32.0 6.0 %collective-permute-start.3 = (f32[184,128]{1,0:T(8,128)S(1)}, f32[184,128]{1,0:T(8,128)S(1)}, u32[]{:S(2)}, u32[]{:S(2)}) collective-permute-start(f32[184,128]{1,0:T(8,128)S(1)} %get-tuple-element.39), channel_id=1, source_target_pairs={{8,16},{24,32},{40,48},{56,64},{72,80},{88,96},{104,112},{120,128}... | collective-permute-start | bytes 282632 | tf_op jit(solution)/shard_map/ppermute | solution.py:435
  32.7 9.1 %collective-permute-start.4 = (f32[184,128]{1,0:T(8,128)S(1)}, f32[184,128]{1,0:T(8,128)S(1)}, u32[]{:S(2)}, u32[]{:S(2)}) collective-permute-start(f32[184,128]{1,0:T(8,128)S(1)} %get-tuple-element.40), channel_id=1, source_target_pairs={{0,8},{8,0},{16,24},{24,16},{32,40},{40,32},{48,56},{56,48},{64,72... | collective-permute-start | bytes 282632 | tf_op jit(solution)/shard_map/ppermute | solution.py:436
  46.9 6.4 %collective-permute-start.5 = (f32[120,128]{1,0:T(8,128)S(1)}, f32[120,128]{1,0:T(8,128)S(1)}, u32[]{:S(2)}, u32[]{:S(2)}) collective-permute-start(f32[120,128]{1,0:T(8,128)S(1)} %get-tuple-element.42), channel_id=1, source_target_pairs={{1,2},{3,4},{5,6},{2,1},{4,3},{6,5},{9,10},{11,12},{13,14},{10,9},... | collective-permute-start | bytes 184328 | tf_op jit(solution)/shard_map/ppermute | solution.py:435
  50.6 3.1 %collective-permute-start.6 = (f32[120,128]{1,0:T(8,128)S(1)}, f32[120,128]{1,0:T(8,128)S(1)}, u32[]{:S(2)}, u32[]{:S(2)}) collective-permute-start(f32[120,128]{1,0:T(8,128)S(1)} %get-tuple-element.43), channel_id=1, source_target_pairs={{0,1},{1,0},{2,3},{3,2},{4,5},{5,4},{6,7},{7,6},{8,9},{9,8},{10,11... | collective-permute-start | bytes 184328 | tf_op jit(solution)/shard_map/ppermute | solution.py:436
  55.1 16.2 %all-to-all-start.1 = ((f32[64,4,128]{2,1,0:T(4,128)}), f32[64,4,128]{2,1,0:T(4,128)S(1)}, u32[]{:S(2)}, u32[]{:S(2)}) async-start(f32[64,4,128]{2,1,0:T(4,128)} %get-tuple-element.47), calls=%async_computation.1 | async-start | bytes 262144 | tf_op jit(solution)/shard_map/all_to_all | solution.py:403
  61.9 3.9 %collective-permute-start.7 = (f32[56,128]{1,0:T(8,128)S(1)}, f32[56,128]{1,0:T(8,128)S(1)}, u32[]{:S(2)}, u32[]{:S(2)}) collective-permute-start(f32[56,128]{1,0:T(8,128)S(1)} %get-tuple-element.50), channel_id=1, source_target_pairs={{0,8},{8,16},{16,24},{24,32},{32,40},{40,48},{48,56},{56,64},{64,7... | collective-permute-start | bytes 86024 | tf_op jit(solution)/shard_map/ppermute | solution.py:400
  71.8 7.8 %collective-permute-start.8 = (f32[96,128]{1,0:T(8,128)S(1)}, f32[96,128]{1,0:T(8,128)S(1)}, u32[]{:S(2)}, u32[]{:S(2)}) collective-permute-start(f32[96,128]{1,0:T(8,128)S(1)} %get-tuple-element.53), channel_id=1, source_target_pairs={{1,2},{3,4},{5,6},{2,1},{4,3},{6,5},{9,10},{11,12},{13,14},{10,9},... | collective-permute-start | bytes 147464 | tf_op jit(solution)/shard_map/ppermute | solution.py:435
  77.6 3.1 %collective-permute-start.9 = (f32[96,128]{1,0:T(8,128)S(1)}, f32[96,128]{1,0:T(8,128)S(1)}, u32[]{:S(2)}, u32[]{:S(2)}) collective-permute-start(f32[96,128]{1,0:T(8,128)S(1)} %get-tuple-element.54), channel_id=1, source_target_pairs={{0,1},{1,0},{2,3},{3,2},{4,5},{5,4},{6,7},{7,6},{8,9},{9,8},{10,11... | collective-permute-start | bytes 147464 | tf_op jit(solution)/shard_map/ppermute | solution.py:436

commit v9 on v8

--- a/solution.py
+++ b/solution.py
@@ -154,7 +154,7 @@
 def diagonal_kernel(own_ref, corner_ref, below_ref, beside_ref, table_ref, matrix_ref, r_ref, ionic_ref, label_ref, coarse_ref,
                     sigma_ref, diagonal_ref, scaled_ref, message_ref, near_ref, far_ref,
                     total_ref, both_ref):
-    sigma_ref[0:1, :] = conductance(corner_ref[...], table_ref)
+    sigma_ref[0:1, :] = conductance(corner_ref[3:4, :], table_ref)
     sigma_ref[1:3, :] = conductance(below_ref[...], table_ref)
     for i in range(2):
         sigma_ref[3 + 3 * i : 4 + 3 * i, :] = conductance(beside_ref[i : i + 1, :], table_ref)
@@ -413,7 +413,7 @@
         for here in range(n_slab - 1)
         for beside in range(n_cross - 1)
     ]
-    corner = lax.ppermute(regions[1, 1:2], ("slab", "cross"), pairs)
+    corner = lax.ppermute(regions.reshape(4, 128), ("slab", "cross"), pairs)
     below = shifted(regions[1], "slab", 1)
     beside = shifted(regions[:, 1], "cross", 1)
     r, ionic, labels, coarse, own, table = call(

time: 113 us -> 112 us (level)
  waiting for transfers between devices: 17.3 us -> 16 us
    ppermute x3, starting transfers between devices: 10.1 us -> 14.5 us  [exchange(): far = lax.ppermute(far, axis, far_pairs)]
    all_to_all x2, starting transfers between devices: 22.1 us -> 18.2 us  [gather(): return lax.all_to_all(copies, 'slab', 0, 0, tiled=True)]
    ppermute x1, starting transfers between devices: 3.62 us -> 6.75 us  [body(): corner = lax.ppermute(regions.reshape(4, 128), ('slab', 'cross'), pairs)]
    ppermute x3, starting transfers between devices: 12 us -> 8.85 us  [shifted(): return lax.ppermute(value, axis, pairs)]
  transfers between devices with their start and end apart: 12 -> 12, of which waited for: 7 -> 6; matrix products, arithmetic and copies ran while one was open for 0% -> 0% of each run, Pallas kernels for 1% -> 1%
where the time goes in v9:
time: 112 us
  starting transfers between devices  57.5 us (51%)
  blocking collectives  30.2 us (27%)
  waiting for transfers between devices  16 us (14%)
  Pallas kernels  6.53 us (6%)
    all_to_all x2, starting transfers between devices, gather(): return lax.all_to_all(copies, 'slab', 0, 0, tiled=True)  18.2 us
    all_to_all x1, blocking collectives, body(): lax.all_to_all(message, 'slab', 0, 0, axis_index_groups=planes, tiled=True)  15.2 us
    all_to_all x1, blocking collectives, body(): lax.all_to_all(parts, ('slab', 'cross'), 0, 0, axis_index_groups=columns,...  15 us
    ppermute x3, starting transfers between devices, exchange(): far = lax.ppermute(far, axis, far_pairs)  14.5 us
    all_to_all x2, waiting for transfers between devices, gather(): return lax.all_to_all(copies, 'slab', 0, 0, tiled=True)  9.36 us
    ppermute x3, starting transfers between devices, exchange(): return (far, lax.ppermute(near, axis, [(c, c ^ 1) for c in range(count)]))  9.18 us
    ppermute x3, starting transfers between devices, shifted(): return lax.ppermute(value, axis, pairs)  8.85 us
    ppermute x1, starting transfers between devices, body(): corner = lax.ppermute(regions.reshape(4, 128), ('slab', 'cross'), pairs)  6.75 us
  transfers between devices with their start and end apart: 12, of which 6 were waited for; matrix products, arithmetic and copies ran while one was open for 0% of the time, Pallas kernels for 1%

profile of v9, /device:TPU:1, one launch (start us, length us, event | category | flops | bytes accessed | tf_op | source)
XLA Modules:
  0.0 111.8 jit_solution(6974480461745388864)
XLA Ops:
  0.6 0.7 copy_add_fusion
  1.3 4.0 %collective-permute-start.1 = (s32[2,128]{1,0:T(2,128)S(1)}, s32[2,128]{1,0:T(2,128)S(1)}, u32[]{:S(2)}, u32[]{:S(2)}) collective-permute-start(s32[2,128]{1,0:T(2,128)S(1)} %bitcast.5), channel_id=1, source_target_pairs={{0,8},{8,16},{16,24},{24,32},{32,40},{40,48},{48,56},{56,64},{64,7... | collective-permute-start | bytes 3080 | tf_op jit(solution)/shard_map/ppermute | solution.py:400
  5.4 6.8 %collective-permute-start = (s32[4,128]{1,0:T(4,128)S(1)}, s32[4,128]{1,0:T(4,128)S(1)}, u32[]{:S(2)}, u32[]{:S(2)}) collective-permute-start(s32[4,128]{1,0:T(4,128)S(1)} %bitcast.4), channel_id=1, source_target_pairs={{0,9},{1,10},{2,11},{3,12},{4,13},{5,14},{6,15},{8,17},{9,18},{10,... | collective-permute-start | bytes 6152 | tf_op jit(solution)/shard_map/ppermute | solution.py:416
  12.1 1.9 %collective-permute-start.2 = (s32[2,128]{1,0:T(2,128)S(1)}, s32[2,128]{1,0:T(2,128)S(1)}, u32[]{:S(2)}, u32[]{:S(2)}) collective-permute-start(s32[2,128]{1,0:T(2,128)S(1)} %slice_bitcast_fusion), channel_id=1, source_target_pairs={{0,1},{1,2},{2,3},{3,4},{4,5},{5,6},{6,7},{8,9},{9,10},{10,11},{11... | collective-permute-start | bytes 3080 | tf_op jit(solution)/shard_map/ppermute | solution.py:400
  14.1 0.0 copy-start
  14.1 1.4 %shard_map.77 = (f32[18,8,128]{2,1,0:T(8,128)S(1)}, f32[18,8,128]{2,1,0:T(8,128)S(1)}, f32[18,8,128]{2,1,0:T(8,128)S(1)}, f32[8,128]{1,0:T(8,128)S(1)}, f32[4,128]{1,0:T(4,128)S(1)}, /*index=5*/f32[4,128]{1,0:T(4,128)S(1)}) custom-call(f32[6,6,384]{2,1,0:T(8,128)} %source_hbm.1, f32[6,6,384]{2,1,0:T(8,128)} %potential_hbm.1, s32[6,6,384]{2,1,0:T(8,128)} %map_hbm.1, ...), custom_call_target="tpu_custom_call" | custom-call | tf_op jit(solution)/shard_map/pallas_call | solution.py:40
  15.5 0.0 collective-permute-done.1.below_ref
  15.5 0.0 collective-permute-done.2.beside_ref
  15.5 0.0 collective-permute-done.corner_ref
  15.6 0.0 copy-done
  15.6 1.1 shard_map.78
  16.7 13.3 %all-to-all-start = ((f32[64,8,128]{2,1,0:T(8,128)}), f32[64,8,128]{2,1,0:T(8,128)S(1)}, u32[]{:S(2)}, u32[]{:S(2)}) async-start(f32[64,8,128]{2,1,0:T(8,128)} %get-tuple-element.37), calls=%async_computation | async-start | bytes 524288 | tf_op jit(solution)/shard_map/all_to_all | solution.py:403
  30.0 0.7 collective-permute-start.3
  30.7 5.3 %collective-permute-start.4 = (f32[184,128]{1,0:T(8,128)S(1)}, f32[184,128]{1,0:T(8,128)S(1)}, u32[]{:S(2)}, u32[]{:S(2)}) collective-permute-start(f32[184,128]{1,0:T(8,128)S(1)} %get-tuple-element.40), channel_id=1, source_target_pairs={{0,8},{8,0},{16,24},{24,16},{32,40},{40,32},{48,56},{56,48},{64,72... | collective-permute-start | bytes 282632 | tf_op jit(solution)/shard_map/ppermute | solution.py:436
  36.0 0.0 collective-permute-done.3.left_ref
  36.0 3.2 %collective-permute-done.4.right_ref = f32[184,128]{1,0:T(8,128)S(1)} collective-permute-done((f32[184,128]{1,0:T(8,128)S(1)}, f32[184,128]{1,0:T(8,128)S(1)}, u32[]{:S(2)}, u32[]{:S(2)}) %collective-permute-start.4) | collective-permute-done | bytes 94240 | tf_op jit(solution)/shard_map/ppermute | solution.py:436
  39.3 3.8 %all-to-all-done.gathered_ref = f32[64,8,128]{2,1,0:T(8,128)S(1)} async-done(((f32[64,8,128]{2,1,0:T(8,128)}), f32[64,8,128]{2,1,0:T(8,128)S(1)}, u32[]{:S(2)}, u32[]{:S(2)}) %all-to-all-start) | async-done | bytes 262176 | tf_op jit(solution)/shard_map/all_to_all | solution.py:403
  43.1 0.5 shard_map.79
  43.6 7.4 %collective-permute-start.5 = (f32[120,128]{1,0:T(8,128)S(1)}, f32[120,128]{1,0:T(8,128)S(1)}, u32[]{:S(2)}, u32[]{:S(2)}) collective-permute-start(f32[120,128]{1,0:T(8,128)S(1)} %get-tuple-element.42), channel_id=1, source_target_pairs={{1,2},{3,4},{5,6},{2,1},{4,3},{6,5},{9,10},{11,12},{13,14},{10,9},... | collective-permute-start | bytes 184328 | tf_op jit(solution)/shard_map/ppermute | solution.py:435
  51.0 1.9 %collective-permute-start.6 = (f32[120,128]{1,0:T(8,128)S(1)}, f32[120,128]{1,0:T(8,128)S(1)}, u32[]{:S(2)}, u32[]{:S(2)}) collective-permute-start(f32[120,128]{1,0:T(8,128)S(1)} %get-tuple-element.43), channel_id=1, source_target_pairs={{0,1},{1,0},{2,3},{3,2},{4,5},{5,4},{6,7},{7,6},{8,9},{9,8},{10,11... | collective-permute-start | bytes 184328 | tf_op jit(solution)/shard_map/ppermute | solution.py:436
  52.9 0.0 collective-permute-done.5.far_ref
  52.9 1.2 %collective-permute-done.6.near_ref = f32[120,128]{1,0:T(8,128)S(1)} collective-permute-done((f32[120,128]{1,0:T(8,128)S(1)}, f32[120,128]{1,0:T(8,128)S(1)}, u32[]{:S(2)}, u32[]{:S(2)}) %collective-permute-start.6) | collective-permute-done | bytes 61472 | tf_op jit(solution)/shard_map/ppermute | solution.py:436
  54.1 1.3 %shard_map.80 = (f32[18,8,128]{2,1,0:T(8,128)S(1)}, f32[18,8,128]{2,1,0:T(8,128)S(1)}, f32[64,4,128]{2,1,0:T(4,128)}, f32[56,128]{1,0:T(8,128)S(1)}) custom-call(f32[18,16,128]{2,1,0:T(8,128)S(1)} %get-tuple-element.41.wide_ref, f32[120,128]{1,0:T(8,128)S(1)} %collective-permute-done.5.far_ref, f32[120,128]{1,0:T(8,128)S(1)} %collective-permute-done.6.near_ref, ...), custom_call_target="tpu_custom_call" | custom-call | tf_op jit(solution)/shard_map/pallas_call | solution.py:40
  55.4 4.9 %all-to-all-start.1 = ((f32[64,4,128]{2,1,0:T(4,128)}), f32[64,4,128]{2,1,0:T(4,128)S(1)}, u32[]{:S(2)}, u32[]{:S(2)}) async-start(f32[64,4,128]{2,1,0:T(4,128)} %get-tuple-element.47), calls=%async_computation.1 | async-start | bytes 262144 | tf_op jit(solution)/shard_map/all_to_all | solution.py:403
  60.4 2.9 %collective-permute-start.7 = (f32[56,128]{1,0:T(8,128)S(1)}, f32[56,128]{1,0:T(8,128)S(1)}, u32[]{:S(2)}, u32[]{:S(2)}) collective-permute-start(f32[56,128]{1,0:T(8,128)S(1)} %get-tuple-element.50), channel_id=1, source_target_pairs={{0,8},{8,16},{16,24},{24,32},{32,40},{40,48},{48,56},{56,64},{64,7... | collective-permute-start | bytes 86024 | tf_op jit(solution)/shard_map/ppermute | solution.py:400
  63.3 1.0 collective-permute-done.7.low_ref
  64.3 5.5 %all-to-all-done.1.gathered_ref = f32[64,4,128]{2,1,0:T(4,128)S(1)} async-done(((f32[64,4,128]{2,1,0:T(4,128)}), f32[64,4,128]{2,1,0:T(4,128)S(1)}, u32[]{:S(2)}, u32[]{:S(2)}) %all-to-all-start.1) | async-done | bytes 131104 | tf_op jit(solution)/shard_map/all_to_all | solution.py:403
  69.8 0.4 shard_map.81
  70.2 6.4 %collective-permute-start.8 = (f32[96,128]{1,0:T(8,128)S(1)}, f32[96,128]{1,0:T(8,128)S(1)}, u32[]{:S(2)}, u32[]{:S(2)}) collective-permute-start(f32[96,128]{1,0:T(8,128)S(1)} %get-tuple-element.53), channel_id=1, source_target_pairs={{1,2},{3,4},{5,6},{2,1},{4,3},{6,5},{9,10},{11,12},{13,14},{10,9},... | collective-permute-start | bytes 147464 | tf_op jit(solution)/shard_map/ppermute | solution.py:435
  76.7 1.9 %collective-permute-start.9 = (f32[96,128]{1,0:T(8,128)S(1)}, f32[96,128]{1,0:T(8,128)S(1)}, u32[]{:S(2)}, u32[]{:S(2)}) collective-permute-start(f32[96,128]{1,0:T(8,128)S(1)} %get-tuple-element.54), channel_id=1, source_target_pairs={{0,1},{1,0},{2,3},{3,2},{4,5},{5,4},{6,7},{7,6},{8,9},{9,8},{10,11... | collective-permute-start | bytes 147464 | tf_op jit(solution)/shard_map/ppermute | solution.py:436
  78.6 0.0 collective-permute-done.8.far_ref
  78.6 1.2 %collective-permute-done.9.near_ref = f32[96,128]{1,0:T(8,128)S(1)} collective-permute-done((f32[96,128]{1,0:T(8,128)S(1)}, f32[96,128]{1,0:T(8,128)S(1)}, u32[]{:S(2)}, u32[]{:S(2)}) %collective-permute-start.9) | collective-permute-done | bytes 49184 | tf_op jit(solution)/shard_map/ppermute | solution.py:436
  79.8 0.6 shard_map.82
  80.4 15.2 %all_to_all.20 = f32[32,1,128]{2,1,0:T(1,128)S(1)} all-to-all(f32[32,1,128]{2,1,0:T(1,128)S(1)} %get-tuple-element.58), channel_id=1, replica_groups={{0,16,32,48,64,80,96,112,128,144,160,176,192,208,224,240,256,272,288,30..., dimensions={0} | all-to-all | bytes 32768 | tf_op jit(solution)/shard_map/all_to_all | solution.py:456
  95.7 0.1 reduce_sum.9
  95.7 15.0 %all_to_all.21.dots_ref = f32[16,1,128]{2,1,0:T(1,128)S(1)} all-to-all(f32[16,1,128]{2,1,0:T(1,128)S(1)} %broadcast_in_dim.2), channel_id=1, replica_groups={{0,1,2,3,4,5,6,7,8,9,10,11,12,13,14,15},{16,17,18,19,20,21,22,23,24,25,..., dimensions={0} | all-to-all | bytes 16384 | tf_op jit(solution)/shard_map/all_to_all | solution.py:458
  110.7 1.1 shard_map.83
  (4 shorter events, 0.0 us)
Async XLA Ops:
  1.3 14.2 %collective-permute-start.1 = (s32[2,128]{1,0:T(2,128)S(1)}, s32[2,128]{1,0:T(2,128)S(1)}, u32[]{:S(2)}, u32[]{:S(2)}) collective-permute-start(s32[2,128]{1,0:T(2,128)S(1)} %bitcast.5), channel_id=1, source_target_pairs={{0,8},{8,16},{16,24},{24,32},{32,40},{40,48},{48,56},{56,64},{64,7... | collective-permute-start | bytes 3080 | tf_op jit(solution)/shard_map/ppermute | solution.py:400
  5.4 10.2 %collective-permute-start = (s32[4,128]{1,0:T(4,128)S(1)}, s32[4,128]{1,0:T(4,128)S(1)}, u32[]{:S(2)}, u32[]{:S(2)}) collective-permute-start(s32[4,128]{1,0:T(4,128)S(1)} %bitcast.4), channel_id=1, source_target_pairs={{0,9},{1,10},{2,11},{3,12},{4,13},{5,14},{6,15},{8,17},{9,18},{10,... | collective-permute-start | bytes 6152 | tf_op jit(solution)/shard_map/ppermute | solution.py:416
  12.1 3.4 %collective-permute-start.2 = (s32[2,128]{1,0:T(2,128)S(1)}, s32[2,128]{1,0:T(2,128)S(1)}, u32[]{:S(2)}, u32[]{:S(2)}) collective-permute-start(s32[2,128]{1,0:T(2,128)S(1)} %slice_bitcast_fusion), channel_id=1, source_target_pairs={{0,1},{1,2},{2,3},{3,4},{4,5},{5,6},{6,7},{8,9},{9,10},{10,11},{11... | collective-permute-start | bytes 3080 | tf_op jit(solution)/shard_map/ppermute | solution.py:400
  14.1 1.5 %copy-start = (f32[64,64]{1,0:T(8,128)S(1)}, f32[64,64]{1,0:T(8,128)}, u32[]{:S(2)}) copy-start(f32[64,64]{1,0:T(8,128)} %matrix_ref.5) | copy-start | bytes 49156
  16.7 26.5 %all-to-all-start = ((f32[64,8,128]{2,1,0:T(8,128)}), f32[64,8,128]{2,1,0:T(8,128)S(1)}, u32[]{:S(2)}, u32[]{:S(2)}) async-start(f32[64,8,128]{2,1,0:T(8,128)} %get-tuple-element.37), calls=%async_computation | async-start | bytes 524288 | tf_op jit(solution)/shard_map/all_to_all | solution.py:403
  30.0 6.0 %collective-permute-start.3 = (f32[184,128]{1,0:T(8,128)S(1)}, f32[184,128]{1,0:T(8,128)S(1)}, u32[]{:S(2)}, u32[]{:S(2)}) collective-permute-start(f32[184,128]{1,0:T(8,128)S(1)} %get-tuple-element.39), channel_id=1, source_target_pairs={{8,16},{24,32},{40,48},{56,64},{72,80},{88,96},{104,112},{120,128}... | collective-permute-start | bytes 282632 | tf_op jit(solution)/shard_map/ppermute | solution.py:435
  30.7 8.6 %collective-permute-start.4 = (f32[184,128]{1,0:T(8,128)S(1)}, f32[184,128]{1,0:T(8,128)S(1)}, u32[]{:S(2)}, u32[]{:S(2)}) collective-permute-start(f32[184,128]{1,0:T(8,128)S(1)} %get-tuple-element.40), channel_id=1, source_target_pairs={{0,8},{8,0},{16,24},{24,16},{32,40},{40,32},{48,56},{56,48},{64,72... | collective-permute-start | bytes 282632 | tf_op jit(solution)/shard_map/ppermute | solution.py:436
  43.6 9.3 %collective-permute-start.5 = (f32[120,128]{1,0:T(8,128)S(1)}, f32[120,128]{1,0:T(8,128)S(1)}, u32[]{:S(2)}, u32[]{:S(2)}) collective-permute-start(f32[120,128]{1,0:T(8,128)S(1)} %get-tuple-element.42), channel_id=1, source_target_pairs={{1,2},{3,4},{5,6},{2,1},{4,3},{6,5},{9,10},{11,12},{13,14},{10,9},... | collective-permute-start | bytes 184328 | tf_op jit(solution)/shard_map/ppermute | solution.py:435
  51.0 3.1 %collective-permute-start.6 = (f32[120,128]{1,0:T(8,128)S(1)}, f32[120,128]{1,0:T(8,128)S(1)}, u32[]{:S(2)}, u32[]{:S(2)}) collective-permute-start(f32[120,128]{1,0:T(8,128)S(1)} %get-tuple-element.43), channel_id=1, source_target_pairs={{0,1},{1,0},{2,3},{3,2},{4,5},{5,4},{6,7},{7,6},{8,9},{9,8},{10,11... | collective-permute-start | bytes 184328 | tf_op jit(solution)/shard_map/ppermute | solution.py:436
  55.4 14.3 %all-to-all-start.1 = ((f32[64,4,128]{2,1,0:T(4,128)}), f32[64,4,128]{2,1,0:T(4,128)S(1)}, u32[]{:S(2)}, u32[]{:S(2)}) async-start(f32[64,4,128]{2,1,0:T(4,128)} %get-tuple-element.47), calls=%async_computation.1 | async-start | bytes 262144 | tf_op jit(solution)/shard_map/all_to_all | solution.py:403
  60.4 3.9 %collective-permute-start.7 = (f32[56,128]{1,0:T(8,128)S(1)}, f32[56,128]{1,0:T(8,128)S(1)}, u32[]{:S(2)}, u32[]{:S(2)}) collective-permute-start(f32[56,128]{1,0:T(8,128)S(1)} %get-tuple-element.50), channel_id=1, source_target_pairs={{0,8},{8,16},{16,24},{24,32},{32,40},{40,48},{48,56},{56,64},{64,7... | collective-permute-start | bytes 86024 | tf_op jit(solution)/shard_map/ppermute | solution.py:400
  70.2 8.4 %collective-permute-start.8 = (f32[96,128]{1,0:T(8,128)S(1)}, f32[96,128]{1,0:T(8,128)S(1)}, u32[]{:S(2)}, u32[]{:S(2)}) collective-permute-start(f32[96,128]{1,0:T(8,128)S(1)} %get-tuple-element.53), channel_id=1, source_target_pairs={{1,2},{3,4},{5,6},{2,1},{4,3},{6,5},{9,10},{11,12},{13,14},{10,9},... | collective-permute-start | bytes 147464 | tf_op jit(solution)/shard_map/ppermute | solution.py:435
  76.7 3.1 %collective-permute-start.9 = (f32[96,128]{1,0:T(8,128)S(1)}, f32[96,128]{1,0:T(8,128)S(1)}, u32[]{:S(2)}, u32[]{:S(2)}) collective-permute-start(f32[96,128]{1,0:T(8,128)S(1)} %get-tuple-element.54), channel_id=1, source_target_pairs={{0,1},{1,0},{2,3},{3,2},{4,5},{5,4},{6,7},{7,6},{8,9},{9,8},{10,11... | collective-permute-start | bytes 147464 | tf_op jit(solution)/shard_map/ppermute | solution.py:436

commit v10 on v9

--- a/solution.py
+++ b/solution.py
@@ -450,12 +450,12 @@
         gather(message), scaled, wide_labels, shifted(up, "slab", 1), scale,
     )
     t, message = call(
-        next_image_kernel, [field, (n_slab // 2, 1, 128)], space(3, 96),
+        next_image_kernel, [field, (2 * n_cross, 1, 128)], space(3, 96),
         wide_w, *exchange(near, far, "cross"), sigma, element_matrix, ionic, w, r, z, q,
     )
-    parts = lax.all_to_all(message, "slab", 0, 0, axis_index_groups=planes, tiled=True)
-    parts = jnp.broadcast_to(jnp.sum(parts, 0)[None], (2 * n_cross, 1, 128))
-    dots = lax.all_to_all(parts, ("slab", "cross"), 0, 0, axis_index_groups=columns, tiled=True)
+    parts = lax.all_to_all(message, ("slab", "cross"), 0, 0, axis_index_groups=columns, tiled=True)
+    parts = jnp.broadcast_to(jnp.sum(parts, 0)[None], (n_slab // 2, 1, 128))
+    dots = lax.all_to_all(parts, "slab", 0, 0, axis_index_groups=planes, tiled=True)
     return tuple(call(finish_kernel, [(6, 6, 384)] * 2, [(128, 128), (384, 128)], dots, r, z, q, w, t))
 
 

time: 112 us -> 111 us (level)
  blocking collectives: 30.2 us -> 28.8 us
    all_to_all x2, blocking collectives: 30.2 us -> 28.8 us  [the longest x1 14.9 us: body(): lax.all_to_all(parts, 'slab', 0, 0, axis_index_groups=planes, tiled=True)]
where the time goes in v10:
time: 111 us; the launch traced here: 110 us
  starting transfers between devices  57.5 us (52%)
  blocking collectives  28.8 us (26%)
  waiting for transfers between devices  16 us (14%)
  Pallas kernels  6.54 us (6%)
    all_to_all x2, starting transfers between devices, gather(): return lax.all_to_all(copies, 'slab', 0, 0, tiled=True)  18.2 us
    all_to_all x1, blocking collectives, body(): lax.all_to_all(parts, 'slab', 0, 0, axis_index_groups=planes, tiled=True)  14.9 us
    ppermute x3, starting transfers between devices, exchange(): far = lax.ppermute(far, axis, far_pairs)  14.5 us
    all_to_all x1, blocking collectives, body(): lax.all_to_all(message, ('slab', 'cross'), 0, 0, axis_index_groups=column...  13.9 us
    all_to_all x2, waiting for transfers between devices, gather(): return lax.all_to_all(copies, 'slab', 0, 0, tiled=True)  9.36 us
    ppermute x3, starting transfers between devices, exchange(): return (far, lax.ppermute(near, axis, [(c, c ^ 1) for c in range(count)]))  9.18 us
    ppermute x3, starting transfers between devices, shifted(): return lax.ppermute(value, axis, pairs)  8.85 us
    ppermute x1, starting transfers between devices, body(): corner = lax.ppermute(regions.reshape(4, 128), ('slab', 'cross'), pairs)  6.75 us
  transfers between devices with their start and end apart: 12, of which 6 were waited for; matrix products, arithmetic and copies ran while one was open for 0% of the time, Pallas kernels for 1%

profile of v10, /device:TPU:1, one launch (start us, length us, event | category | flops | bytes accessed | tf_op | source)
XLA Modules:
  0.0 110.4 jit_solution(2586287438247408416)
XLA Ops:
  0.6 0.7 copy_add_fusion
  1.3 4.0 %collective-permute-start.1 = (s32[2,128]{1,0:T(2,128)S(1)}, s32[2,128]{1,0:T(2,128)S(1)}, u32[]{:S(2)}, u32[]{:S(2)}) collective-permute-start(s32[2,128]{1,0:T(2,128)S(1)} %bitcast.5), channel_id=1, source_target_pairs={{0,8},{8,16},{16,24},{24,32},{32,40},{40,48},{48,56},{56,64},{64,7... | collective-permute-start | bytes 3080 | tf_op jit(solution)/shard_map/ppermute | solution.py:400
  5.4 6.8 %collective-permute-start = (s32[4,128]{1,0:T(4,128)S(1)}, s32[4,128]{1,0:T(4,128)S(1)}, u32[]{:S(2)}, u32[]{:S(2)}) collective-permute-start(s32[4,128]{1,0:T(4,128)S(1)} %bitcast.4), channel_id=1, source_target_pairs={{0,9},{1,10},{2,11},{3,12},{4,13},{5,14},{6,15},{8,17},{9,18},{10,... | collective-permute-start | bytes 6152 | tf_op jit(solution)/shard_map/ppermute | solution.py:416
  12.1 1.9 %collective-permute-start.2 = (s32[2,128]{1,0:T(2,128)S(1)}, s32[2,128]{1,0:T(2,128)S(1)}, u32[]{:S(2)}, u32[]{:S(2)}) collective-permute-start(s32[2,128]{1,0:T(2,128)S(1)} %slice_bitcast_fusion), channel_id=1, source_target_pairs={{0,1},{1,2},{2,3},{3,4},{4,5},{5,6},{6,7},{8,9},{9,10},{10,11},{11... | collective-permute-start | bytes 3080 | tf_op jit(solution)/shard_map/ppermute | solution.py:400
  14.1 0.0 copy-start
  14.1 1.4 %shard_map.77 = (f32[18,8,128]{2,1,0:T(8,128)S(1)}, f32[18,8,128]{2,1,0:T(8,128)S(1)}, f32[18,8,128]{2,1,0:T(8,128)S(1)}, f32[8,128]{1,0:T(8,128)S(1)}, f32[4,128]{1,0:T(4,128)S(1)}, /*index=5*/f32[4,128]{1,0:T(4,128)S(1)}) custom-call(f32[6,6,384]{2,1,0:T(8,128)} %source_hbm.1, f32[6,6,384]{2,1,0:T(8,128)} %potential_hbm.1, s32[6,6,384]{2,1,0:T(8,128)} %map_hbm.1, ...), custom_call_target="tpu_custom_call" | custom-call | tf_op jit(solution)/shard_map/pallas_call | solution.py:40
  15.5 0.0 collective-permute-done.1.below_ref
  15.5 0.0 collective-permute-done.2.beside_ref
  15.5 0.0 collective-permute-done.corner_ref
  15.6 0.0 copy-done
  15.6 1.1 %shard_map.78 = (f32[9,128]{1,0:T(8,128)S(1)}, f32[18,8,128]{2,1,0:T(8,128)S(1)}, f32[18,8,128]{2,1,0:T(8,128)S(1)}, f32[64,8,128]{2,1,0:T(8,128)}, f32[184,128]{1,0:T(8,128)S(1)}, /*index=5*/f32[184,128]{1,0:T(8,128)S(1)}) custom-call(f32[4,128]{1,0:T(4,128)S(1)} %get-tuple-element.31.own_ref, s32[4,128]{1,0:T(4,128)S(1)} %collective-permute-done.corner_ref, ...), custom_call_target="tpu_custom_call" | custom-call | tf_op jit(solution)/shard_map/pallas_call | solution.py:40
  16.7 13.3 %all-to-all-start = ((f32[64,8,128]{2,1,0:T(8,128)}), f32[64,8,128]{2,1,0:T(8,128)S(1)}, u32[]{:S(2)}, u32[]{:S(2)}) async-start(f32[64,8,128]{2,1,0:T(8,128)} %get-tuple-element.37), calls=%async_computation | async-start | bytes 524288 | tf_op jit(solution)/shard_map/all_to_all | solution.py:403
  30.0 0.7 collective-permute-start.3
  30.7 5.3 %collective-permute-start.4 = (f32[184,128]{1,0:T(8,128)S(1)}, f32[184,128]{1,0:T(8,128)S(1)}, u32[]{:S(2)}, u32[]{:S(2)}) collective-permute-start(f32[184,128]{1,0:T(8,128)S(1)} %get-tuple-element.40), channel_id=1, source_target_pairs={{0,8},{8,0},{16,24},{24,16},{32,40},{40,32},{48,56},{56,48},{64,72... | collective-permute-start | bytes 282632 | tf_op jit(solution)/shard_map/ppermute | solution.py:436
  36.0 0.0 collective-permute-done.3.left_ref
  36.0 3.2 %collective-permute-done.4.right_ref = f32[184,128]{1,0:T(8,128)S(1)} collective-permute-done((f32[184,128]{1,0:T(8,128)S(1)}, f32[184,128]{1,0:T(8,128)S(1)}, u32[]{:S(2)}, u32[]{:S(2)}) %collective-permute-start.4) | collective-permute-done | bytes 94240 | tf_op jit(solution)/shard_map/ppermute | solution.py:436
  39.3 3.8 %all-to-all-done.gathered_ref = f32[64,8,128]{2,1,0:T(8,128)S(1)} async-done(((f32[64,8,128]{2,1,0:T(8,128)}), f32[64,8,128]{2,1,0:T(8,128)S(1)}, u32[]{:S(2)}, u32[]{:S(2)}) %all-to-all-start) | async-done | bytes 262176 | tf_op jit(solution)/shard_map/all_to_all | solution.py:403
  43.1 0.5 shard_map.79
  43.6 7.4 %collective-permute-start.5 = (f32[120,128]{1,0:T(8,128)S(1)}, f32[120,128]{1,0:T(8,128)S(1)}, u32[]{:S(2)}, u32[]{:S(2)}) collective-permute-start(f32[120,128]{1,0:T(8,128)S(1)} %get-tuple-element.42), channel_id=1, source_target_pairs={{1,2},{3,4},{5,6},{2,1},{4,3},{6,5},{9,10},{11,12},{13,14},{10,9},... | collective-permute-start | bytes 184328 | tf_op jit(solution)/shard_map/ppermute | solution.py:435
  51.0 1.9 %collective-permute-start.6 = (f32[120,128]{1,0:T(8,128)S(1)}, f32[120,128]{1,0:T(8,128)S(1)}, u32[]{:S(2)}, u32[]{:S(2)}) collective-permute-start(f32[120,128]{1,0:T(8,128)S(1)} %get-tuple-element.43), channel_id=1, source_target_pairs={{0,1},{1,0},{2,3},{3,2},{4,5},{5,4},{6,7},{7,6},{8,9},{9,8},{10,11... | collective-permute-start | bytes 184328 | tf_op jit(solution)/shard_map/ppermute | solution.py:436
  52.9 0.0 collective-permute-done.5.far_ref
  52.9 1.2 %collective-permute-done.6.near_ref = f32[120,128]{1,0:T(8,128)S(1)} collective-permute-done((f32[120,128]{1,0:T(8,128)S(1)}, f32[120,128]{1,0:T(8,128)S(1)}, u32[]{:S(2)}, u32[]{:S(2)}) %collective-permute-start.6) | collective-permute-done | bytes 61472 | tf_op jit(solution)/shard_map/ppermute | solution.py:436
  54.1 1.3 %shard_map.80 = (f32[18,8,128]{2,1,0:T(8,128)S(1)}, f32[18,8,128]{2,1,0:T(8,128)S(1)}, f32[64,4,128]{2,1,0:T(4,128)}, f32[56,128]{1,0:T(8,128)S(1)}) custom-call(f32[18,16,128]{2,1,0:T(8,128)S(1)} %get-tuple-element.41.wide_ref, f32[120,128]{1,0:T(8,128)S(1)} %collective-permute-done.5.far_ref, f32[120,128]{1,0:T(8,128)S(1)} %collective-permute-done.6.near_ref, ...), custom_call_target="tpu_custom_call" | custom-call | tf_op jit(solution)/shard_map/pallas_call | solution.py:40
  55.4 4.9 %all-to-all-start.1 = ((f32[64,4,128]{2,1,0:T(4,128)}), f32[64,4,128]{2,1,0:T(4,128)S(1)}, u32[]{:S(2)}, u32[]{:S(2)}) async-start(f32[64,4,128]{2,1,0:T(4,128)} %get-tuple-element.47), calls=%async_computation.1 | async-start | bytes 262144 | tf_op jit(solution)/shard_map/all_to_all | solution.py:403
  60.4 2.9 %collective-permute-start.7 = (f32[56,128]{1,0:T(8,128)S(1)}, f32[56,128]{1,0:T(8,128)S(1)}, u32[]{:S(2)}, u32[]{:S(2)}) collective-permute-start(f32[56,128]{1,0:T(8,128)S(1)} %get-tuple-element.50), channel_id=1, source_target_pairs={{0,8},{8,16},{16,24},{24,32},{32,40},{40,48},{48,56},{56,64},{64,7... | collective-permute-start | bytes 86024 | tf_op jit(solution)/shard_map/ppermute | solution.py:400
  63.3 1.0 collective-permute-done.7.low_ref
  64.3 5.5 %all-to-all-done.1.gathered_ref = f32[64,4,128]{2,1,0:T(4,128)S(1)} async-done(((f32[64,4,128]{2,1,0:T(4,128)}), f32[64,4,128]{2,1,0:T(4,128)S(1)}, u32[]{:S(2)}, u32[]{:S(2)}) %all-to-all-start.1) | async-done | bytes 131104 | tf_op jit(solution)/shard_map/all_to_all | solution.py:403
  69.8 0.4 shard_map.81
  70.2 6.4 %collective-permute-start.8 = (f32[96,128]{1,0:T(8,128)S(1)}, f32[96,128]{1,0:T(8,128)S(1)}, u32[]{:S(2)}, u32[]{:S(2)}) collective-permute-start(f32[96,128]{1,0:T(8,128)S(1)} %get-tuple-element.53), channel_id=1, source_target_pairs={{1,2},{3,4},{5,6},{2,1},{4,3},{6,5},{9,10},{11,12},{13,14},{10,9},... | collective-permute-start | bytes 147464 | tf_op jit(solution)/shard_map/ppermute | solution.py:435
  76.7 1.9 %collective-permute-start.9 = (f32[96,128]{1,0:T(8,128)S(1)}, f32[96,128]{1,0:T(8,128)S(1)}, u32[]{:S(2)}, u32[]{:S(2)}) collective-permute-start(f32[96,128]{1,0:T(8,128)S(1)} %get-tuple-element.54), channel_id=1, source_target_pairs={{0,1},{1,0},{2,3},{3,2},{4,5},{5,4},{6,7},{7,6},{8,9},{9,8},{10,11... | collective-permute-start | bytes 147464 | tf_op jit(solution)/shard_map/ppermute | solution.py:436
  78.6 0.0 collective-permute-done.8.far_ref
  78.6 1.2 %collective-permute-done.9.near_ref = f32[96,128]{1,0:T(8,128)S(1)} collective-permute-done((f32[96,128]{1,0:T(8,128)S(1)}, f32[96,128]{1,0:T(8,128)S(1)}, u32[]{:S(2)}, u32[]{:S(2)}) %collective-permute-start.9) | collective-permute-done | bytes 49184 | tf_op jit(solution)/shard_map/ppermute | solution.py:436
  79.8 0.6 shard_map.82
  80.4 13.9 %all_to_all.20 = f32[16,1,128]{2,1,0:T(1,128)S(1)} all-to-all(f32[16,1,128]{2,1,0:T(1,128)S(1)} %get-tuple-element.58), channel_id=1, replica_groups={{0,1,2,3,4,5,6,7,8,9,10,11,12,13,14,15},{16,17,18,19,20,21,22,23,24,25,..., dimensions={0} | all-to-all | bytes 16384 | tf_op jit(solution)/shard_map/all_to_all | solution.py:456
  94.4 14.9 %all_to_all.21.dots_ref = f32[32,1,128]{2,1,0:T(1,128)S(1)} all-to-all(f32[32,1,128]{2,1,0:T(1,128)S(1)} %broadcast_in_dim.2), channel_id=1, replica_groups={{0,16,32,48,64,80,96,112,128,144,160,176,192,208,224,240,256,272,288,30..., dimensions={0} | all-to-all | bytes 32768 | tf_op jit(solution)/shard_map/all_to_all | solution.py:458
  109.3 1.1 %shard_map.83 = (f32[6,6,384]{2,1,0:T(8,128)}, f32[6,6,384]{2,1,0:T(8,128)}) custom-call(f32[32,1,128]{2,1,0:T(1,128)S(1)} %all_to_all.21.dots_ref, f32[18,8,128]{2,1,0:T(8,128)S(1)} %get-tuple-element.33.r_ref, f32[18,8,128]{2,1,0:T(8,128)S(1)} %get-tuple-element.56.z_ref, f32[18,8,128]{2,1,0:T(8,128)S(1)} %get-tuple-element.57.q_ref, ...), custom_call_target="tpu_custom_call" | custom-call | tf_op jit(solution)/shard_map/pallas_call | solution.py:40
  (5 shorter events, 0.1 us)
Async XLA Ops:
  1.3 14.2 %collective-permute-start.1 = (s32[2,128]{1,0:T(2,128)S(1)}, s32[2,128]{1,0:T(2,128)S(1)}, u32[]{:S(2)}, u32[]{:S(2)}) collective-permute-start(s32[2,128]{1,0:T(2,128)S(1)} %bitcast.5), channel_id=1, source_target_pairs={{0,8},{8,16},{16,24},{24,32},{32,40},{40,48},{48,56},{56,64},{64,7... | collective-permute-start | bytes 3080 | tf_op jit(solution)/shard_map/ppermute | solution.py:400
  5.4 10.2 %collective-permute-start = (s32[4,128]{1,0:T(4,128)S(1)}, s32[4,128]{1,0:T(4,128)S(1)}, u32[]{:S(2)}, u32[]{:S(2)}) collective-permute-start(s32[4,128]{1,0:T(4,128)S(1)} %bitcast.4), channel_id=1, source_target_pairs={{0,9},{1,10},{2,11},{3,12},{4,13},{5,14},{6,15},{8,17},{9,18},{10,... | collective-permute-start | bytes 6152 | tf_op jit(solution)/shard_map/ppermute | solution.py:416
  12.1 3.4 %collective-permute-start.2 = (s32[2,128]{1,0:T(2,128)S(1)}, s32[2,128]{1,0:T(2,128)S(1)}, u32[]{:S(2)}, u32[]{:S(2)}) collective-permute-start(s32[2,128]{1,0:T(2,128)S(1)} %slice_bitcast_fusion), channel_id=1, source_target_pairs={{0,1},{1,2},{2,3},{3,4},{4,5},{5,6},{6,7},{8,9},{9,10},{10,11},{11... | collective-permute-start | bytes 3080 | tf_op jit(solution)/shard_map/ppermute | solution.py:400
  14.1 1.5 %copy-start = (f32[64,64]{1,0:T(8,128)S(1)}, f32[64,64]{1,0:T(8,128)}, u32[]{:S(2)}) copy-start(f32[64,64]{1,0:T(8,128)} %matrix_ref.5) | copy-start | bytes 49156
  16.7 26.5 %all-to-all-start = ((f32[64,8,128]{2,1,0:T(8,128)}), f32[64,8,128]{2,1,0:T(8,128)S(1)}, u32[]{:S(2)}, u32[]{:S(2)}) async-start(f32[64,8,128]{2,1,0:T(8,128)} %get-tuple-element.37), calls=%async_computation | async-start | bytes 524288 | tf_op jit(solution)/shard_map/all_to_all | solution.py:403
  30.0 6.0 %collective-permute-start.3 = (f32[184,128]{1,0:T(8,128)S(1)}, f32[184,128]{1,0:T(8,128)S(1)}, u32[]{:S(2)}, u32[]{:S(2)}) collective-permute-start(f32[184,128]{1,0:T(8,128)S(1)} %get-tuple-element.39), channel_id=1, source_target_pairs={{8,16},{24,32},{40,48},{56,64},{72,80},{88,96},{104,112},{120,128}... | collective-permute-start | bytes 282632 | tf_op jit(solution)/shard_map/ppermute | solution.py:435
  30.7 8.6 %collective-permute-start.4 = (f32[184,128]{1,0:T(8,128)S(1)}, f32[184,128]{1,0:T(8,128)S(1)}, u32[]{:S(2)}, u32[]{:S(2)}) collective-permute-start(f32[184,128]{1,0:T(8,128)S(1)} %get-tuple-element.40), channel_id=1, source_target_pairs={{0,8},{8,0},{16,24},{24,16},{32,40},{40,32},{48,56},{56,48},{64,72... | collective-permute-start | bytes 282632 | tf_op jit(solution)/shard_map/ppermute | solution.py:436
  43.6 9.3 %collective-permute-start.5 = (f32[120,128]{1,0:T(8,128)S(1)}, f32[120,128]{1,0:T(8,128)S(1)}, u32[]{:S(2)}, u32[]{:S(2)}) collective-permute-start(f32[120,128]{1,0:T(8,128)S(1)} %get-tuple-element.42), channel_id=1, source_target_pairs={{1,2},{3,4},{5,6},{2,1},{4,3},{6,5},{9,10},{11,12},{13,14},{10,9},... | collective-permute-start | bytes 184328 | tf_op jit(solution)/shard_map/ppermute | solution.py:435
  51.0 3.1 %collective-permute-start.6 = (f32[120,128]{1,0:T(8,128)S(1)}, f32[120,128]{1,0:T(8,128)S(1)}, u32[]{:S(2)}, u32[]{:S(2)}) collective-permute-start(f32[120,128]{1,0:T(8,128)S(1)} %get-tuple-element.43), channel_id=1, source_target_pairs={{0,1},{1,0},{2,3},{3,2},{4,5},{5,4},{6,7},{7,6},{8,9},{9,8},{10,11... | collective-permute-start | bytes 184328 | tf_op jit(solution)/shard_map/ppermute | solution.py:436
  55.4 14.3 %all-to-all-start.1 = ((f32[64,4,128]{2,1,0:T(4,128)}), f32[64,4,128]{2,1,0:T(4,128)S(1)}, u32[]{:S(2)}, u32[]{:S(2)}) async-start(f32[64,4,128]{2,1,0:T(4,128)} %get-tuple-element.47), calls=%async_computation.1 | async-start | bytes 262144 | tf_op jit(solution)/shard_map/all_to_all | solution.py:403
  60.4 3.9 %collective-permute-start.7 = (f32[56,128]{1,0:T(8,128)S(1)}, f32[56,128]{1,0:T(8,128)S(1)}, u32[]{:S(2)}, u32[]{:S(2)}) collective-permute-start(f32[56,128]{1,0:T(8,128)S(1)} %get-tuple-element.50), channel_id=1, source_target_pairs={{0,8},{8,16},{16,24},{24,32},{32,40},{40,48},{48,56},{56,64},{64,7... | collective-permute-start | bytes 86024 | tf_op jit(solution)/shard_map/ppermute | solution.py:400
  70.2 8.4 %collective-permute-start.8 = (f32[96,128]{1,0:T(8,128)S(1)}, f32[96,128]{1,0:T(8,128)S(1)}, u32[]{:S(2)}, u32[]{:S(2)}) collective-permute-start(f32[96,128]{1,0:T(8,128)S(1)} %get-tuple-element.53), channel_id=1, source_target_pairs={{1,2},{3,4},{5,6},{2,1},{4,3},{6,5},{9,10},{11,12},{13,14},{10,9},... | collective-permute-start | bytes 147464 | tf_op jit(solution)/shard_map/ppermute | solution.py:435
  76.7 3.1 %collective-permute-start.9 = (f32[96,128]{1,0:T(8,128)S(1)}, f32[96,128]{1,0:T(8,128)S(1)}, u32[]{:S(2)}, u32[]{:S(2)}) collective-permute-start(f32[96,128]{1,0:T(8,128)S(1)} %get-tuple-element.54), channel_id=1, source_target_pairs={{0,1},{1,0},{2,3},{3,2},{4,5},{5,4},{6,7},{7,6},{8,9},{9,8},{10,11... | collective-permute-start | bytes 147464 | tf_op jit(solution)/shard_map/ppermute | solution.py:436
